TPU v7x, 256 devices: a whole 4x4x8 slice. The times are simulated.
256 devices in a mesh: tok: 4 (over z_hi), voc: 32 (over x, y, core), sub: 2 (over z_lo).
Axes of the slice: x: 4, y: 4, z: 8 (z_hi: 4, z_lo: 2; z = z_hi * 2 + z_lo), core: 2. Of those that a mesh axis runs over, the one named last changes fastest.
Arguments:
- final_state_vectors: bfloat16 [1024, 4096], P(('tok', 'sub')), may hold values from -40 to 40
- learner_output_weights: bfloat16 [4096, 81920], P(('tok', 'sub'), 'voc'), may hold values from -2 to 2
- mentor_raw_scores: bfloat16 [2048, 81920], P('tok', ('voc', 'sub')), may hold values from -256 to 256
- kept_source_lines: int32 [1024], P('tok'), may hold values from 0 to 2047, as said below
- group_sizes_list: int32 [32], replicated, may hold values from 1 to 64, 1024 in all
Outputs:
- head_grad: float32 [4096, 81920], P(('tok', 'sub'), 'voc')
- feature_grad: float32 [1024, 4096], P('voc', ('tok', 'sub'))
- logit_grad: bfloat16 [1024, 81920], P(('tok', 'sub'), 'voc')
- divergence: float32 [1024], P(('tok', 'sub'))
Inputs may be any that keep to these rules, and one draw needn't show every extreme that they name: Rows b * 256 to (b + 1) * 256 - 1 of kept_source_lines are distinct, increasing, and lie in b * 512 to (b + 1) * 512 - 1, both ends included.
All inputs are finite; a program needn't handle non-finite values.
Results may differ from a plain program's by a relative error of at most 0.014.
Values may be sent and summed in bfloat16 or wider, within the bound.
No kernel may reach another device: no remote copies, remote signals or barrier semaphores. Data moves between devices by JAX's collectives and lax.ppermute only.
A program may use at most 128 MiB of HBM per device.

v0:
```python
import jax
import jax.numpy as jnp
from jax import lax
from jax.sharding import PartitionSpec as P

LOSS_SCALE = 65536


floor_bound_value = -1e30


def group_weights(group_sizes_list, row_ids):
    ends = jnp.cumsum(group_sizes_list)
    starts = ends - group_sizes_list
    member = (row_ids[:, None] >= starts[None, :]) & (row_ids[:, None] < ends[None, :])
    length_of = jnp.sum(jnp.where(member, group_sizes_list[None, :], 0), axis=1).astype(jnp.float32)
    return jnp.float32(LOSS_SCALE) / (jnp.float32(group_sizes_list.shape[0]) * length_of)


def broaden_lines(values, line_start_shift, requested_rows, filler):
    empty = jnp.full((requested_rows,), filler, jnp.float32)
    return lax.dynamic_update_slice_in_dim(empty, values, line_start_shift, 0)


def narrow_rows(values, line_start_shift, requested_rows):
    return lax.dynamic_slice_in_dim(values, line_start_shift, requested_rows, 0)


def on_device(
    final_state_vectors,
    learner_output_weights,
    mentor_raw_scores,
    kept_source_lines,
    group_sizes_list,
):
    pair_size = lax.axis_size("sub")
    vocabulary_breadth = lax.axis_size("tok")
    blocks = vocabulary_breadth * pair_size
    kept_entry_number = kept_source_lines.shape[0]
    overall_line_number = kept_entry_number * vocabulary_breadth
    row_share = overall_line_number // blocks
    columns = lax.all_to_all(
        final_state_vectors, ("tok", "sub"), split_axis=1, concat_axis=0, tiled=True
    )
    word_slot_number = lax.axis_index("tok")
    place_within_group = kept_source_lines - word_slot_number * mentor_raw_scores.shape[0]
    picked = jnp.take(mentor_raw_scores, place_within_group, axis=0)
    student = lax.psum_scatter(
        jnp.dot(columns, learner_output_weights, preferred_element_type=jnp.float32),
        ("tok", "sub"),
        scatter_dimension=0,
        tiled=True,
    )
    mentor_network = lax.all_to_all(picked, "sub", split_axis=0, concat_axis=1, tiled=True)
    line_start_shift = lax.axis_index("sub") * row_share
    first_row = lax.axis_index(("tok", "sub")) * row_share
    local_count = student.shape[0]
    teacher_wide = mentor_network.astype(jnp.float32)
    learner_maximum = jnp.max(student, axis=1)
    mentor_maximum = jnp.max(teacher_wide, axis=1)
    student_top, teacher_top = lax.pmax(
        (
            broaden_lines(learner_maximum, line_start_shift, kept_entry_number, floor_bound_value),
            broaden_lines(mentor_maximum, line_start_shift, kept_entry_number, floor_bound_value),
        ),
        ("voc", "sub"),
    )
    student_top = narrow_rows(student_top, line_start_shift, local_count)
    teacher_top = narrow_rows(teacher_top, line_start_shift, local_count)
    learner_exponential = jnp.exp(student - student_top[:, None])
    mentor_exponential = jnp.exp(teacher_wide - teacher_top[:, None])
    student_total, teacher_total, cross_total = lax.psum(
        (
            broaden_lines(
                jnp.sum(learner_exponential, axis=1), line_start_shift, kept_entry_number, 0.0
            ),
            broaden_lines(
                jnp.sum(mentor_exponential, axis=1), line_start_shift, kept_entry_number, 0.0
            ),
            broaden_lines(
                jnp.sum(mentor_exponential * (teacher_wide - student), axis=1),
                line_start_shift,
                kept_entry_number,
                0.0,
            ),
        ),
        ("voc", "sub"),
    )
    student_total = narrow_rows(student_total, line_start_shift, local_count)
    teacher_total = narrow_rows(teacher_total, line_start_shift, local_count)
    cross_total = narrow_rows(cross_total, line_start_shift, local_count)
    divergence = (
        cross_total / teacher_total
        - teacher_top
        - jnp.log(teacher_total)
        + student_top
        + jnp.log(student_total)
    )
    row_ids = first_row + jnp.arange(local_count, dtype=jnp.int32)
    weights = group_weights(group_sizes_list, row_ids)
    local_grad = (
        weights[:, None]
        * (
            learner_exponential / student_total[:, None]
            - mentor_exponential / teacher_total[:, None]
        )
    ).astype(jnp.bfloat16)
    grad_block = lax.all_gather(local_grad, ("tok", "sub"), axis=0, tiled=True)
    head_part = lax.dot_general(
        columns, grad_block, (((0,), (0,)), ((), ())), preferred_element_type=jnp.float32
    )
    feature_part = lax.dot_general(
        grad_block,
        learner_output_weights,
        (((1,), (1,)), ((), ())),
        preferred_element_type=jnp.float32,
    )
    feature_grad = lax.psum_scatter(
        feature_part.astype(jnp.bfloat16), "voc", scatter_dimension=0, tiled=True
    ).astype(jnp.float32)
    return (head_part, feature_grad, local_grad, divergence)


def solution(mesh):
    return jax.shard_map(
        on_device,
        mesh=mesh,
        in_specs=(
            P(("tok", "sub"), None),
            P(("tok", "sub"), "voc"),
            P("tok", ("voc", "sub")),
            P("tok"),
            P(),
        ),
        out_specs=(
            P(("tok", "sub"), "voc"),
            P("voc", ("tok", "sub")),
            P(("tok", "sub"), "voc"),
            P(("tok", "sub")),
        ),
        check_vma=False,
    )
```

profile of v0, /device:TPU:1, one launch (start us, length us, event | category | flops | bytes accessed | tf_op | source)
XLA Modules:
  0.0 619.2 jit_solution(15311241548663879292)
XLA Ops:
  7.2 0.0 copy-start
  7.2 0.0 reduce-scatter.3.cloned.1.call-start
  7.2 2.4 copy.28
  9.6 36.3 %all_to_all.29 = bf16[128,8,512]{0,2,1:T(8,128)(2,1)} all-to-all(bf16[128,8,512]{0,2,1:T(8,128)(2,1)} %bitcast.22), channel_id=1, replica_groups=mesh['tok'=4,'voc'=32,'sub'=2] {'tok','sub'}, dimensions={1} | all-to-all | bytes 2097152 | tf_op jit(solution)/shard_map/all_to_all | solution.py:42
  46.0 2.3 copy.29
  48.2 0.0 copy-done
  48.2 6.7 %fusion.4 = f32[1024,2560]{1,0:T(8,128)} fusion(bf16[1024,512]{1,0:T(8,128)(2,1)} %bitcast.24, bf16[512,2560]{1,0:T(8,128)(2,1)S(1)} %copy-done), kind=kOutput, calls=%fused_computation.22 | convolution fusion | flops 2684354560 | bytes 14155776 | tf_op jit(solution)/shard_map/dot_general | solution.py:49
  54.9 0.0 copy-start.2
  54.9 0.0 reduce-scatter.3.cloned.1.call-update
  55.0 0.6 copy-done.2
  55.6 3.3 gather_fusion
  58.9 0.0 copy-start.1
  58.9 1.0 broadcast_select_fusion
  59.9 3.5 all-to-all-start.1
  63.4 0.0 all-gather.2.cloned.1.call-start
  63.5 0.0 copy-done.1
  63.5 0.1 copy.27
  63.6 0.1 reduce-window.8
  63.6 0.1 reduce.5
  63.8 0.1 select_reduce_fusion
  63.9 14.9 %all-to-all-done.1 = bf16[2,128,1280]{2,1,0:T(8,128)(2,1)S(1)} async-done(((bf16[2,128,1280]{2,1,0:T(8,128)(2,1)}), bf16[2,128,1280]{2,1,0:T(8,128)(2,1)S(1)}, u32[]{:S(2)}, u32[]{:S(2)}) %all-to-all-start.1) | async-done | bytes 655392 | tf_op jit(solution)/shard_map/all_to_all | solution.py:54
  78.7 0.2 fusion.3
  79.0 1.2 copy.32
  80.2 0.1 convert_dynamic-update-slice_fusion
  80.3 92.8 %reduce-scatter.3.cloned.1.call-done = f32[128,2560]{1,0:T(8,128)} async-done(((f32[1024,2560]{1,0:T(8,128)}), f32[128,2560]{1,0:T(8,128)}) %reduce-scatter.3.cloned.1.call-update) | async-done | bytes 1310736 | tf_op jit(solution)/shard_map/reduce_scatter | solution.py:48
  173.1 1.5 reduce_max.23
  174.6 0.2 dynamic_update_slice.15
  174.8 140.1 %all-reduce.1 = (f32[256]{0:T(256)S(1)}, f32[256]{0:T(256)S(1)}) all-reduce(f32[256]{0:T(256)S(1)} %convert_dynamic-update-slice_fusion, f32[256]{0:T(256)S(1)} %dynamic_update_slice.15), channel_id=1, replica_groups=mesh['tok'=4,'voc'=32,'sub'=2] {'voc','sub'}, use_global_device_ids=true, to_apply=%region_8.9 | all-reduce | flops 512 | bytes 4096 | tf_op jit(solution)/shard_map/pmax | solution.py:61
  314.9 0.1 dynamic_slice.17
  315.0 0.1 dynamic_slice.15
  315.1 0.4 fusion.1
  315.5 0.2 dynamic_update_slice.18
  315.7 2.3 multiply_reduce_fusion
  318.0 0.2 dynamic_update_slice.19
  318.2 0.2 dynamic_update_slice.16
  318.5 139.4 %all-reduce = (f32[256]{0:T(256)S(1)}, f32[256]{0:T(256)S(1)}, f32[256]{0:T(256)S(1)}) all-reduce(f32[256]{0:T(256)S(1)} %dynamic_update_slice.18, f32[256]{0:T(256)S(1)} %dynamic_update_slice.16, f32[256]{0:T(256)S(1)} %dynamic_update_slice.19), channel_id=1, replica_groups=mesh['tok'=4,'voc'=32,'sub'=2] {'voc','sub'}, use_global_device_ids=true, to_apply=%region_10.11 | all-reduce | flops 768 | bytes 6144 | tf_op jit(solution)/shard_map/psum | solution.py:72
  457.9 0.6 log_add_fusion
  458.5 3.1 multiply_convert_fusion
  461.6 0.0 all-gather.2.cloned.1.call-update
  461.6 0.0 reduce-scatter.5.cloned.1.call-start
  461.6 61.0 %all-gather.2.cloned.1.call-done = bf16[1024,2560]{1,0:T(8,128)(2,1)} async-done(((bf16[128,2560]{1,0:T(8,128)(2,1)}), bf16[1024,2560]{1,0:T(8,128)(2,1)}) %all-gather.2.cloned.1.call-update) | async-done | bytes 5242896 | tf_op jit(solution)/shard_map/all_gather | solution.py:108
  522.6 6.4 %convolution_convert_fusion = bf16[1024,512]{1,0:T(8,128)(2,1)} fusion(bf16[1024,2560]{1,0:T(8,128)(2,1)} %all-gather.2.cloned.1.call-done, bf16[512,2560]{1,0:T(8,128)(2,1)S(1)} %copy-done), kind=kOutput, calls=%fused_computation.4 | convolution fusion | flops 2684878848 | bytes 8912896 | tf_op jit(solution)/shard_map/dot_general | solution.py:112
  529.0 0.0 reduce-scatter.5.cloned.1.call-update
  529.0 8.1 %convolution_bitcast_fusion = f32[512,2560]{0,1:T(8,128)} fusion(bf16[1024,2560]{1,0:T(8,128)(2,1)} %all-gather.2.cloned.1.call-done, bf16[1024,512]{1,0:T(8,128)(2,1)} %bitcast.25), kind=kOutput, calls=%fused_computation.1 | convolution fusion | flops 2684354560 | bytes 11534336 | tf_op jit(solution)/shard_map/dot_general | solution.py:109
  537.1 5.9 copy.31
  543.0 68.3 %reduce-scatter.5.cloned.1.call-done = bf16[32,512]{1,0:T(8,128)(2,1)} async-done(((bf16[1024,512]{1,0:T(8,128)(2,1)}), bf16[32,512]{1,0:T(8,128)(2,1)}) %reduce-scatter.5.cloned.1.call-update) | async-done | bytes 32784 | tf_op jit(solution)/shard_map/reduce_scatter | solution.py:118
  611.3 1.4 convert_element_type.36
  (10 shorter events, 0.0 us)
Async XLA Ops:
  7.2 41.1 %copy-start = (bf16[512,2560]{1,0:T(8,128)(2,1)S(1)}, bf16[512,2560]{1,0:T(8,128)(2,1)}, u32[]{:S(2)}) copy-start(bf16[512,2560]{1,0:T(8,128)(2,1)} %param.6) | copy-start | bytes 7864324
  7.2 165.9 %reduce-scatter.3.cloned.1.call-start = ((), (), s32[]{:S(2)}) async-start(), calls=%async_computation.4 | async-start | bytes 11796480 | tf_op jit(solution)/shard_map/reduce_scatter | solution.py:48
  54.9 0.7 copy-start.2
  58.9 4.6 copy-start.1
  59.9 18.8 %all-to-all-start.1 = ((bf16[2,128,1280]{2,1,0:T(8,128)(2,1)}), bf16[2,128,1280]{2,1,0:T(8,128)(2,1)S(1)}, u32[]{:S(2)}, u32[]{:S(2)}) async-start(bf16[2,128,1280]{2,1,0:T(8,128)(2,1)} %broadcast_select_fusion), calls=%async_computation.2 | async-start | bytes 1310720 | tf_op jit(solution)/shard_map/all_to_all | solution.py:54
  63.4 459.2 %all-gather.2.cloned.1.call-start = ((), (), s32[]{:S(2)}) async-start(), calls=%async_computation.5 | async-start | bytes 5898240 | tf_op jit(solution)/shard_map/all_gather | solution.py:108
  461.6 149.7 %reduce-scatter.5.cloned.1.call-start = ((), (), s32[]{:S(2)}) async-start(), calls=%async_computation.6 | async-start | bytes 1081344 | tf_op jit(solution)/shard_map/reduce_scatter | solution.py:118
Sparse Core Ops, SparseCore 0:
  55.1 117.9 reduce-scatter.2
  461.7 60.8 all-gather.1
  529.1 82.0 reduce-scatter.4
where the time goes:
time: 620 us; the launch traced here: 619 us
  blocking collectives  316 us (51%)
  waiting for transfers between devices  237 us (38%)
  matrix products  21.1 us (3%)
  local copies, waits for them, and re-layouts  16.9 us (3%)
  between operations  13.8 us (2%)
  other arithmetic  10.8 us (2%)
    pmax x1, blocking collectives, on_device(): lax.pmax((broaden_lines(learner_maximum, line_start_shift, kept_entry_num...  140 us
    psum x1, blocking collectives, on_device(): lax.psum((broaden_lines(jnp.sum(learner_exponential, axis=1), line_start_...  139 us
    reduce_scatter x1, waiting for transfers between devices, on_device(): lax.psum_scatter(jnp.dot(columns, learner_output_weights, preferred_eleme...  92.8 us
    reduce_scatter x1, waiting for transfers between devices, on_device(): lax.psum_scatter(feature_part.astype(jnp.bfloat16), 'voc', scatter_dimens...  68.3 us
    all_gather x1, waiting for transfers between devices, on_device(): grad_block = lax.all_gather(local_grad, ('tok', 'sub'), axis=0, tiled=True)  61 us
    all_to_all x1, blocking collectives, on_device(): lax.all_to_all(final_state_vectors, ('tok', 'sub'), split_axis=1, concat_...  36.3 us
    all_to_all x1, waiting for transfers between devices, on_device(): lax.all_to_all(picked, 'sub', split_axis=0, concat_axis=1, tiled=True)  14.9 us
  transfers between devices with their start and end apart: 4, of which 4 were waited for; matrix products, arithmetic and copies ran while one was open for 3% of the time, Pallas kernels for 0%

commit v1 on v0

v1 whole, which is shorter than its diff:
```python
import jax
import jax.numpy as jnp
from jax import lax
from jax.experimental import pallas as pl
from jax.experimental.pallas import tpu as pltpu
from jax.sharding import PartitionSpec as P

LOSS_SCALE = 65536
F32 = jnp.float32
BF16 = jnp.bfloat16
RING = ("tok", "sub")


def row_weights(sizes, rows):
    count = sizes.shape[0]
    upto = lax.broadcasted_iota(jnp.int32, (count, count), 0) <= lax.broadcasted_iota(
        jnp.int32, (count, count), 1
    )
    ends = jnp.sum(jnp.where(upto, sizes[:, None], 0), axis=0)
    starts = ends - sizes
    ids = lax.broadcasted_iota(jnp.int32, (count, rows), 1)
    member = (ids >= starts[:, None]) & (ids < ends[:, None])
    lengths = jnp.sum(jnp.where(member, sizes[:, None], 0), axis=0).astype(F32)
    return F32(LOSS_SCALE) / (F32(count) * lengths)


def student_kernel(head_ref, rows_ref, student_ref, lse_ref):
    step = pl.program_id(0)
    part = jnp.dot(head_ref[0], rows_ref[...], preferred_element_type=F32)

    @pl.when(step == 0)
    def _():
        student_ref[...] = part

    @pl.when(step > 0)
    def _():
        student_ref[...] += part

    @pl.when(step == pl.num_programs(0) - 1)
    def _():
        logits = student_ref[...]
        top = jnp.max(logits, axis=0, keepdims=True)
        lse_ref[...] = top + jnp.log(jnp.sum(jnp.exp(logits - top), axis=0, keepdims=True))


def student_logits(head, rows):
    blocks, v, d = head.shape
    r = rows.shape[1]
    return pl.pallas_call(
        student_kernel,
        grid=(blocks,),
        in_specs=[
            pl.BlockSpec((1, v, d), lambda i: (i, 0, 0)),
            pl.BlockSpec((d, r), lambda i: (i, 0)),
        ],
        out_specs=[
            pl.BlockSpec((v, r), lambda i: (0, 0)),
            pl.BlockSpec((1, r), lambda i: (0, 0)),
        ],
        out_shape=[
            jax.ShapeDtypeStruct((v, r), F32),
            jax.ShapeDtypeStruct((1, r), F32),
        ],
        compiler_params=pltpu.CompilerParams(vmem_limit_bytes=32 * 1024 * 1024),
    )(head, rows)


def grad_kernel(student_ref, teacher_ref, scale_ref, grad_ref, cross_ref):
    student = student_ref[...]
    teacher = teacher_ref[0].astype(F32)
    chance = jnp.exp(teacher - scale_ref[1:2, :])
    cross_ref[...] = jnp.sum(chance * (teacher - student), axis=0, keepdims=True)
    grad = scale_ref[2:3, :] * (jnp.exp(student - scale_ref[0:1, :]) - chance)
    grad_ref[...] = grad.astype(BF16)


def logit_grads(student, teacher, scales):
    v, r = student.shape
    parts, _, width = teacher.shape
    return pl.pallas_call(
        grad_kernel,
        grid=(parts,),
        in_specs=[
            pl.BlockSpec((v, width), lambda i: (0, i)),
            pl.BlockSpec((1, v, width), lambda i: (i, 0, 0)),
            pl.BlockSpec((3, width), lambda i: (0, i)),
        ],
        out_specs=[
            pl.BlockSpec((v, width), lambda i: (0, i)),
            pl.BlockSpec((1, width), lambda i: (0, i)),
        ],
        out_shape=[
            jax.ShapeDtypeStruct((v, r), BF16),
            jax.ShapeDtypeStruct((1, r), F32),
        ],
        compiler_params=pltpu.CompilerParams(vmem_limit_bytes=32 * 1024 * 1024),
    )(student, teacher, scales)


def to_all(values, axis):
    size = lax.axis_size(axis)
    return lax.all_to_all(jnp.broadcast_to(values[None], (size,) + values.shape), axis, 0, 0)


def merge(parts):
    top = jnp.max(parts, axis=0)
    return top + jnp.log(jnp.sum(jnp.exp(parts - top[None]), axis=0))


def on_device(hidden, head, pool, lines, sizes):
    toks, subs, vocs = lax.axis_size("tok"), lax.axis_size("sub"), lax.axis_size("voc")
    ring = toks * subs
    share, width = hidden.shape
    rows = share * ring
    depth, vocab = head.shape
    cut = vocab // ring
    place = lax.axis_index(RING)
    core = lax.axis_index("voc") % 2

    piece = width // vocs
    own = lax.dynamic_slice_in_dim(hidden, lax.axis_index("voc") * piece, piece, 1)
    column = to_all(own, RING).reshape(rows, piece).T
    features = lax.all_gather(column, "voc", axis=0, tiled=True)

    slices = head.reshape(depth, subs, toks, cut).transpose(2, 1, 3, 0).reshape(ring, cut, depth)
    head_cut = lax.all_to_all(slices, RING, 0, 0)

    wanted = lines - lax.axis_index("tok") * pool.shape[0]
    choose = (
        lax.broadcasted_iota(jnp.int32, (pool.shape[0], lines.shape[0]), 0) == wanted[None, :]
    ).astype(BF16)
    picked = lax.dot_general(
        pool, choose, (((0,), (0,)), ((), ())), preferred_element_type=F32
    ).astype(BF16)
    teacher = lax.all_to_all(picked.reshape(toks, cut, lines.shape[0]), "tok", 0, 0)

    student, student_lse = student_logits(head_cut, features)
    teacher_wide = teacher.astype(F32)
    teacher_top = jnp.max(teacher_wide, axis=1)
    teacher_lse = teacher_top + jnp.log(
        jnp.sum(jnp.exp(teacher_wide - teacher_top[:, None]), axis=1)
    )
    stats = jnp.stack([student_lse.reshape(8, rows // 8), teacher_lse.reshape(8, rows // 8)])
    stats = merge(to_all(stats, RING))
    stats = merge(to_all(stats, "voc")).reshape(2, rows)

    weights = row_weights(sizes, rows)
    scales = jnp.concatenate([stats, weights[None]])
    grad_cut, cross = logit_grads(student, teacher, scales)
    grads = lax.all_gather(grad_cut, ("sub", "tok"), axis=0, tiled=True)

    cross = jnp.sum(lax.all_to_all(cross.reshape(ring, share), RING, 0, 0), axis=0)
    cross = jnp.sum(to_all(cross, "voc"), axis=0)
    own_stats = lax.dynamic_slice_in_dim(stats, place * share, share, 1)
    divergence = cross + own_stats[0] - own_stats[1]

    feature_part = lax.dot_general(
        grads, head, (((0,), (1,)), ((), ())), preferred_element_type=F32
    )
    chips = vocs // 2
    halves = feature_part.reshape(chips, 2, rows // vocs, depth)
    keep = jnp.where(core == 0, halves[:, 0], halves[:, 1])
    give = jnp.where(core == 0, halves[:, 1], halves[:, 0])
    given = lax.ppermute(give, "voc", [(i, i ^ 1) for i in range(vocs)])
    groups = [[2 * i + c for i in range(chips)] for c in range(2)]
    sums = lax.all_to_all((keep + given).astype(BF16), "voc", 0, 0, axis_index_groups=groups)
    feature_grad = jnp.sum(sums.astype(F32), axis=0)

    own_features = lax.dynamic_slice_in_dim(features, place * depth, depth, 0)
    head_grad = lax.dot_general(
        own_features, grads, (((1,), (1,)), ((), ())), preferred_element_type=F32
    )
    local_grad = lax.dynamic_slice_in_dim(grads, place * share, share, 1).T
    return head_grad, feature_grad, local_grad, divergence


def solution(mesh):
    return jax.shard_map(
        on_device,
        mesh=mesh,
        in_specs=(
            P(RING, None),
            P(RING, "voc"),
            P("tok", ("voc", "sub")),
            P("tok"),
            P(),
        ),
        out_specs=(
            P(RING, "voc"),
            P("voc", RING),
            P(RING, "voc"),
            P(RING),
        ),
        check_vma=False,
    )
```

time: 620 us -> 332 us (0.54)
  blocking collectives: 316 us -> 19.2 us
  starting transfers between devices: 3.63 us -> 37.6 us
  waiting for transfers between devices: 237 us -> 209 us
  Pallas kernels: 0 us -> 9.24 us
  matrix products: 21.1 us -> 14.3 us
    reduce_scatter x2 -> x0, waiting for transfers between devices: 161 us -> none  [the longest x1 92.8 us: on_device(): lax.psum_scatter(jnp.dot(columns, learner_output_weights, preferred_eleme...]
    pmax x1 -> x0, blocking collectives: 140 us -> none  [on_device(): lax.pmax((broaden_lines(learner_maximum, line_start_shift, kept_entry_num...]
    psum x1 -> x0, blocking collectives: 139 us -> none  [on_device(): lax.psum((broaden_lines(jnp.sum(learner_exponential, axis=1), line_start_...]
    all_to_all x1 -> x7, waiting for transfers between devices: 14.9 us -> 103 us  [the longest x1 62.7 us: on_device(): head_cut = lax.all_to_all(slices, RING, 0, 0)]
    all_gather x1 -> x2, waiting for transfers between devices: 61 us -> 106 us  [the longest x1 106 us: on_device(): grads = lax.all_gather(grad_cut, ('sub', 'tok'), axis=0, tiled=True)]
    all_to_all x1 -> x7, starting transfers between devices: 3.51 us -> 36.9 us  [the longest x3 20.4 us: to_all(): lax.all_to_all(jnp.broadcast_to(values[None], (size,) + values.shape), ax...]
    all_to_all x1, blocking collectives: 36.3 us -> 19.2 us  [to_all(): lax.all_to_all(jnp.broadcast_to(values[None], (size,) + values.shape), ax...]
    pallas_call x0 -> x2, Pallas kernels: none -> 9.24 us  [the longest x1 7.43 us: student_logits(): pl.pallas_call(student_kernel, grid=(blocks,), in_specs=[pl.BlockSpec((1,...]
  transfers between devices with their start and end apart: 4 -> 10, of which waited for: 4 -> 8; matrix products, arithmetic and copies ran while one was open for 3% -> 7% of each run, Pallas kernels for 0% -> 0%
where the time goes in v1:
time: 332 us; the launch traced here: 331 us
  waiting for transfers between devices  209 us (63%)
  starting transfers between devices  37.6 us (11%)
  local copies, waits for them, and re-layouts  21.2 us (6%)
  blocking collectives  19.2 us (6%)
  matrix products  14.3 us (4%)
  between operations  14.3 us (4%)
  Pallas kernels  9.24 us (3%)
  other arithmetic  6.19 us (2%)
    all_gather x1, waiting for transfers between devices, on_device(): grads = lax.all_gather(grad_cut, ('sub', 'tok'), axis=0, tiled=True)  106 us
    all_to_all x1, waiting for transfers between devices, on_device(): head_cut = lax.all_to_all(slices, RING, 0, 0)  62.7 us
    all_to_all x3, waiting for transfers between devices, to_all(): lax.all_to_all(jnp.broadcast_to(values[None], (size,) + values.shape), ax...  22.7 us
    all_to_all x3, starting transfers between devices, to_all(): lax.all_to_all(jnp.broadcast_to(values[None], (size,) + values.shape), ax...  20.4 us
    all_to_all x1, blocking collectives, to_all(): lax.all_to_all(jnp.broadcast_to(values[None], (size,) + values.shape), ax...  19.2 us
    unnamed x11, local copies, waits for them, and re-layouts  10.8 us
    all_to_all x1, waiting for transfers between devices, on_device(): lax.all_to_all(picked.reshape(toks, cut, lines.shape[0]), 'tok', 0, 0)  8.94 us
    dot_general x1, matrix products, on_device(): lax.dot_general(own_features, grads, (((1,), (1,)), ((), ())), preferred_...  8.1 us
  transfers between devices with their start and end apart: 10, of which 8 were waited for; matrix products, arithmetic and copies ran while one was open for 7% of the time, Pallas kernels for 0%

profile of v1, /device:TPU:1, one launch (start us, length us, event | category | flops | bytes accessed | tf_op | source)
XLA Modules:
  0.0 331.4 jit_solution(8837046581787684432)
XLA Ops:
  7.2 0.0 copy-start
  7.2 0.0 all-gather.3.cloned.1.call-start
  7.2 0.9 constant_dynamic-slice_fusion.1
  8.1 0.1 copy.48
  8.3 19.2 %all_to_all.45 = bf16[8,128,128]{1,2,0:T(8,128)(2,1)S(1)} all-to-all(bf16[8,128,128]{1,2,0:T(8,128)(2,1)S(1)} %broadcast_in_dim.28), channel_id=1, replica_groups=mesh['tok'=4,'voc'=32,'sub'=2] {'tok','sub'}, dimensions={0} | all-to-all | bytes 524288 | tf_op jit(solution)/shard_map/all_to_all | solution.py:102
  27.4 0.7 bitcast_bitcast_fusion
  28.2 0.0 all-gather.3.cloned.1.call-update
  28.2 0.7 broadcast_subtract_fusion
  28.9 0.0 copy-done
  28.9 0.6 fusion
  29.4 1.1 copy.52
  30.5 3.5 %all-to-all-start.2 = ((bf16[4,320,256]{2,1,0:T(8,128)(2,1)}), bf16[4,320,256]{2,1,0:T(8,128)(2,1)S(1)}, u32[]{:S(2)}, u32[]{:S(2)}) async-start(bf16[4,320,256]{2,1,0:T(8,128)(2,1)} %bitcast.5), calls=%async_computation.2 | async-start | bytes 1310720 | tf_op jit(solution)/shard_map/all_to_all | solution.py:135
  34.0 4.4 %copy.50 = bf16[512,2560]{0,1:T(8,128)(2,1)} copy(bf16[512,2560]{1,0:T(8,128)(2,1)} %param.6) | data formatting | bytes 5242880 | tf_op args[1]
  38.4 3.6 %copy.51 = bf16[4,2,320,512]{3,2,1,0:T(8,128)(2,1)} copy(bf16[4,2,320,512]{3,2,0,1:T(8,128)(2,1)} %bitcast.62) | data formatting | bytes 5242880 | tf_op jit(solution)/shard_map/transpose | solution.py:125
  42.0 8.9 %all-to-all-done.2.teacher_ref = bf16[4,320,256]{2,1,0:T(8,128)(2,1)S(1)} async-done(((bf16[4,320,256]{2,1,0:T(8,128)(2,1)}), bf16[4,320,256]{2,1,0:T(8,128)(2,1)S(1)}, u32[]{:S(2)}, u32[]{:S(2)}) %all-to-all-start.2) | async-done | bytes 655392 | tf_op jit(solution)/shard_map/all_to_all | solution.py:135
  50.9 4.4 %all-to-all-start.1 = ((bf16[8,320,512]{2,1,0:T(8,128)(2,1)}), bf16[8,320,512]{2,1,0:T(8,128)(2,1)}, u32[]{:S(2)}, u32[]{:S(2)}) async-start(bf16[8,320,512]{2,1,0:T(8,128)(2,1)} %bitcast.61), calls=%async_computation.1 | async-start | bytes 5242880 | tf_op jit(solution)/shard_map/all_to_all | solution.py:126
  55.4 0.1 reduce_max.32
  55.5 0.2 exponential_reduce_fusion
  55.7 0.0 copy-start.3
  55.8 62.7 %all-to-all-done.1.head_ref = bf16[8,320,512]{2,1,0:T(8,128)(2,1)} async-done(((bf16[8,320,512]{2,1,0:T(8,128)(2,1)}), bf16[8,320,512]{2,1,0:T(8,128)(2,1)}, u32[]{:S(2)}, u32[]{:S(2)}) %all-to-all-start.1) | async-done | bytes 2621472 | tf_op jit(solution)/shard_map/all_to_all | solution.py:126
  118.4 0.0 all-gather.3.cloned.1.call-done.rows_ref
  118.4 0.0 copy-start.1
  118.4 3.4 %copy-done.1 = bf16[4096,1024]{1,0:T(8,128)(2,1)S(1)} copy-done((bf16[4096,1024]{1,0:T(8,128)(2,1)S(1)}, bf16[4096,1024]{1,0:T(8,128)(2,1)}, u32[]{:S(2)}) %copy-start.1) | copy-done | bytes 8388632
  121.8 7.4 %shard_map.84 = (f32[320,1024]{1,0:T(8,128)S(1)}, f32[1,1024]{1,0:T(1,128)S(1)}) custom-call(bf16[8,320,512]{2,1,0:T(8,128)(2,1)} %all-to-all-done.1.head_ref, bf16[4096,1024]{1,0:T(8,128)(2,1)S(1)} %copy-done.1), custom_call_target="tpu_custom_call" | custom-call | tf_op jit(solution)/shard_map/pallas_call | solution.py:49
  129.3 0.6 broadcast_in_dim.29
  129.9 3.4 %all-to-all-start.3 = ((f32[8,2,8,128]{3,2,1,0:T(8,128)}), f32[8,2,8,128]{3,2,1,0:T(8,128)S(1)}, u32[]{:S(2)}, u32[]{:S(2)}) async-start(f32[8,2,8,128]{3,2,1,0:T(8,128)} %broadcast_in_dim.29), calls=%async_computation.3 | async-start | bytes 131072 | tf_op jit(solution)/shard_map/all_to_all | solution.py:102
  133.3 0.0 copy-done.3
  133.3 0.1 select_reduce_fusion.1
  133.4 7.0 %all-to-all-done.3 = f32[8,2,8,128]{3,2,1,0:T(8,128)S(1)} async-done(((f32[8,2,8,128]{3,2,1,0:T(8,128)}), f32[8,2,8,128]{3,2,1,0:T(8,128)S(1)}, u32[]{:S(2)}, u32[]{:S(2)}) %all-to-all-start.3) | async-done | bytes 65568 | tf_op jit(solution)/shard_map/all_to_all | solution.py:102
  140.5 0.7 broadcast_in_dim.30
  141.2 8.8 %all-to-all-start.4 = ((f32[32,2,8,128]{3,2,1,0:T(8,128)}), f32[32,2,8,128]{3,2,1,0:T(8,128)S(1)}, u32[]{:S(2)}, u32[]{:S(2)}) async-start(f32[32,2,8,128]{3,2,1,0:T(8,128)} %broadcast_in_dim.30), calls=%async_computation.4 | async-start | bytes 524288 | tf_op jit(solution)/shard_map/all_to_all | solution.py:102
  150.0 0.0 all-gather.5.cloned.1.call-start
  150.0 0.1 select_reduce_fusion
  150.1 8.8 %all-to-all-done.4 = f32[32,2,8,128]{3,2,1,0:T(8,128)S(1)} async-done(((f32[32,2,8,128]{3,2,1,0:T(8,128)}), f32[32,2,8,128]{3,2,1,0:T(8,128)S(1)}, u32[]{:S(2)}, u32[]{:S(2)}) %all-to-all-start.4) | async-done | bytes 262176 | tf_op jit(solution)/shard_map/all_to_all | solution.py:102
  159.0 0.1 exponential_reduce_fusion.1
  159.1 1.8 shard_map.85
  160.9 0.0 copy-start.2
  160.9 0.8 copy-done.2
  161.8 0.0 all-gather.5.cloned.1.call-update
  161.8 106.3 %all-gather.5.cloned.1.call-done = bf16[2560,1024]{1,0:T(8,128)(2,1)} async-done(((bf16[320,1024]{1,0:T(8,128)(2,1)}), bf16[2560,1024]{1,0:T(8,128)(2,1)}) %all-gather.5.cloned.1.call-update) | async-done | bytes 5242896 | tf_op jit(solution)/shard_map/all_gather | solution.py:150
  268.1 5.7 %fusion.9 = f32[1024,512]{1,0:T(8,128)S(1)} fusion(bf16[2560,1024]{1,0:T(8,128)(2,1)} %all-gather.5.cloned.1.call-done, bf16[512,2560]{1,0:T(8,128)(2,1)} %param.6), kind=kOutput, calls=%fused_computation.36 | convolution fusion | flops 2684354560 | bytes 9961472 | tf_op jit(solution)/shard_map/dot_general | solution.py:157
  273.8 1.2 select_bitcast_fusion
  275.0 0.7 collective-permute-start
  275.7 4.9 %all-to-all-start.6 = ((f32[8,1,128]{2,1,0:T(1,128)}), f32[8,1,128]{2,1,0:T(1,128)S(1)}, u32[]{:S(2)}, u32[]{:S(2)}) async-start(f32[8,1,128]{2,1,0:T(1,128)} %bitcast.16), calls=%async_computation.6 | async-start | bytes 8192 | tf_op jit(solution)/shard_map/all_to_all | solution.py:152
  280.6 6.5 %all-to-all-done.6 = f32[8,1,128]{2,1,0:T(1,128)S(1)} async-done(((f32[8,1,128]{2,1,0:T(1,128)}), f32[8,1,128]{2,1,0:T(1,128)S(1)}, u32[]{:S(2)}, u32[]{:S(2)}) %all-to-all-start.6) | async-done | bytes 4128 | tf_op jit(solution)/shard_map/all_to_all | solution.py:152
  287.1 0.6 broadcast_in_dim.39
  287.7 8.3 %all-to-all-start.7 = ((f32[32,1,128]{2,1,0:T(1,128)}), f32[32,1,128]{2,1,0:T(1,128)S(1)}, u32[]{:S(2)}, u32[]{:S(2)}) async-start(f32[32,1,128]{2,1,0:T(1,128)} %broadcast_in_dim.39), calls=%async_computation.7 | async-start | bytes 32768 | tf_op jit(solution)/shard_map/all_to_all | solution.py:102
  296.1 6.8 %all-to-all-done.7 = f32[32,1,128]{2,1,0:T(1,128)S(1)} async-done(((f32[32,1,128]{2,1,0:T(1,128)}), f32[32,1,128]{2,1,0:T(1,128)S(1)}, u32[]{:S(2)}, u32[]{:S(2)}) %all-to-all-start.7) | async-done | bytes 16416 | tf_op jit(solution)/shard_map/all_to_all | solution.py:102
  303.0 0.5 bitcast_subtract_fusion
  303.5 2.0 dynamic-slice_bitcast_fusion
  305.5 2.2 copy.59
  307.6 0.0 collective-permute-done
  307.6 2.3 fusion.3
  309.9 3.6 %all-to-all-start.5 = ((bf16[16,32,512]{2,1,0:T(8,128)(2,1)}), bf16[16,32,512]{2,1,0:T(8,128)(2,1)S(1)}, u32[]{:S(2)}, u32[]{:S(2)}) async-start(bf16[16,32,512]{2,1,0:T(8,128)(2,1)} %fusion.3), calls=%async_computation.5 | async-start | bytes 1048576 | tf_op jit(solution)/shard_map/all_to_all | solution.py:166
  313.5 8.1 %fusion.4 = f32[512,2560]{1,0:T(8,128)} fusion(bf16[2560,1024]{1,0:T(8,128)(2,1)} %all-gather.5.cloned.1.call-done, bf16[4096,1024]{1,0:T(8,128)(2,1)} %all-gather.3.cloned.1.call-done.rows_ref, s32[]{:T(128)S(6)} %select_n.44), kind=kOutput, calls=%fused_computation.9 | convolution fusion | flops 2684354560 | bytes 11534340 | tf_op jit(solution)/shard_map/dot_general | solution.py:170
  321.6 2.3 all-to-all-done.5
  323.9 0.7 convert_reduce_fusion
  (17 shorter events, 0.2 us)
Async XLA Ops:
  7.2 21.7 %copy-start = (bf16[512,1280]{1,0:T(8,128)(2,1)S(1)}, bf16[512,1280]{1,0:T(8,128)(2,1)}, u32[]{:S(2)}) copy-start(bf16[512,1280]{1,0:T(8,128)(2,1)} %param.7) | copy-start | bytes 3932164
  7.2 111.2 %all-gather.3.cloned.1.call-start = ((), (), s32[]{:S(2)}) async-start(), calls=%async_computation.8 | async-start | bytes 8650752 | tf_op jit(solution)/shard_map/all_gather | solution.py:123
  30.5 20.4 %all-to-all-start.2 = ((bf16[4,320,256]{2,1,0:T(8,128)(2,1)}), bf16[4,320,256]{2,1,0:T(8,128)(2,1)S(1)}, u32[]{:S(2)}, u32[]{:S(2)}) async-start(bf16[4,320,256]{2,1,0:T(8,128)(2,1)} %bitcast.5), calls=%async_computation.2 | async-start | bytes 1310720 | tf_op jit(solution)/shard_map/all_to_all | solution.py:135
  50.9 67.5 %all-to-all-start.1 = ((bf16[8,320,512]{2,1,0:T(8,128)(2,1)}), bf16[8,320,512]{2,1,0:T(8,128)(2,1)}, u32[]{:S(2)}, u32[]{:S(2)}) async-start(bf16[8,320,512]{2,1,0:T(8,128)(2,1)} %bitcast.61), calls=%async_computation.1 | async-start | bytes 5242880 | tf_op jit(solution)/shard_map/all_to_all | solution.py:126
  55.7 77.5 %copy-start.3 = (s32[32]{0:T(128)S(1)}, s32[32]{0:T(128)}, u32[]{:S(2)}) copy-start(s32[32]{0:T(128)} %param.9) | copy-start | bytes 388
  118.4 3.4 %copy-start.1 = (bf16[4096,1024]{1,0:T(8,128)(2,1)S(1)}, bf16[4096,1024]{1,0:T(8,128)(2,1)}, u32[]{:S(2)}) copy-start(bf16[4096,1024]{1,0:T(8,128)(2,1)} %all-gather.3.cloned.1.call-done.rows_ref) | copy-start | bytes 25165828
  129.9 10.5 %all-to-all-start.3 = ((f32[8,2,8,128]{3,2,1,0:T(8,128)}), f32[8,2,8,128]{3,2,1,0:T(8,128)S(1)}, u32[]{:S(2)}, u32[]{:S(2)}) async-start(f32[8,2,8,128]{3,2,1,0:T(8,128)} %broadcast_in_dim.29), calls=%async_computation.3 | async-start | bytes 131072 | tf_op jit(solution)/shard_map/all_to_all | solution.py:102
  141.2 17.8 %all-to-all-start.4 = ((f32[32,2,8,128]{3,2,1,0:T(8,128)}), f32[32,2,8,128]{3,2,1,0:T(8,128)S(1)}, u32[]{:S(2)}, u32[]{:S(2)}) async-start(f32[32,2,8,128]{3,2,1,0:T(8,128)} %broadcast_in_dim.30), calls=%async_computation.4 | async-start | bytes 524288 | tf_op jit(solution)/shard_map/all_to_all | solution.py:102
  150.0 118.2 %all-gather.5.cloned.1.call-start = ((), (), s32[]{:S(2)}) async-start(), calls=%async_computation.9 | async-start | bytes 5898240 | tf_op jit(solution)/shard_map/all_gather | solution.py:150
  160.9 0.8 copy-start.2
  275.0 32.6 %collective-permute-start = (f32[16,32,512]{2,1,0:T(8,128)}, f32[16,32,512]{2,1,0:T(8,128)}, u32[]{:S(2)}, u32[]{:S(2)}) collective-permute-start(f32[16,32,512]{2,1,0:T(8,128)} %select_bitcast_fusion), channel_id=1, source_target_pairs={{0,2},{2,0},{4,6},{6,4},{8,10},{10,8},{12,14},{14,12},{16,18},{18,... | collective-permute-start | bytes 3145736 | tf_op jit(solution)/shard_map/ppermute | solution.py:164
  275.7 11.4 %all-to-all-start.6 = ((f32[8,1,128]{2,1,0:T(1,128)}), f32[8,1,128]{2,1,0:T(1,128)S(1)}, u32[]{:S(2)}, u32[]{:S(2)}) async-start(f32[8,1,128]{2,1,0:T(1,128)} %bitcast.16), calls=%async_computation.6 | async-start | bytes 8192 | tf_op jit(solution)/shard_map/all_to_all | solution.py:152
  287.7 15.2 %all-to-all-start.7 = ((f32[32,1,128]{2,1,0:T(1,128)}), f32[32,1,128]{2,1,0:T(1,128)S(1)}, u32[]{:S(2)}, u32[]{:S(2)}) async-start(f32[32,1,128]{2,1,0:T(1,128)} %broadcast_in_dim.39), calls=%async_computation.7 | async-start | bytes 32768 | tf_op jit(solution)/shard_map/all_to_all | solution.py:102
  309.9 14.0 %all-to-all-start.5 = ((bf16[16,32,512]{2,1,0:T(8,128)(2,1)}), bf16[16,32,512]{2,1,0:T(8,128)(2,1)S(1)}, u32[]{:S(2)}, u32[]{:S(2)}) async-start(bf16[16,32,512]{2,1,0:T(8,128)(2,1)} %fusion.3), calls=%async_computation.5 | async-start | bytes 1048576 | tf_op jit(solution)/shard_map/all_to_all | solution.py:166
Sparse Core Ops, SparseCore 0:
  28.3 56.4 all-gather.2
  161.9 106.1 all-gather.4

commit v2 on v1

v2 whole, which is shorter than its diff:
```python
import functools

import jax
import jax.numpy as jnp
from jax import lax
from jax.experimental import pallas as pl
from jax.experimental.pallas import tpu as pltpu
from jax.sharding import PartitionSpec as P

LOSS_SCALE = 65536
F32 = jnp.float32
BF16 = jnp.bfloat16
RING = ("tok", "sub")


def row_weights(sizes, rows):
    count = sizes.shape[0]
    upto = lax.broadcasted_iota(jnp.int32, (count, count), 0) <= lax.broadcasted_iota(
        jnp.int32, (count, count), 1
    )
    ends = jnp.sum(jnp.where(upto, sizes[:, None], 0), axis=0)
    starts = ends - sizes
    ids = lax.broadcasted_iota(jnp.int32, (count, rows), 1)
    member = (ids >= starts[:, None]) & (ids < ends[:, None])
    lengths = jnp.sum(jnp.where(member, sizes[:, None], 0), axis=0).astype(F32)
    return F32(LOSS_SCALE) / (F32(count) * lengths)


def student_kernel(head_ref, rows_ref, student_ref, lse_ref):
    step = pl.program_id(0)
    part = jnp.dot(head_ref[0], rows_ref[...], preferred_element_type=F32)

    @pl.when(step == 0)
    def _():
        student_ref[...] = part

    @pl.when(step > 0)
    def _():
        student_ref[...] += part

    @pl.when(step == pl.num_programs(0) - 1)
    def _():
        logits = student_ref[...]
        top = jnp.max(logits, axis=0, keepdims=True)
        lse_ref[...] = top + jnp.log(jnp.sum(jnp.exp(logits - top), axis=0, keepdims=True))


def student_logits(head, rows, subs):
    blocks, v, d = head.shape
    r = rows.shape[1]
    toks = blocks // subs
    return pl.pallas_call(
        student_kernel,
        grid=(blocks,),
        in_specs=[
            pl.BlockSpec((1, v, d), lambda i: (i, 0, 0)),
            pl.BlockSpec((d, r), lambda i: (i % toks * subs + i // toks, 0)),
        ],
        out_specs=[
            pl.BlockSpec((v, r), lambda i: (0, 0)),
            pl.BlockSpec((1, r), lambda i: (0, 0)),
        ],
        out_shape=[
            jax.ShapeDtypeStruct((v, r), F32),
            jax.ShapeDtypeStruct((1, r), F32),
        ],
        compiler_params=pltpu.CompilerParams(vmem_limit_bytes=58 * 1024 * 1024),
    )(head, rows)


def grad_kernel(tok_ref, student_ref, *refs):
    teacher_refs, (scale_ref, low_ref, high_ref, cross_ref) = refs[:-4], refs[-4:]
    toks = len(teacher_refs)
    width = teacher_refs[0].shape[1]
    half = low_ref.shape[0]
    for shift, teacher_ref in enumerate(teacher_refs):
        block = lax.rem(tok_ref[0] + toks - shift, toks)
        cols = pl.ds(pl.multiple_of(block * width, width), width)
        student = student_ref[:, cols]
        teacher = teacher_ref[...].astype(F32)
        chance = jnp.exp(teacher - scale_ref[1:2, cols])
        cross_ref[:, cols] = jnp.sum(chance * (teacher - student), axis=0, keepdims=True)
        grad = scale_ref[2:3, cols] * (jnp.exp(student - scale_ref[0:1, cols]) - chance)
        grad = grad.astype(BF16)
        low_ref[:, cols] = grad[:half]
        high_ref[:, cols] = grad[half:]


def logit_grads(tok, student, teachers, scales):
    v, r = student.shape
    vmem = pl.BlockSpec(memory_space=pltpu.VMEM)
    return pl.pallas_call(
        grad_kernel,
        in_specs=[pl.BlockSpec(memory_space=pltpu.SMEM)] + [vmem] * (2 + len(teachers)),
        out_specs=[vmem] * 3,
        out_shape=[
            jax.ShapeDtypeStruct((v // 2, r), BF16),
            jax.ShapeDtypeStruct((v // 2, r), BF16),
            jax.ShapeDtypeStruct((1, r), F32),
        ],
        compiler_params=pltpu.CompilerParams(vmem_limit_bytes=32 * 1024 * 1024),
    )(tok, student, *teachers, scales)


def fetch_blocks(where_ref, block_refs, hops, all_ref, sem):
    height = block_refs[0].shape[0]
    ring = all_ref.shape[0] // (2 * height)
    copies = []
    for index, (block_ref, (back, half)) in enumerate(zip(block_refs, hops)):
        origin = lax.rem(where_ref[0] + ring - back, ring)
        slot = lax.rem(origin, 2) * (ring // 2) + origin // 2
        start = pl.multiple_of(slot * (2 * height) + half * height, 16)
        copies.append(
            pltpu.make_async_copy(block_ref, all_ref.at[pl.ds(start, height)], sem.at[index])
        )
    for copy in copies:
        copy.start()
    for copy in copies:
        copy.wait()


def feature_kernel(hops, where_ref, *refs):
    blocks, (head_ref, keep_ref, give_ref, all_ref, sem) = refs[: len(hops)], refs[len(hops) :]
    fetch_blocks(where_ref, blocks, hops, all_ref, sem)
    first = where_ref[1] == 0
    tile = 256
    per = keep_ref.shape[1]
    chips = tile // (2 * per)

    @pl.loop(0, all_ref.shape[1] // tile)
    def _(i):
        cols = pl.ds(pl.multiple_of(i * tile, tile), tile)
        part = jnp.dot(head_ref[...], all_ref[:, cols], preferred_element_type=F32).T
        part = part.reshape(chips, 2, per, part.shape[1])
        even, odd = part[:, 0], part[:, 1]
        keep_ref[pl.ds(i * chips, chips)] = jnp.where(first, even, odd)
        give_ref[pl.ds(i * chips, chips)] = jnp.where(first, odd, even)


def feature_parts(where, blocks, hops, head, per):
    depth, vocab = head.shape
    rows = blocks[0].shape[1]
    vmem = pl.BlockSpec(memory_space=pltpu.VMEM)
    shape = jax.ShapeDtypeStruct((rows // (2 * per), per, depth), F32)
    return pl.pallas_call(
        functools.partial(feature_kernel, hops),
        in_specs=[pl.BlockSpec(memory_space=pltpu.SMEM)]
        + [pl.BlockSpec(memory_space=pl.ANY)] * len(blocks)
        + [vmem],
        out_specs=[vmem] * 2,
        out_shape=[shape, shape],
        scratch_shapes=[pltpu.VMEM((vocab, rows), BF16), pltpu.SemaphoreType.DMA((len(blocks),))],
        compiler_params=pltpu.CompilerParams(vmem_limit_bytes=40 * 1024 * 1024),
        cost_estimate=pl.CostEstimate(
            flops=2 * rows * depth * vocab, bytes_accessed=12 * 1024 * 1024, transcendentals=0
        ),
    )(where, *blocks, head)


def head_kernel(hops, where_ref, *refs):
    blocks, rest = refs[: len(hops)], refs[len(hops) :]
    features_ref, out_ref, own_ref, all_ref, own_features, sem, other_sem = rest
    depth = own_features.shape[0]
    mine = pl.ds(pl.multiple_of(where_ref[0] * depth, depth), depth)
    copy = pltpu.make_async_copy(features_ref.at[mine], own_features, other_sem)
    copy.start()
    fetch_blocks(where_ref, blocks, hops, all_ref, sem)
    copy.wait()
    tile = 256
    share = own_ref.shape[0]
    own_cols = pl.ds(pl.multiple_of(where_ref[0] * share, share), share)

    @pl.loop(0, all_ref.shape[0] // tile)
    def _(i):
        rows = pl.ds(pl.multiple_of(i * tile, tile), tile)
        out_ref[:, rows] = lax.dot_general(
            own_features[...],
            all_ref[rows, :],
            (((1,), (1,)), ((), ())),
            preferred_element_type=F32,
        )
        own_ref[:, rows] = all_ref[rows, own_cols].astype(F32).T.astype(BF16)


def head_parts(where, blocks, hops, features, depth, vocab, share):
    rows = blocks[0].shape[1]
    vmem = pl.BlockSpec(memory_space=pltpu.VMEM)
    return pl.pallas_call(
        functools.partial(head_kernel, hops),
        in_specs=[pl.BlockSpec(memory_space=pltpu.SMEM)]
        + [pl.BlockSpec(memory_space=pl.ANY)] * (len(blocks) + 1),
        out_specs=[vmem] * 2,
        out_shape=[
            jax.ShapeDtypeStruct((depth, vocab), F32),
            jax.ShapeDtypeStruct((share, vocab), BF16),
        ],
        scratch_shapes=[
            pltpu.VMEM((vocab, rows), BF16),
            pltpu.VMEM((depth, rows), BF16),
            pltpu.SemaphoreType.DMA((len(blocks),)),
            pltpu.SemaphoreType.DMA,
        ],
        compiler_params=pltpu.CompilerParams(vmem_limit_bytes=58 * 1024 * 1024),
        cost_estimate=pl.CostEstimate(
            flops=2 * rows * depth * vocab, bytes_accessed=12 * 1024 * 1024, transcendentals=0
        ),
    )(where, *blocks, features)


def to_all(values, axis, **groups):
    size = lax.axis_size(axis)
    if groups:
        size = len(groups["axis_index_groups"][0])
    return lax.all_to_all(jnp.broadcast_to(values[None], (size,) + values.shape), axis, 0, 0, **groups)


def merge(parts, axis=0):
    top = jnp.max(parts, axis=axis, keepdims=True)
    total = jnp.sum(jnp.exp(parts - top), axis=axis, keepdims=True)
    return jnp.squeeze(top + jnp.log(total), axis)


def ring_shift(values, step, size):
    return lax.ppermute(values, RING, [(i, (i + step) % size) for i in range(size)])


def ring_gather(halves, size):
    blocks, hops = list(halves), [(0, 0), (0, 1)]
    ahead, behind = list(halves), list(halves)
    for step in range(1, size // 2 + 1):
        last = step == size // 2
        for half in range(2):
            if not last or half == 1:
                ahead[half] = ring_shift(ahead[half], 1, size)
                blocks.append(ahead[half])
                hops.append((step, half))
            if not last or half == 0:
                behind[half] = ring_shift(behind[half], -1, size)
                blocks.append(behind[half])
                hops.append((size - step, half))
    return blocks, hops


def on_device(hidden, head, pool, lines, sizes):
    toks, subs, vocs = lax.axis_size("tok"), lax.axis_size("sub"), lax.axis_size("voc")
    ring = toks * subs
    chips = vocs // 2
    share, width = hidden.shape
    rows = share * ring
    depth, vocab = head.shape
    cut = vocab // ring
    kept = lines.shape[0]
    tok = lax.axis_index("tok")
    place = lax.axis_index(RING)
    core = lax.axis_index("voc") % 2
    cores = [(i, i ^ 1) for i in range(vocs)]
    groups = [[2 * i + c for i in range(chips)] for c in range(2)]

    wanted = lines - tok * pool.shape[0]
    choose = (
        lax.broadcasted_iota(jnp.int32, (pool.shape[0], kept), 0) == wanted[None, :]
    ).astype(BF16)
    picked = lax.dot_general(
        pool, choose, (((0,), (0,)), ((), ())), preferred_element_type=F32
    )
    teacher_lse = merge(picked).reshape(kept // 128, 128)
    picked = picked.astype(BF16).reshape(toks, cut, kept)

    piece = width // vocs
    own = lax.dynamic_slice_in_dim(hidden, lax.axis_index("voc") * piece, piece, 1)
    column = to_all(own, RING)
    slices = head.T.reshape(ring, cut, depth)
    slices, picked, teacher_lse, column = lax.optimization_barrier(
        (slices, picked, teacher_lse, column)
    )
    features = lax.all_gather(column.reshape(rows, piece).T, "voc", axis=0, tiled=True)
    head_cut = lax.all_to_all(slices, ("sub", "tok"), 0, 0)
    head_cut, picked = lax.optimization_barrier((head_cut, picked))

    teachers = []
    for shift in range(toks):
        part = lax.dynamic_index_in_dim(picked, (tok + shift) % toks, 0, keepdims=False)
        if shift:
            part = lax.ppermute(part, "tok", [(i, (i + shift) % toks) for i in range(toks)])
        teachers.append(part)

    student, student_lse = student_logits(head_cut, features, subs)
    stats = jnp.concatenate([student_lse.reshape(rows // 128, 128), teacher_lse])
    stats = to_all(stats, RING)
    ours = merge(stats[:, : rows // 128])
    theirs = stats[:, rows // 128 :].reshape(toks, subs, kept // 128, 128)
    stats = jnp.stack([ours, merge(theirs, 1).reshape(rows // 128, 128)])
    stats = merge(jnp.stack([stats, lax.ppermute(stats, "voc", cores)]))
    stats = merge(to_all(stats, "voc", axis_index_groups=groups)).reshape(2, rows)

    scales = jnp.concatenate([stats, row_weights(sizes, rows)[None]])
    low, high, cross = logit_grads(tok.reshape(1), student, teachers, scales)
    blocks, hops = ring_gather((low, high), ring)

    cross = jnp.sum(lax.all_to_all(cross.reshape(ring, share), RING, 0, 0), axis=0)
    cross = jnp.sum(to_all(cross, "voc"), axis=0)
    own_stats = lax.dynamic_slice_in_dim(stats, place * share, share, 1)
    divergence = cross + own_stats[0] - own_stats[1]
    *blocks, divergence = lax.optimization_barrier((*blocks, divergence))

    where = jnp.stack([place, core])
    keep, give = feature_parts(where, blocks, hops, head, rows // vocs)
    given = lax.ppermute(give, "voc", cores)
    sums, where = lax.optimization_barrier(((keep + given).astype(BF16), where))
    sums = lax.all_to_all(sums, "voc", 0, 0, axis_index_groups=groups)
    feature_grad = jnp.sum(sums.astype(F32), axis=0)

    head_grad, local_grad = head_parts(where, blocks, hops, features, depth, vocab, share)
    return head_grad, feature_grad, local_grad, divergence


def solution(mesh):
    return jax.shard_map(
        on_device,
        mesh=mesh,
        in_specs=(
            P(RING, None),
            P(RING, "voc"),
            P("tok", ("voc", "sub")),
            P("tok"),
            P(),
        ),
        out_specs=(
            P(RING, "voc"),
            P("voc", RING),
            P(RING, "voc"),
            P(RING),
        ),
        check_vma=False,
    )
```

time: 332 us -> 258 us (0.78)
  waiting for transfers between devices: 209 us -> 122 us
  starting transfers between devices: 37.6 us -> 68.8 us
  Pallas kernels: 9.24 us -> 29.2 us
  blocking collectives: 19.2 us -> 0 us
  matrix products: 14.3 us -> 0.64 us
  local copies, waits for them, and re-layouts: 21.2 us -> 16.4 us
    all_gather x2 -> x1, waiting for transfers between devices: 106 us -> 0.01 us  [on_device(): lax.all_gather(column.reshape(rows, piece).T, 'voc', axis=0, tiled=True)]
    ppermute x1 -> x19, waiting for transfers between devices: 0.01 us -> 36.5 us  [the longest x14 25.3 us: ring_shift(): lax.ppermute(values, RING, [(i, (i + step) % size) for i in range(size)])]
    ppermute x1 -> x19, starting transfers between devices: 0.68 us -> 24.1 us  [the longest x14 17.3 us: ring_shift(): lax.ppermute(values, RING, [(i, (i + step) % size) for i in range(size)])]
    all_to_all x1 -> x0, blocking collectives: 19.2 us -> none  [to_all(): lax.all_to_all(jnp.broadcast_to(values[None], (size,) + values.shape), ax...]
    pallas_call x1 -> x3, Pallas kernels: 1.81 us -> 19.1 us  [the longest x1 10.9 us: head_parts(): pl.pallas_call(functools.partial(head_kernel, hops), in_specs=[pl.BlockSp...]
    all_to_all x3 -> x2, waiting for transfers between devices: 73.9 us -> 59.2 us  [the longest x1 59.2 us: on_device(): head_cut = lax.all_to_all(slices, ('sub', 'tok'), 0, 0)]
    dot_general x2 -> x0, matrix products: 13.8 us -> none  [the longest x1 8.1 us: on_device(): lax.dot_general(own_features, grads, (((1,), (1,)), ((), ())), preferred_...]
    all_to_all x3 -> x4, starting transfers between devices: 20.4 us -> 29.6 us  [to_all(): lax.all_to_all(jnp.broadcast_to(values[None], (size,) + values.shape), ax...]
  transfers between devices with their start and end apart: 10 -> 27, of which waited for: 8 -> 15; matrix products, arithmetic and copies ran while one was open for 7% -> 4% of each run, Pallas kernels for 0% -> 4%
where the time goes in v2:
time: 258 us; the launch traced here: 257 us
  waiting for transfers between devices  122 us (47%)
  starting transfers between devices  68.8 us (27%)
  Pallas kernels  29.2 us (11%)
  local copies, waits for them, and re-layouts  16.4 us (6%)
  between operations  14.3 us (6%)
  other arithmetic  6.27 us (2%)
    all_to_all x1, waiting for transfers between devices, on_device(): head_cut = lax.all_to_all(slices, ('sub', 'tok'), 0, 0)  59.2 us
    all_to_all x4, starting transfers between devices, to_all(): lax.all_to_all(jnp.broadcast_to(values[None], (size,) + values.shape), ax...  29.6 us
    ppermute x14, waiting for transfers between devices, ring_shift(): lax.ppermute(values, RING, [(i, (i + step) % size) for i in range(size)])  25.3 us
    ppermute x14, starting transfers between devices, ring_shift(): lax.ppermute(values, RING, [(i, (i + step) % size) for i in range(size)])  17.3 us
    all_to_all x4, waiting for transfers between devices, to_all(): lax.all_to_all(jnp.broadcast_to(values[None], (size,) + values.shape), ax...  16.3 us
    pallas_call x1, Pallas kernels, head_parts(): pl.pallas_call(functools.partial(head_kernel, hops), in_specs=[pl.BlockSp...  10.9 us
    pallas_call x1, Pallas kernels, student_logits(): pl.pallas_call(student_kernel, grid=(blocks,), in_specs=[pl.BlockSpec((1,...  10.1 us
    all_to_all x1, waiting for transfers between devices, on_device(): lax.all_to_all(cross.reshape(ring, share), RING, 0, 0)  9.73 us
  transfers between devices with their start and end apart: 27, of which 15 were waited for; matrix products, arithmetic and copies ran while one was open for 4% of the time, Pallas kernels for 4%

profile of v2, /device:TPU:1, one launch (start us, length us, event | category | flops | bytes accessed | tf_op | source)
XLA Modules:
  0.0 257.4 jit_solution(16814148359924322764)
XLA Ops:
  7.2 0.9 constant_dynamic-slice_fusion.1
  8.2 0.7 broadcast_in_dim.24
  8.9 9.0 %all-to-all-start = ((bf16[8,128,128]{1,2,0:T(8,128)(2,1)}), bf16[8,128,128]{1,2,0:T(8,128)(2,1)S(1)}, u32[]{:S(2)}, u32[]{:S(2)}) async-start(bf16[8,128,128]{1,2,0:T(8,128)(2,1)} %broadcast_in_dim.24), calls=%async_computation | async-start | bytes 524288 | tf_op jit(solution)/shard_map/all_to_all | solution.py:214
  18.0 0.7 broadcast_subtract_fusion
  18.7 0.6 fusion.7
  19.3 0.3 exponential_reduce_fusion
  19.9 4.4 %copy.39 = bf16[2560,512]{1,0:T(8,128)(2,1)} copy(bf16[2560,512]{0,1:T(8,128)(2,1)} %bitcast.53) | data formatting | bytes 5242880 | tf_op jit(solution)/shard_map/transpose | solution.py:272
  24.3 4.0 %all-to-all-done = bf16[8,128,128]{1,2,0:T(8,128)(2,1)S(1)} async-done(((bf16[8,128,128]{1,2,0:T(8,128)(2,1)}), bf16[8,128,128]{1,2,0:T(8,128)(2,1)S(1)}, u32[]{:S(2)}, u32[]{:S(2)}) %all-to-all-start) | async-done | bytes 262176 | tf_op jit(solution)/shard_map/all_to_all | solution.py:214
  28.3 0.7 bitcast_bitcast_fusion
  29.1 4.4 %all-to-all-start.1 = ((bf16[8,320,512]{2,1,0:T(8,128)(2,1)}), bf16[8,320,512]{2,1,0:T(8,128)(2,1)}, u32[]{:S(2)}, u32[]{:S(2)}) async-start(bf16[8,320,512]{2,1,0:T(8,128)(2,1)} %bitcast.54), calls=%async_computation.1 | async-start | bytes 5242880 | tf_op jit(solution)/shard_map/all_to_all | solution.py:277
  33.6 59.2 %all-to-all-done.1.head_ref = bf16[8,320,512]{2,1,0:T(8,128)(2,1)} async-done(((bf16[8,320,512]{2,1,0:T(8,128)(2,1)}), bf16[8,320,512]{2,1,0:T(8,128)(2,1)}, u32[]{:S(2)}, u32[]{:S(2)}) %all-to-all-start.1) | async-done | bytes 2621472 | tf_op jit(solution)/shard_map/all_to_all | solution.py:277
  92.8 10.1 %shard_map.84 = (f32[320,1024]{1,0:T(8,128)}, f32[1,1024]{1,0:T(1,128)}) custom-call(bf16[8,320,512]{2,1,0:T(8,128)(2,1)} %all-to-all-done.1.head_ref, bf16[4096,1024]{1,0:T(8,128)(2,1)} %all-gather.2.cloned.1.call-done.rows_ref.refs_16_), custom_call_target="tpu_custom_call" | custom-call | tf_op jit(solution)/shard_map/pallas_call | solution.py:52
  102.9 0.7 pad_maximum_fusion.1
  103.6 0.6 broadcast_in_dim.25
  104.3 5.1 %all-to-all-start.2 = ((f32[8,10,128]{2,1,0:T(8,128)}), f32[8,10,128]{2,1,0:T(8,128)S(1)}, u32[]{:S(2)}, u32[]{:S(2)}) async-start(f32[8,10,128]{2,1,0:T(8,128)} %broadcast_in_dim.25), calls=%async_computation.2 | async-start | bytes 131072 | tf_op jit(solution)/shard_map/all_to_all | solution.py:214
  109.5 7.2 %all-to-all-done.2 = f32[8,10,128]{2,1,0:T(8,128)S(1)} async-done(((f32[8,10,128]{2,1,0:T(8,128)}), f32[8,10,128]{2,1,0:T(8,128)S(1)}, u32[]{:S(2)}, u32[]{:S(2)}) %all-to-all-start.2) | async-done | bytes 40992 | tf_op jit(solution)/shard_map/all_to_all | solution.py:214
  116.9 2.2 collective-permute-start.3
  119.1 0.8 collective-permute-done.3
  119.9 0.7 broadcast_in_dim.26
  120.6 6.8 %all-to-all-start.3 = ((f32[16,2,8,128]{3,2,1,0:T(8,128)}), f32[16,2,8,128]{3,2,1,0:T(8,128)}, u32[]{:S(2)}, u32[]{:S(2)}) async-start(f32[16,2,8,128]{3,2,1,0:T(8,128)} %broadcast_in_dim.26), calls=%async_computation.3 | async-start | bytes 262144 | tf_op jit(solution)/shard_map/all_to_all | solution.py:214
  127.4 0.8 dynamic-slice_bitcast_fusion
  128.3 3.3 %collective-permute-start.1 = (bf16[320,256]{1,0:T(8,128)(2,1)}, bf16[320,256]{1,0:T(8,128)(2,1)S(1)}, u32[]{:S(2)}, u32[]{:S(2)}) collective-permute-start(bf16[320,256]{1,0:T(8,128)(2,1)} %get-tuple-element.75), channel_id=1, source_target_pairs={{0,128},{64,192},{128,0},{192,64},{1,129},{65,193},{129,1},{193,65... | collective-permute-start | bytes 491528 | tf_op jit(solution)/shard_map/ppermute | solution.py:284
  131.7 2.5 all-to-all-done.3
  134.1 0.9 reduce_max.49
  135.1 0.9 exponential_reduce_fusion.1
  136.1 8.1 %collective-permute-done.2.refs_3_ = bf16[320,256]{1,0:T(8,128)(2,1)S(1)} collective-permute-done((bf16[320,256]{1,0:T(8,128)(2,1)}, bf16[320,256]{1,0:T(8,128)(2,1)S(1)}, u32[]{:S(2)}, u32[]{:S(2)}) %collective-permute-start.2) | collective-permute-done | bytes 163872 | tf_op jit(solution)/shard_map/ppermute | solution.py:284
  144.2 0.7 copy-done.9
  144.9 0.7 copy-done.11
  145.5 0.7 copy-done.13
  146.2 0.9 copy-done.10
  147.1 0.9 copy-done.12
  148.0 0.9 copy-done.14
  149.0 1.2 shard_map.85
  150.1 3.9 %collective-permute-start.5 = (bf16[160,1024]{1,0:T(8,128)(2,1)S(1)}, bf16[160,1024]{1,0:T(8,128)(2,1)S(1)}, u32[]{:S(2)}, u32[]{:S(2)}) collective-permute-start(bf16[160,1024]{1,0:T(8,128)(2,1)S(1)} %get-tuple-element.49.refs_0_), channel_id=1, source_target_pairs={{0,193},{1,0},{64,1},{65,64},{128,65},{129,128},{192,129},{193,192... | collective-permute-start | bytes 983048 | tf_op jit(solution)/shard_map/ppermute | solution.py:224
  154.0 0.9 collective-permute-start.6
  154.9 1.5 collective-permute-start.4
  156.4 1.2 collective-permute-start.7
  157.6 5.0 %collective-permute-done.5.refs_3_ = bf16[160,1024]{1,0:T(8,128)(2,1)S(1)} collective-permute-done((bf16[160,1024]{1,0:T(8,128)(2,1)S(1)}, bf16[160,1024]{1,0:T(8,128)(2,1)S(1)}, u32[]{:S(2)}, u32[]{:S(2)}) %collective-permute-start.5) | collective-permute-done | bytes 327712 | tf_op jit(solution)/shard_map/ppermute | solution.py:224
  162.6 1.4 collective-permute-start.9
  164.0 6.7 %collective-permute-done.4.refs_2_ = bf16[160,1024]{1,0:T(8,128)(2,1)S(1)} collective-permute-done((bf16[160,1024]{1,0:T(8,128)(2,1)S(1)}, bf16[160,1024]{1,0:T(8,128)(2,1)S(1)}, u32[]{:S(2)}, u32[]{:S(2)}) %collective-permute-start.4) | collective-permute-done | bytes 327712 | tf_op jit(solution)/shard_map/ppermute | solution.py:224
  170.7 2.6 %collective-permute-start.11 = (bf16[160,1024]{1,0:T(8,128)(2,1)S(1)}, bf16[160,1024]{1,0:T(8,128)(2,1)}, u32[]{:S(2)}, u32[]{:S(2)}) collective-permute-start(bf16[160,1024]{1,0:T(8,128)(2,1)S(1)} %collective-permute-done.7.refs_5_), channel_id=1, source_target_pairs={{0,193},{1,0},{64,1},{65,64},{128,65},{129,128},{192,129},{193,192... | collective-permute-start | bytes 983048 | tf_op jit(solution)/shard_map/ppermute | solution.py:224
  173.4 3.3 %collective-permute-done.9.refs_7_ = bf16[160,1024]{1,0:T(8,128)(2,1)} collective-permute-done((bf16[160,1024]{1,0:T(8,128)(2,1)S(1)}, bf16[160,1024]{1,0:T(8,128)(2,1)}, u32[]{:S(2)}, u32[]{:S(2)}) %collective-permute-start.9) | collective-permute-done | bytes 327712 | tf_op jit(solution)/shard_map/ppermute | solution.py:224
  176.7 1.4 collective-permute-start.13
  178.2 3.9 %all-to-all-start.4 = ((f32[8,1,128]{2,1,0:T(1,128)}), f32[8,1,128]{2,1,0:T(1,128)S(1)}, u32[]{:S(2)}, u32[]{:S(2)}) async-start(f32[8,1,128]{2,1,0:T(1,128)} %bitcast.21), calls=%async_computation.4 | async-start | bytes 8192 | tf_op jit(solution)/shard_map/all_to_all | solution.py:300
  182.2 9.7 %all-to-all-done.4 = f32[8,1,128]{2,1,0:T(1,128)S(1)} async-done(((f32[8,1,128]{2,1,0:T(1,128)}), f32[8,1,128]{2,1,0:T(1,128)S(1)}, u32[]{:S(2)}, u32[]{:S(2)}) %all-to-all-start.4) | async-done | bytes 4128 | tf_op jit(solution)/shard_map/all_to_all | solution.py:300
  192.0 0.6 broadcast_in_dim.35
  192.6 8.6 %all-to-all-start.5 = ((f32[32,1,128]{2,1,0:T(1,128)}), f32[32,1,128]{2,1,0:T(1,128)S(1)}, u32[]{:S(2)}, u32[]{:S(2)}) async-start(f32[32,1,128]{2,1,0:T(1,128)} %broadcast_in_dim.35), calls=%async_computation.5 | async-start | bytes 32768 | tf_op jit(solution)/shard_map/all_to_all | solution.py:214
  201.2 1.1 collective-permute-start.12
  202.3 1.6 collective-permute-start.15
  204.0 0.4 collective-permute-start.16
  204.4 1.0 collective-permute-start.17
  205.4 2.6 %all-to-all-done.5 = f32[32,1,128]{2,1,0:T(1,128)S(1)} async-done(((f32[32,1,128]{2,1,0:T(1,128)}), f32[32,1,128]{2,1,0:T(1,128)S(1)}, u32[]{:S(2)}, u32[]{:S(2)}) %all-to-all-start.5) | async-done | bytes 16416 | tf_op jit(solution)/shard_map/all_to_all | solution.py:214
  208.1 0.5 bitcast_subtract_fusion
  208.6 3.3 %collective-permute-done.12.refs_10_ = bf16[160,1024]{1,0:T(8,128)(2,1)} collective-permute-done((bf16[160,1024]{1,0:T(8,128)(2,1)}, bf16[160,1024]{1,0:T(8,128)(2,1)}, u32[]{:S(2)}, u32[]{:S(2)}) %collective-permute-start.12) | collective-permute-done | bytes 327712 | tf_op jit(solution)/shard_map/ppermute | solution.py:224
  211.9 6.6 %collective-permute-done.16.refs_14_ = bf16[160,1024]{1,0:T(8,128)(2,1)} collective-permute-done((bf16[160,1024]{1,0:T(8,128)(2,1)}, bf16[160,1024]{1,0:T(8,128)(2,1)}, u32[]{:S(2)}, u32[]{:S(2)}) %collective-permute-start.16) | collective-permute-done | bytes 327712 | tf_op jit(solution)/shard_map/ppermute | solution.py:224
  218.4 0.5 collective-permute-done.17.refs_15_
  218.9 1.7 copy-done.1
  220.7 7.1 %shard_map.86 = (f32[16,32,512]{2,1,0:T(8,128)S(1)}, f32[16,32,512]{2,1,0:T(8,128)S(1)}) custom-call(s32[2]{0:T(128)S(1)} %pad_add_fusion.where_ref, bf16[160,1024]{1,0:T(8,128)(2,1)S(1)} %get-tuple-element.49.refs_0_, bf16[160,1024]{1,0:T(8,128)(2,1)S(1)} %get-tuple-element.50.refs_1_, bf16[160,1024]{1,0:T(8,128)(2,1)S(1)} %collective-permute-done.4.refs_2_, ...), custom_call_target="tpu_custom_call" | custom-call | flops 2684354560 | bytes 12582912 | tf_op jit(solution)/shard_map/pallas_call | solution.py:145
  227.8 1.1 collective-permute-start.18
  228.9 2.3 collective-permute-done.18
  231.2 1.0 add_convert_fusion
  232.2 6.7 %all-to-all-start.6 = ((bf16[16,32,512]{2,1,0:T(8,128)(2,1)}), bf16[16,32,512]{2,1,0:T(8,128)(2,1)S(1)}, u32[]{:S(2)}, u32[]{:S(2)}) async-start(bf16[16,32,512]{2,1,0:T(8,128)(2,1)} %add_convert_fusion), calls=%async_computation.6 | async-start | bytes 1048576 | tf_op jit(solution)/shard_map/all_to_all | solution.py:310
  238.9 10.9 %shard_map.87 = (f32[512,2560]{1,0:T(8,128)}, bf16[128,2560]{1,0:T(8,128)(2,1)}) custom-call(s32[2]{0:T(128)} %copy-done.15, bf16[160,1024]{1,0:T(8,128)(2,1)} %copy-done.3, bf16[160,1024]{1,0:T(8,128)(2,1)} %copy-done.4, bf16[160,1024]{1,0:T(8,128)(2,1)} %copy-done.7, bf16[160,1024]{1,0:T(8,128)(2,1)} %copy-done.5, bf16[160,1024]{1,0:T(8,128)(2,1)} %copy-done.6, ...), custom_call_target="tpu_custom_call" | custom-call | flops 2684354560 | bytes 12582912 | tf_op jit(solution)/shard_map/pallas_call | solution.py:188
  249.8 0.7 convert_reduce_fusion
  (73 shorter events, 1.2 us)
Async XLA Ops:
  7.2 11.5 %copy-start = (bf16[512,1280]{1,0:T(8,128)(2,1)S(1)}, bf16[512,1280]{1,0:T(8,128)(2,1)}, u32[]{:S(2)}) copy-start(bf16[512,1280]{1,0:T(8,128)(2,1)} %param.7) | copy-start | bytes 3932164
  8.9 19.4 %all-to-all-start = ((bf16[8,128,128]{1,2,0:T(8,128)(2,1)}), bf16[8,128,128]{1,2,0:T(8,128)(2,1)S(1)}, u32[]{:S(2)}, u32[]{:S(2)}) async-start(bf16[8,128,128]{1,2,0:T(8,128)(2,1)} %broadcast_in_dim.24), calls=%async_computation | async-start | bytes 524288 | tf_op jit(solution)/shard_map/all_to_all | solution.py:214
  17.9 74.9 %all-gather.2.cloned.1.call-start = ((), (), s32[]{:S(2)}) async-start(), calls=%async_computation.7 | async-start | bytes 8650752 | tf_op jit(solution)/shard_map/all_gather | solution.py:276
  29.1 4.4 %copy-start.16 = (s32[32]{0:T(128)S(1)}, s32[32]{0:T(128)}, u32[]{:S(2)}) copy-start(s32[32]{0:T(128)} %param.9) | copy-start | bytes 388
  29.1 63.7 %all-to-all-start.1 = ((bf16[8,320,512]{2,1,0:T(8,128)(2,1)}), bf16[8,320,512]{2,1,0:T(8,128)(2,1)}, u32[]{:S(2)}, u32[]{:S(2)}) async-start(bf16[8,320,512]{2,1,0:T(8,128)(2,1)} %bitcast.54), calls=%async_computation.1 | async-start | bytes 5242880 | tf_op jit(solution)/shard_map/all_to_all | solution.py:277
  104.3 42.0 %copy-start.2 = (f32[320,1024]{1,0:T(8,128)S(1)}, f32[320,1024]{1,0:T(8,128)}, u32[]{:S(2)}) copy-start(f32[320,1024]{1,0:T(8,128)} %get-tuple-element.42.student_ref) | copy-start | bytes 3932164
  104.3 12.5 %all-to-all-start.2 = ((f32[8,10,128]{2,1,0:T(8,128)}), f32[8,10,128]{2,1,0:T(8,128)S(1)}, u32[]{:S(2)}, u32[]{:S(2)}) async-start(f32[8,10,128]{2,1,0:T(8,128)} %broadcast_in_dim.25), calls=%async_computation.2 | async-start | bytes 131072 | tf_op jit(solution)/shard_map/all_to_all | solution.py:214
  116.9 3.0 %collective-permute-start.3 = (f32[2,8,128]{2,1,0:T(8,128)S(1)}, f32[2,8,128]{2,1,0:T(8,128)S(1)}, u32[]{:S(2)}, u32[]{:S(2)}) collective-permute-start(f32[2,8,128]{2,1,0:T(8,128)S(1)} %pad_maximum_fusion.2), channel_id=1, source_target_pairs={{0,2},{2,0},{4,6},{6,4},{8,10},{10,8},{12,14},{14,12},{16,18},{18,... | collective-permute-start | bytes 24584 | tf_op jit(solution)/shard_map/ppermute | solution.py:293
  120.6 13.6 %all-to-all-start.3 = ((f32[16,2,8,128]{3,2,1,0:T(8,128)}), f32[16,2,8,128]{3,2,1,0:T(8,128)}, u32[]{:S(2)}, u32[]{:S(2)}) async-start(f32[16,2,8,128]{3,2,1,0:T(8,128)} %broadcast_in_dim.26), calls=%async_computation.3 | async-start | bytes 262144 | tf_op jit(solution)/shard_map/all_to_all | solution.py:214
  128.2 16.0 %collective-permute-start.2 = (bf16[320,256]{1,0:T(8,128)(2,1)}, bf16[320,256]{1,0:T(8,128)(2,1)S(1)}, u32[]{:S(2)}, u32[]{:S(2)}) collective-permute-start(bf16[320,256]{1,0:T(8,128)(2,1)} %get-tuple-element.74), channel_id=1, source_target_pairs={{0,192},{64,0},{128,64},{192,128},{1,193},{65,1},{129,65},{193,129... | collective-permute-start | bytes 491528 | tf_op jit(solution)/shard_map/ppermute | solution.py:284
  128.3 16.5 %collective-permute-start.1 = (bf16[320,256]{1,0:T(8,128)(2,1)}, bf16[320,256]{1,0:T(8,128)(2,1)S(1)}, u32[]{:S(2)}, u32[]{:S(2)}) collective-permute-start(bf16[320,256]{1,0:T(8,128)(2,1)} %get-tuple-element.75), channel_id=1, source_target_pairs={{0,128},{64,192},{128,0},{192,64},{1,129},{65,193},{129,1},{193,65... | collective-permute-start | bytes 491528 | tf_op jit(solution)/shard_map/ppermute | solution.py:284
  131.7 13.9 %collective-permute-start = (bf16[320,256]{1,0:T(8,128)(2,1)}, bf16[320,256]{1,0:T(8,128)(2,1)S(1)}, u32[]{:S(2)}, u32[]{:S(2)}) collective-permute-start(bf16[320,256]{1,0:T(8,128)(2,1)} %get-tuple-element.76), channel_id=1, source_target_pairs={{0,64},{64,128},{128,192},{192,0},{1,65},{65,129},{129,193},{193,1... | collective-permute-start | bytes 491528 | tf_op jit(solution)/shard_map/ppermute | solution.py:284
  144.2 0.7 copy-start.9
  144.9 0.7 copy-start.11
  145.5 0.7 copy-start.13
  146.2 0.9 copy-start.10
  147.1 0.9 copy-start.12
  148.0 0.9 copy-start.14
  150.1 77.6 %copy-start.3 = (bf16[160,1024]{1,0:T(8,128)(2,1)}, bf16[160,1024]{1,0:T(8,128)(2,1)S(1)}, u32[]{:S(2)}) copy-start(bf16[160,1024]{1,0:T(8,128)(2,1)S(1)} %get-tuple-element.49.refs_0_) | copy-start | bytes 983044
  150.1 77.6 %copy-start.4 = (bf16[160,1024]{1,0:T(8,128)(2,1)}, bf16[160,1024]{1,0:T(8,128)(2,1)S(1)}, u32[]{:S(2)}) copy-start(bf16[160,1024]{1,0:T(8,128)(2,1)S(1)} %get-tuple-element.50.refs_1_) | copy-start | bytes 983044
  150.1 12.4 %collective-permute-start.5 = (bf16[160,1024]{1,0:T(8,128)(2,1)S(1)}, bf16[160,1024]{1,0:T(8,128)(2,1)S(1)}, u32[]{:S(2)}, u32[]{:S(2)}) collective-permute-start(bf16[160,1024]{1,0:T(8,128)(2,1)S(1)} %get-tuple-element.49.refs_0_), channel_id=1, source_target_pairs={{0,193},{1,0},{64,1},{65,64},{128,65},{129,128},{192,129},{193,192... | collective-permute-start | bytes 983048 | tf_op jit(solution)/shard_map/ppermute | solution.py:224
  154.0 10.0 %collective-permute-start.6 = (bf16[160,1024]{1,0:T(8,128)(2,1)S(1)}, bf16[160,1024]{1,0:T(8,128)(2,1)S(1)}, u32[]{:S(2)}, u32[]{:S(2)}) collective-permute-start(bf16[160,1024]{1,0:T(8,128)(2,1)S(1)} %get-tuple-element.50.refs_1_), channel_id=1, source_target_pairs={{0,1},{1,64},{64,65},{65,128},{128,129},{129,192},{192,193},{193,0... | collective-permute-start | bytes 983048 | tf_op jit(solution)/shard_map/ppermute | solution.py:224
  154.9 15.8 %collective-permute-start.4 = (bf16[160,1024]{1,0:T(8,128)(2,1)S(1)}, bf16[160,1024]{1,0:T(8,128)(2,1)S(1)}, u32[]{:S(2)}, u32[]{:S(2)}) collective-permute-start(bf16[160,1024]{1,0:T(8,128)(2,1)S(1)} %get-tuple-element.49.refs_0_), channel_id=1, source_target_pairs={{0,1},{1,64},{64,65},{65,128},{128,129},{129,192},{192,193},{193,0... | collective-permute-start | bytes 983048 | tf_op jit(solution)/shard_map/ppermute | solution.py:224
  156.4 14.4 %collective-permute-start.7 = (bf16[160,1024]{1,0:T(8,128)(2,1)S(1)}, bf16[160,1024]{1,0:T(8,128)(2,1)S(1)}, u32[]{:S(2)}, u32[]{:S(2)}) collective-permute-start(bf16[160,1024]{1,0:T(8,128)(2,1)S(1)} %get-tuple-element.50.refs_1_), channel_id=1, source_target_pairs={{0,193},{1,0},{64,1},{65,64},{128,65},{129,128},{192,129},{193,192... | collective-permute-start | bytes 983048 | tf_op jit(solution)/shard_map/ppermute | solution.py:224
  162.6 65.2 %copy-start.5 = (bf16[160,1024]{1,0:T(8,128)(2,1)}, bf16[160,1024]{1,0:T(8,128)(2,1)S(1)}, u32[]{:S(2)}) copy-start(bf16[160,1024]{1,0:T(8,128)(2,1)S(1)} %collective-permute-done.5.refs_3_) | copy-start | bytes 983044
  162.6 14.1 %collective-permute-start.9 = (bf16[160,1024]{1,0:T(8,128)(2,1)S(1)}, bf16[160,1024]{1,0:T(8,128)(2,1)}, u32[]{:S(2)}, u32[]{:S(2)}) collective-permute-start(bf16[160,1024]{1,0:T(8,128)(2,1)S(1)} %collective-permute-done.5.refs_3_), channel_id=1, source_target_pairs={{0,193},{1,0},{64,1},{65,64},{128,65},{129,128},{192,129},{193,192... | collective-permute-start | bytes 983048 | tf_op jit(solution)/shard_map/ppermute | solution.py:224
  164.0 63.7 %copy-start.6 = (bf16[160,1024]{1,0:T(8,128)(2,1)}, bf16[160,1024]{1,0:T(8,128)(2,1)S(1)}, u32[]{:S(2)}) copy-start(bf16[160,1024]{1,0:T(8,128)(2,1)S(1)} %collective-permute-done.6.refs_4_) | copy-start | bytes 983044
  164.0 14.1 %collective-permute-start.10 = (bf16[160,1024]{1,0:T(8,128)(2,1)S(1)}, bf16[160,1024]{1,0:T(8,128)(2,1)}, u32[]{:S(2)}, u32[]{:S(2)}) collective-permute-start(bf16[160,1024]{1,0:T(8,128)(2,1)S(1)} %collective-permute-done.6.refs_4_), channel_id=1, source_target_pairs={{0,1},{1,64},{64,65},{65,128},{128,129},{129,192},{192,193},{193,0... | collective-permute-start | bytes 983048 | tf_op jit(solution)/shard_map/ppermute | solution.py:224
  170.7 57.1 %copy-start.7 = (bf16[160,1024]{1,0:T(8,128)(2,1)}, bf16[160,1024]{1,0:T(8,128)(2,1)S(1)}, u32[]{:S(2)}) copy-start(bf16[160,1024]{1,0:T(8,128)(2,1)S(1)} %collective-permute-done.4.refs_2_) | copy-start | bytes 983044
  170.7 30.5 %collective-permute-start.8 = (bf16[160,1024]{1,0:T(8,128)(2,1)S(1)}, bf16[160,1024]{1,0:T(8,128)(2,1)}, u32[]{:S(2)}, u32[]{:S(2)}) collective-permute-start(bf16[160,1024]{1,0:T(8,128)(2,1)S(1)} %collective-permute-done.4.refs_2_), channel_id=1, source_target_pairs={{0,1},{1,64},{64,65},{65,128},{128,129},{129,192},{192,193},{193,0... | collective-permute-start | bytes 983048 | tf_op jit(solution)/shard_map/ppermute | solution.py:224
  170.7 57.0 %copy-start.8 = (bf16[160,1024]{1,0:T(8,128)(2,1)}, bf16[160,1024]{1,0:T(8,128)(2,1)S(1)}, u32[]{:S(2)}) copy-start(bf16[160,1024]{1,0:T(8,128)(2,1)S(1)} %collective-permute-done.7.refs_5_) | copy-start | bytes 983044
  170.7 31.6 %collective-permute-start.11 = (bf16[160,1024]{1,0:T(8,128)(2,1)S(1)}, bf16[160,1024]{1,0:T(8,128)(2,1)}, u32[]{:S(2)}, u32[]{:S(2)}) collective-permute-start(bf16[160,1024]{1,0:T(8,128)(2,1)S(1)} %collective-permute-done.7.refs_5_), channel_id=1, source_target_pairs={{0,193},{1,0},{64,1},{65,64},{128,65},{129,128},{192,129},{193,192... | collective-permute-start | bytes 983048 | tf_op jit(solution)/shard_map/ppermute | solution.py:224
  176.7 27.2 %collective-permute-start.13 = (bf16[160,1024]{1,0:T(8,128)(2,1)}, bf16[160,1024]{1,0:T(8,128)(2,1)}, u32[]{:S(2)}, u32[]{:S(2)}) collective-permute-start(bf16[160,1024]{1,0:T(8,128)(2,1)} %collective-permute-done.9.refs_7_), channel_id=1, source_target_pairs={{0,193},{1,0},{64,1},{65,64},{128,65},{129,128},{192,129},{193,192... | collective-permute-start | bytes 983048 | tf_op jit(solution)/shard_map/ppermute | solution.py:224
  178.2 26.2 %collective-permute-start.14 = (bf16[160,1024]{1,0:T(8,128)(2,1)}, bf16[160,1024]{1,0:T(8,128)(2,1)}, u32[]{:S(2)}, u32[]{:S(2)}) collective-permute-start(bf16[160,1024]{1,0:T(8,128)(2,1)} %collective-permute-done.10.refs_8_), channel_id=1, source_target_pairs={{0,1},{1,64},{64,65},{65,128},{128,129},{129,192},{192,193},{193,0... | collective-permute-start | bytes 983048 | tf_op jit(solution)/shard_map/ppermute | solution.py:224
  178.2 13.7 %all-to-all-start.4 = ((f32[8,1,128]{2,1,0:T(1,128)}), f32[8,1,128]{2,1,0:T(1,128)S(1)}, u32[]{:S(2)}, u32[]{:S(2)}) async-start(f32[8,1,128]{2,1,0:T(1,128)} %bitcast.21), calls=%async_computation.4 | async-start | bytes 8192 | tf_op jit(solution)/shard_map/all_to_all | solution.py:300
  182.2 45.6 %copy-start.15 = (s32[2]{0:T(128)}, s32[2]{0:T(128)S(1)}, u32[]{:S(2)}) copy-start(s32[2]{0:T(128)S(1)} %pad_add_fusion.where_ref) | copy-start | bytes 28
  192.6 15.5 %all-to-all-start.5 = ((f32[32,1,128]{2,1,0:T(1,128)}), f32[32,1,128]{2,1,0:T(1,128)S(1)}, u32[]{:S(2)}, u32[]{:S(2)}) async-start(f32[32,1,128]{2,1,0:T(1,128)} %broadcast_in_dim.35), calls=%async_computation.5 | async-start | bytes 32768 | tf_op jit(solution)/shard_map/all_to_all | solution.py:214
  201.2 10.7 %collective-permute-start.12 = (bf16[160,1024]{1,0:T(8,128)(2,1)}, bf16[160,1024]{1,0:T(8,128)(2,1)}, u32[]{:S(2)}, u32[]{:S(2)}) collective-permute-start(bf16[160,1024]{1,0:T(8,128)(2,1)} %collective-permute-done.8.refs_6_), channel_id=1, source_target_pairs={{0,1},{1,64},{64,65},{65,128},{128,129},{129,192},{192,193},{193,0... | collective-permute-start | bytes 983048 | tf_op jit(solution)/shard_map/ppermute | solution.py:224
  202.3 9.5 %collective-permute-start.15 = (bf16[160,1024]{1,0:T(8,128)(2,1)}, bf16[160,1024]{1,0:T(8,128)(2,1)}, u32[]{:S(2)}, u32[]{:S(2)}) collective-permute-start(bf16[160,1024]{1,0:T(8,128)(2,1)} %collective-permute-done.11.refs_9_), channel_id=1, source_target_pairs={{0,193},{1,0},{64,1},{65,64},{128,65},{129,128},{192,129},{193,192... | collective-permute-start | bytes 983048 | tf_op jit(solution)/shard_map/ppermute | solution.py:224
  204.0 14.5 %collective-permute-start.16 = (bf16[160,1024]{1,0:T(8,128)(2,1)}, bf16[160,1024]{1,0:T(8,128)(2,1)}, u32[]{:S(2)}, u32[]{:S(2)}) collective-permute-start(bf16[160,1024]{1,0:T(8,128)(2,1)} %collective-permute-done.13.refs_11_), channel_id=1, source_target_pairs={{0,193},{1,0},{64,1},{65,64},{128,65},{129,128},{192,129},{193,192... | collective-permute-start | bytes 983048 | tf_op jit(solution)/shard_map/ppermute | solution.py:224
  204.4 14.5 %collective-permute-start.17 = (bf16[160,1024]{1,0:T(8,128)(2,1)}, bf16[160,1024]{1,0:T(8,128)(2,1)}, u32[]{:S(2)}, u32[]{:S(2)}) collective-permute-start(bf16[160,1024]{1,0:T(8,128)(2,1)} %collective-permute-done.14.refs_12_), channel_id=1, source_target_pairs={{0,1},{1,64},{64,65},{65,128},{128,129},{129,192},{192,193},{193,0... | collective-permute-start | bytes 983048 | tf_op jit(solution)/shard_map/ppermute | solution.py:224
  218.9 1.7 copy-start.1
  227.8 3.4 %collective-permute-start.18 = (f32[16,32,512]{2,1,0:T(8,128)S(1)}, f32[16,32,512]{2,1,0:T(8,128)S(1)}, u32[]{:S(2)}, u32[]{:S(2)}) collective-permute-start(f32[16,32,512]{2,1,0:T(8,128)S(1)} %get-tuple-element.66), channel_id=1, source_target_pairs={{0,2},{2,0},{4,6},{6,4},{8,10},{10,8},{12,14},{14,12},{16,18},{18,... | collective-permute-start | bytes 3145736 | tf_op jit(solution)/shard_map/ppermute | solution.py:308
  232.2 17.6 %all-to-all-start.6 = ((bf16[16,32,512]{2,1,0:T(8,128)(2,1)}), bf16[16,32,512]{2,1,0:T(8,128)(2,1)S(1)}, u32[]{:S(2)}, u32[]{:S(2)}) async-start(bf16[16,32,512]{2,1,0:T(8,128)(2,1)} %add_convert_fusion), calls=%async_computation.6 | async-start | bytes 1048576 | tf_op jit(solution)/shard_map/all_to_all | solution.py:310
Sparse Core Ops, SparseCore 0:
  29.2 56.4 all-gather.1

commit v3 on v2

v3 whole, which is shorter than its diff:
```python
import functools
import math

import jax
import jax.numpy as jnp
from jax import lax
from jax.experimental import pallas as pl
from jax.experimental.pallas import tpu as pltpu
from jax.sharding import PartitionSpec as P

LOSS_SCALE = 65536
F32 = jnp.float32
BF16 = jnp.bfloat16
RING = ("tok", "sub")


def row_weights(sizes, rows):
    count = sizes.shape[0]
    upto = lax.broadcasted_iota(jnp.int32, (count, count), 0) <= lax.broadcasted_iota(
        jnp.int32, (count, count), 1
    )
    ends = jnp.sum(jnp.where(upto, sizes[:, None], 0), axis=0)
    starts = ends - sizes
    ids = lax.broadcasted_iota(jnp.int32, (count, rows), 1)
    member = (ids >= starts[:, None]) & (ids < ends[:, None])
    lengths = jnp.sum(jnp.where(member, sizes[:, None], 0), axis=0).astype(F32)
    return F32(LOSS_SCALE) / (F32(count) * lengths)


MIB = 1024 * 1024
VMEM = pl.BlockSpec(memory_space=pltpu.VMEM)
SMEM = pl.BlockSpec(memory_space=pltpu.SMEM)
HBM = pl.BlockSpec(memory_space=pl.ANY)


def params(mib):
    return pltpu.CompilerParams(vmem_limit_bytes=mib * MIB)


def log_sum_exp(values):
    top = jnp.max(values, axis=0, keepdims=True)
    return top + jnp.log(jnp.sum(jnp.exp(values - top), axis=0, keepdims=True))


def merged(stats):
    k = stats.shape[1] // 3
    student, teacher, cross = stats[:, :k], stats[:, k : 2 * k], stats[:, 2 * k :]
    student_lse, teacher_lse = log_sum_exp(student), log_sum_exp(teacher)
    cross = jnp.sum(jnp.exp(teacher - teacher_lse) * cross, axis=0)
    return student_lse[0], teacher_lse[0], cross


def place_columns(voc, side, array_refs, origins, out_ref, sem):
    core, chip = lax.rem(voc, 2), voc // 2
    x, y = chip // side, lax.rem(chip, side)
    copies = []
    for array_ref, (steps, other, which) in zip(array_refs, origins):
        half = array_ref.shape[0] // len(steps)
        for index, (back_x, back_y) in enumerate(steps):
            from_x = lax.rem(x + side - back_x, side)
            from_y = lax.rem(y + side - back_y, side)
            from_core = 1 - core if other else core
            start = ((from_x * side + from_y) * 2 + from_core) * (2 * half) + which * half
            copy = pltpu.make_async_copy(
                array_ref.at[index * half : (index + 1) * half],
                out_ref.at[pl.ds(pl.multiple_of(start, half), half)],
                sem.at[len(copies)],
            )
            copy.start()
            copies.append(copy)
    return copies


def student_kernel(order, side, origins, where_ref, head_ref, teacher_ref, *refs):
    arrays, rest = refs[: len(origins)], refs[len(origins) :]
    student_ref, stats_ref, own_ref, features, sem = rest
    depth = head_ref.shape[2]
    for copy in place_columns(where_ref[2], side, arrays, origins, features, sem):
        copy.wait()
    mine = pl.multiple_of(where_ref[0] * depth, depth)
    own_ref[...] = features[pl.ds(mine, depth), :]
    copies, height, lanes = stats_ref.shape
    toks, _, width = teacher_ref.shape

    @pl.loop(0, toks)
    def _(i):
        cols = pl.ds(pl.multiple_of(i * width, width), width)
        student = None
        for index, block in enumerate(order):
            part = jnp.dot(
                head_ref[index],
                features[block * depth : (block + 1) * depth, cols],
                preferred_element_type=F32,
            )
            student = part if student is None else student + part
        student_ref[:, cols] = student
        teacher = teacher_ref[i].astype(F32)
        student_lse, teacher_lse = log_sum_exp(student), log_sum_exp(teacher)
        cross = jnp.sum(
            jnp.exp(teacher - teacher_lse) * (teacher - student), axis=0, keepdims=True
        )
        pieces = width // lanes
        for index, row in enumerate((student_lse, teacher_lse, cross)):
            for piece in range(pieces):
                place = index * (height // 3) + i * pieces + piece
                values = row[:, piece * lanes : (piece + 1) * lanes]
                stats_ref[:, pl.ds(place, 1), :] = jnp.broadcast_to(
                    values[None], (copies, 1, lanes)
                )


def student_logits(where, head, teachers, arrays, origins, side, subs):
    blocks, v, d = head.shape
    toks, _, width = teachers.shape
    r = toks * width
    order = [i % toks * subs + i // toks for i in range(blocks)]
    count = sum(len(steps) for steps, _, _ in origins)
    return pl.pallas_call(
        functools.partial(student_kernel, order, side, origins),
        in_specs=[SMEM] + [VMEM] * 2 + [HBM] * len(arrays),
        out_specs=[VMEM] * 3,
        out_shape=[
            jax.ShapeDtypeStruct((v, r), F32),
            jax.ShapeDtypeStruct((blocks, 3 * r // 128, 128), F32),
            jax.ShapeDtypeStruct((d, r), BF16),
        ],
        scratch_shapes=[pltpu.VMEM((blocks * d, r), BF16), pltpu.SemaphoreType.DMA((count,))],
        compiler_params=params(58),
        cost_estimate=pl.CostEstimate(
            flops=2 * r * v * d * blocks, bytes_accessed=12 * MIB, transcendentals=0
        ),
    )(where, head, teachers, *arrays)


def merge(stats):
    return jnp.concatenate(merged(stats))


def grad_kernel(
    where_ref, stats_ref, weight_ref, student_ref, teacher_ref, low_ref, high_ref, divergence_ref
):
    student_lse, teacher_lse, cross = merged(stats_ref[...])
    divergence = cross + student_lse - teacher_lse
    index = lax.broadcasted_iota(jnp.int32, divergence.shape, 0)
    divergence_ref[...] = jnp.sum(
        jnp.where(index == where_ref[0], divergence, 0.0), axis=0, keepdims=True
    )
    half, rows = low_ref.shape
    width = teacher_ref.shape[2]
    for j in range(rows // 128):
        cols = slice(j * 128, (j + 1) * 128)
        inner = slice(j * 128 % width, j * 128 % width + 128)
        teacher = teacher_ref[j * 128 // width, :, inner].astype(F32)
        grad = weight_ref[j : j + 1, :] * (
            jnp.exp(student_ref[:, cols] - student_lse[j : j + 1, :])
            - jnp.exp(teacher - teacher_lse[j : j + 1, :])
        )
        grad = grad.astype(BF16)
        low_ref[:, cols] = grad[:half]
        high_ref[:, cols] = grad[half:]


def logit_grads(where, stats, weights, student, teachers):
    v, r = student.shape
    return pl.pallas_call(
        grad_kernel,
        in_specs=[SMEM] + [VMEM] * 4,
        out_specs=[VMEM] * 3,
        out_shape=[
            jax.ShapeDtypeStruct((v // 2, r), BF16),
            jax.ShapeDtypeStruct((v // 2, r), BF16),
            jax.ShapeDtypeStruct((1, 128), F32),
        ],
        compiler_params=params(58),
    )(where, stats, weights, student, teachers)


def ring_slot(where_ref, back, ring):
    origin = lax.rem(where_ref[0] + ring - back, ring)
    return lax.rem(origin, 2) * (ring // 2) + origin // 2


def fetch_blocks(where_ref, block_refs, hops, all_ref, sem):
    height = block_refs[0].shape[0]
    ring = all_ref.shape[0] // (2 * height)
    copies = []
    for index, (block_ref, (back, half)) in enumerate(zip(block_refs, hops)):
        slot = ring_slot(where_ref, back, ring)
        start = pl.multiple_of(slot * (2 * height) + half * height, 16)
        copies.append(
            pltpu.make_async_copy(block_ref, all_ref.at[pl.ds(start, height)], sem.at[index])
        )
    for copy in copies:
        copy.start()
    for copy in copies:
        copy.wait()


def early_kernel(hops, where_ref, *refs):
    blocks, (head_ref, out_ref, all_ref, sem) = refs[: len(hops)], refs[len(hops) :]
    height = blocks[0].shape[0]
    ring = all_ref.shape[0] // (2 * height)
    for back in range(ring):
        if (back, 0) not in hops:
            missing = ring_slot(where_ref, back, ring) * (2 * height)
            empty = all_ref.at[pl.ds(pl.multiple_of(missing, 2 * height), 2 * height)]
            empty[...] = jnp.zeros(empty.shape, BF16)
    fetch_blocks(where_ref, blocks, hops, all_ref, sem)
    tile = 256

    @pl.loop(0, all_ref.shape[1] // tile)
    def _(i):
        rows = pl.ds(pl.multiple_of(i * tile, tile), tile)
        out_ref[rows, :] = jnp.dot(
            head_ref[...], all_ref[:, rows], preferred_element_type=F32
        ).T


def early_features(where, blocks, hops, head):
    depth, vocab = head.shape
    rows = blocks[0].shape[1]
    return pl.pallas_call(
        functools.partial(early_kernel, hops),
        in_specs=[SMEM] + [HBM] * len(blocks) + [VMEM],
        out_specs=VMEM,
        out_shape=jax.ShapeDtypeStruct((rows, depth), F32),
        scratch_shapes=[pltpu.VMEM((vocab, rows), BF16), pltpu.SemaphoreType.DMA((len(blocks),))],
        compiler_params=params(32),
        cost_estimate=pl.CostEstimate(
            flops=2 * rows * depth * vocab, bytes_accessed=8 * MIB, transcendentals=0
        ),
    )(where, *blocks, head)


def late_kernel(ring, hops, where_ref, *refs):
    block_refs, rest = refs[: len(hops)], refs[len(hops) :]
    head_ref, part_ref, keep_ref, give_ref, window, block, sem = rest
    height = block_refs[0].shape[0]
    backs = sorted({back for back, _ in hops})
    span = window.shape[1] // len(backs)
    gap = span - 2 * height
    copies = []
    for index, back in enumerate(backs):
        offset = ring_slot(where_ref, back, ring) * (2 * height)
        start = pl.multiple_of(offset // 128 * 128, 128)
        base = index * span
        copy = pltpu.make_async_copy(
            head_ref.at[:, pl.ds(start, span)], window.at[:, base : base + span], sem.at[index]
        )
        copy.start()
        copies.append(copy)
        block[base : base + gap] = jnp.zeros((gap, block.shape[1]), BF16)
        block[base + span - gap : base + span] = jnp.zeros((gap, block.shape[1]), BF16)
        for block_ref, hop in zip(block_refs, hops):
            if hop[0] == back:
                at = pl.multiple_of(base + offset - start + hop[1] * height, 32)
                block[pl.ds(at, height)] = block_ref[...]
    for copy in copies:
        copy.wait()
    first = where_ref[1] == 0
    tile = 256
    per = keep_ref.shape[1]
    chips = tile // (2 * per)

    @pl.loop(0, block.shape[1] // tile)
    def _(i):
        rows = pl.ds(pl.multiple_of(i * tile, tile), tile)
        part = jnp.dot(window[...], block[:, rows], preferred_element_type=F32).T
        part = part + part_ref[rows, :]
        part = part.reshape(chips, 2, per, part.shape[1])
        even, odd = part[:, 0], part[:, 1]
        keep_ref[pl.ds(i * chips, chips)] = jnp.where(first, even, odd)
        give_ref[pl.ds(i * chips, chips)] = jnp.where(first, odd, even)


def late_features(where, blocks, hops, head, part, ring, per):
    depth, _ = head.shape
    height, rows = blocks[0].shape
    count = len({back for back, _ in hops})
    span = -(-2 * height // 128) * 128
    shape = jax.ShapeDtypeStruct((rows // (2 * per), per, depth), F32)
    return pl.pallas_call(
        functools.partial(late_kernel, ring, hops),
        in_specs=[SMEM] + [VMEM] * len(blocks) + [HBM, VMEM],
        out_specs=[VMEM] * 2,
        out_shape=[shape, shape],
        scratch_shapes=[
            pltpu.VMEM((depth, count * span), BF16),
            pltpu.VMEM((count * span, rows), BF16),
            pltpu.SemaphoreType.DMA((count,)),
        ],
        compiler_params=params(32),
        cost_estimate=pl.CostEstimate(
            flops=2 * rows * depth * span * count, bytes_accessed=6 * MIB, transcendentals=0
        ),
    )(where, *blocks, head, part)


def head_kernel(hops, where_ref, *refs):
    blocks, rest = refs[: len(hops)], refs[len(hops) :]
    features_ref, out_ref, own_ref, all_ref, sem = rest
    step = pl.program_id(0)

    @pl.when(step == 0)
    def _():
        fetch_blocks(where_ref, blocks, hops, all_ref, sem)

    share, tile = own_ref.shape
    own_cols = pl.ds(pl.multiple_of(where_ref[0] * share, share), share)
    rows = pl.ds(pl.multiple_of(step * tile, tile), tile)
    out_ref[...] = lax.dot_general(
        features_ref[...], all_ref[rows, :], (((1,), (1,)), ((), ())), preferred_element_type=F32
    )
    own_ref[...] = all_ref[rows, own_cols].astype(F32).T.astype(BF16)


def head_parts(where, blocks, hops, features, vocab, share):
    depth, rows = features.shape
    tile = 512
    return pl.pallas_call(
        functools.partial(head_kernel, hops),
        grid=(vocab // tile,),
        in_specs=[SMEM] + [HBM] * len(blocks) + [pl.BlockSpec((depth, rows), lambda i: (0, 0))],
        out_specs=[
            pl.BlockSpec((depth, tile), lambda i: (0, i)),
            pl.BlockSpec((share, tile), lambda i: (0, i)),
        ],
        out_shape=[
            jax.ShapeDtypeStruct((depth, vocab), F32),
            jax.ShapeDtypeStruct((share, vocab), BF16),
        ],
        scratch_shapes=[
            pltpu.VMEM((vocab, rows), BF16),
            pltpu.SemaphoreType.DMA((len(blocks),)),
        ],
        compiler_params=params(58),
        cost_estimate=pl.CostEstimate(
            flops=2 * rows * depth * vocab, bytes_accessed=12 * MIB, transcendentals=0
        ),
    )(where, *blocks, features)


def ring_shift(values, step, size):
    return lax.ppermute(values, RING, [(i, (i + step) % size) for i in range(size)])


def ring_gather(halves, size):
    blocks, hops = list(halves), [(0, 0), (0, 1)]
    ahead, behind = list(halves), list(halves)
    for step in range(1, size // 2 + 1):
        last = step == size // 2
        for half in range(2):
            if not last or half == 1:
                ahead[half] = ring_shift(ahead[half], 1, size)
                blocks.append(ahead[half])
                hops.append((step, half))
            if not last or half == 0:
                behind[half] = ring_shift(behind[half], -1, size)
                blocks.append(behind[half])
                hops.append((size - step, half))
    return blocks, hops


def to_all(values, axis, **groups):
    size = lax.axis_size(axis)
    if groups:
        size = len(groups["axis_index_groups"][0])
    return lax.all_to_all(jnp.broadcast_to(values[None], (size,) + values.shape), axis, 0, 0, **groups)


def spread(column, chips_x, chips_y):
    def shift(values, x, y, core):
        pairs = []
        for i in range(chips_x):
            for j in range(chips_y):
                for c in range(2):
                    target = ((i + x) % chips_x * chips_y + (j + y) % chips_y) * 2 + (c ^ core)
                    pairs.append(((i * chips_y + j) * 2 + c, target))
        return lax.ppermute(values, "voc", pairs)

    half = column.shape[0] // 2
    first, second = column[:half], column[half:]
    along_x = [first] + [shift(first, k, 0, 0) for k in range(1, chips_x)]
    along_y = [second] + [shift(second, 0, k, 0) for k in range(1, chips_y)]
    along_x, along_y = lax.optimization_barrier((along_x, along_y))
    first, second = jnp.concatenate(along_x), jnp.concatenate(along_y)
    arrays = [(first, [(i, 0) for i in range(chips_x)], 0), (second, [(0, i) for i in range(chips_y)], 1)]
    for k in range(1, max(chips_x, chips_y)):
        if k < chips_y:
            arrays.append((shift(first, 0, k, 0), [(i, k) for i in range(chips_x)], 0))
        if k < chips_x:
            arrays.append((shift(second, k, 0, 0), [(k, i) for i in range(chips_y)], 1))
    out, origins = [], []
    for values, steps, which in arrays:
        out += [values, shift(values, 0, 0, 1)]
        origins += [(steps, 0, which), (steps, 1, which)]
    return out, origins


def on_device(hidden, head, pool, lines, sizes):
    toks, subs, vocs = lax.axis_size("tok"), lax.axis_size("sub"), lax.axis_size("voc")
    ring = toks * subs
    chips = vocs // 2
    share, width = hidden.shape
    rows = share * ring
    depth, vocab = head.shape
    cut = vocab // ring
    kept = lines.shape[0]
    tok = lax.axis_index("tok")
    place = lax.axis_index(RING)
    voc = lax.axis_index("voc")
    where = jnp.stack([place, voc % 2, voc])
    cores = [(i, i ^ 1) for i in range(vocs)]
    groups = [[2 * i + c for i in range(chips)] for c in range(2)]

    wanted = lines - tok * pool.shape[0]
    choose = (
        lax.broadcasted_iota(jnp.int32, (pool.shape[0], kept), 0) == wanted[None, :]
    ).astype(BF16)
    picked = lax.dot_general(
        pool, choose, (((0,), (0,)), ((), ())), preferred_element_type=F32
    ).astype(BF16).reshape(toks, cut, kept)
    parts = []
    for shift in range(toks):
        part = lax.dynamic_index_in_dim(picked, (tok + shift) % toks, 0, keepdims=False)
        if shift:
            part = lax.ppermute(part, "tok", [(i, (i + shift) % toks) for i in range(toks)])
        parts.append(part)

    piece = width // vocs
    own = lax.dynamic_slice_in_dim(hidden, voc * piece, piece, 1)
    column = to_all(own, RING)
    slices = head.T.reshape(ring, cut, depth)
    slices, column, *parts = lax.optimization_barrier((slices, column, *parts))
    side = math.isqrt(chips)
    arrays, origins = spread(column.reshape(rows, piece).T, side, side)
    head_cut = lax.all_to_all(slices, ("sub", "tok"), 0, 0)
    teachers = jnp.zeros((toks, cut, kept), BF16)
    for shift, part in enumerate(parts):
        teachers = lax.dynamic_update_index_in_dim(teachers, part, (tok + toks - shift) % toks, 0)
    weights = row_weights(sizes, rows).reshape(rows // 128, 128)

    student, stats, features = student_logits(
        where, head_cut, teachers, arrays, origins, side, subs
    )
    stats = merge(lax.all_to_all(stats, RING, 0, 0))
    stats = merge(jnp.stack([stats, lax.ppermute(stats, "voc", cores)]))
    stats = jnp.broadcast_to(stats[None], (chips,) + stats.shape)
    stats = lax.all_to_all(stats, "voc", 0, 0, axis_index_groups=groups)
    low, high, divergence = logit_grads(where, stats, weights, student, teachers)
    blocks, hops = ring_gather((low, high), ring)

    part = early_features(where, blocks[:-6], hops[:-6], head)
    keep, give = late_features(where, blocks[-6:], hops[-6:], head, part, ring, rows // vocs)
    given = lax.ppermute(give, "voc", cores)
    sums, where = lax.optimization_barrier(((keep + given).astype(BF16), where))
    sums = lax.all_to_all(sums, "voc", 0, 0, axis_index_groups=groups)
    feature_grad = jnp.sum(sums.astype(F32), axis=0)

    head_grad, local_grad = head_parts(where, blocks, hops, features, vocab, share)
    return head_grad, feature_grad, local_grad, divergence.reshape(share)


def solution(mesh):
    return jax.shard_map(
        on_device,
        mesh=mesh,
        in_specs=(
            P(RING, None),
            P(RING, "voc"),
            P("tok", ("voc", "sub")),
            P("tok"),
            P(),
        ),
        out_specs=(
            P(RING, "voc"),
            P("voc", RING),
            P(RING, "voc"),
            P(RING),
        ),
        check_vma=False,
    )
```

time: 258 us -> 221 us (0.86)
  waiting for transfers between devices: 122 us -> 83.2 us
  starting transfers between devices: 68.8 us -> 87.1 us
  between operations: 14.3 us -> 1.21 us
  local copies, waits for them, and re-layouts: 16.4 us -> 12.6 us
  Pallas kernels: 29.2 us -> 32 us
    all_to_all x1, waiting for transfers between devices: 59.2 us -> 8.34 us  [on_device(): head_cut = lax.all_to_all(slices, ('sub', 'tok'), 0, 0)]
    ppermute x0 -> x20, starting transfers between devices: none -> 30.8 us  [shift(): return lax.ppermute(values, 'voc', pairs)]
    all_to_all x4 -> x1, starting transfers between devices: 29.6 us -> 9.01 us  [to_all(): lax.all_to_all(jnp.broadcast_to(values[None], (size,) + values.shape), ax...]
    ppermute x0 -> x20, waiting for transfers between devices: none -> 18.4 us  [shift(): return lax.ppermute(values, 'voc', pairs)]
    all_to_all x4 -> x1, waiting for transfers between devices: 16.3 us -> 0.01 us  [to_all(): lax.all_to_all(jnp.broadcast_to(values[None], (size,) + values.shape), ax...]
    all_to_all x1 -> x2, starting transfers between devices: 3.93 us -> 12.1 us  [the longest x1 6.88 us: on_device(): stats = lax.all_to_all(stats, 'voc', 0, 0, axis_index_groups=groups)]
    ppermute x3, starting transfers between devices: 3.49 us -> 9.02 us  [on_device(): lax.ppermute(part, 'tok', [(i, (i + shift) % toks) for i in range(toks)])]
    ppermute x14, starting transfers between devices: 17.3 us -> 13.1 us  [ring_shift(): lax.ppermute(values, RING, [(i, (i + step) % size) for i in range(size)])]
  transfers between devices with their start and end apart: 27 -> 44, of which waited for: 15 -> 26; matrix products, arithmetic and copies ran while one was open for 4% -> 3% of each run, Pallas kernels for 4% -> 7%
where the time goes in v3:
time: 221 us
  starting transfers between devices  87.1 us (39%)
  waiting for transfers between devices  83.2 us (38%)
  Pallas kernels  32 us (14%)
  local copies, waits for them, and re-layouts  12.6 us (6%)
  other arithmetic  3.83 us (2%)
    ppermute x20, starting transfers between devices, shift(): return lax.ppermute(values, 'voc', pairs)  30.8 us
    ppermute x14, waiting for transfers between devices, ring_shift(): lax.ppermute(values, RING, [(i, (i + step) % size) for i in range(size)])  28.3 us
    ppermute x20, waiting for transfers between devices, shift(): return lax.ppermute(values, 'voc', pairs)  18.4 us
    ppermute x14, starting transfers between devices, ring_shift(): lax.ppermute(values, RING, [(i, (i + step) % size) for i in range(size)])  13.1 us
    pallas_call x1, Pallas kernels, student_logits(): pl.pallas_call(functools.partial(student_kernel, order, side, origins), i...  11.2 us
    ppermute x3, waiting for transfers between devices, on_device(): lax.ppermute(part, 'tok', [(i, (i + shift) % toks) for i in range(toks)])  10.1 us
    pallas_call x1, Pallas kernels, head_parts(): pl.pallas_call(functools.partial(head_kernel, hops), grid=(vocab // tile,...  9.08 us
    ppermute x3, starting transfers between devices, on_device(): lax.ppermute(part, 'tok', [(i, (i + shift) % toks) for i in range(toks)])  9.02 us
  transfers between devices with their start and end apart: 44, of which 26 were waited for; matrix products, arithmetic and copies ran while one was open for 3% of the time, Pallas kernels for 7%

profile of v3, /device:TPU:1, one launch (start us, length us, event | category | flops | bytes accessed | tf_op | source)
XLA Modules:
  0.0 220.5 jit_solution(13920520976597941676)
XLA Ops:
  0.7 0.9 constant_dynamic-slice_fusion
  1.6 0.7 broadcast_in_dim.65
  2.4 9.0 %all-to-all-start = ((bf16[8,128,128]{1,2,0:T(8,128)(2,1)}), bf16[8,128,128]{1,2,0:T(8,128)(2,1)S(1)}, u32[]{:S(2)}, u32[]{:S(2)}) async-start(bf16[8,128,128]{1,2,0:T(8,128)(2,1)} %broadcast_in_dim.65), calls=%async_computation | async-start | bytes 524288 | tf_op jit(solution)/shard_map/all_to_all | solution.py:368
  13.0 2.4 %collective-permute-start = (bf16[320,256]{1,0:T(8,128)(2,1)S(1)}, bf16[320,256]{1,0:T(8,128)(2,1)S(1)}, u32[]{:S(2)}, u32[]{:S(2)}) collective-permute-start(bf16[320,256]{1,0:T(8,128)(2,1)S(1)} %get-tuple-element.66), channel_id=1, source_target_pairs={{0,64},{64,128},{128,192},{192,0},{1,65},{65,129},{129,193},{193,1... | collective-permute-start | bytes 491528 | tf_op jit(solution)/shard_map/ppermute | solution.py:427
  15.4 3.3 %collective-permute-start.1 = (bf16[320,256]{1,0:T(8,128)(2,1)S(1)}, bf16[320,256]{1,0:T(8,128)(2,1)S(1)}, u32[]{:S(2)}, u32[]{:S(2)}) collective-permute-start(bf16[320,256]{1,0:T(8,128)(2,1)S(1)} %get-tuple-element.65), channel_id=1, source_target_pairs={{0,128},{64,192},{128,0},{192,64},{1,129},{65,193},{129,1},{193,65... | collective-permute-start | bytes 491528 | tf_op jit(solution)/shard_map/ppermute | solution.py:427
  18.7 3.3 %collective-permute-start.2 = (bf16[320,256]{1,0:T(8,128)(2,1)S(1)}, bf16[320,256]{1,0:T(8,128)(2,1)S(1)}, u32[]{:S(2)}, u32[]{:S(2)}) collective-permute-start(bf16[320,256]{1,0:T(8,128)(2,1)S(1)} %get-tuple-element.64), channel_id=1, source_target_pairs={{0,192},{64,0},{128,64},{192,128},{1,193},{65,1},{129,65},{193,129... | collective-permute-start | bytes 491528 | tf_op jit(solution)/shard_map/ppermute | solution.py:427
  22.0 4.4 %copy.22 = bf16[2560,512]{1,0:T(8,128)(2,1)} copy(bf16[2560,512]{0,1:T(8,128)(2,1)} %bitcast.38) | data formatting | bytes 5242880 | tf_op jit(solution)/shard_map/transpose | solution.py:433
  26.4 7.7 %collective-permute-done.1 = bf16[320,256]{1,0:T(8,128)(2,1)S(1)} collective-permute-done((bf16[320,256]{1,0:T(8,128)(2,1)S(1)}, bf16[320,256]{1,0:T(8,128)(2,1)S(1)}, u32[]{:S(2)}, u32[]{:S(2)}) %collective-permute-start.1) | collective-permute-done | bytes 163872 | tf_op jit(solution)/shard_map/ppermute | solution.py:427
  34.1 2.4 %collective-permute-done.2 = bf16[320,256]{1,0:T(8,128)(2,1)S(1)} collective-permute-done((bf16[320,256]{1,0:T(8,128)(2,1)S(1)}, bf16[320,256]{1,0:T(8,128)(2,1)S(1)}, u32[]{:S(2)}, u32[]{:S(2)}) %collective-permute-start.2) | collective-permute-done | bytes 163872 | tf_op jit(solution)/shard_map/ppermute | solution.py:427
  36.5 4.4 %all-to-all-start.1 = ((bf16[8,320,512]{2,1,0:T(8,128)(2,1)}), bf16[8,320,512]{2,1,0:T(8,128)(2,1)}, u32[]{:S(2)}, u32[]{:S(2)}) async-start(bf16[8,320,512]{2,1,0:T(8,128)(2,1)} %bitcast.39), calls=%async_computation.1 | async-start | bytes 5242880 | tf_op jit(solution)/shard_map/all_to_all | solution.py:437
  41.0 1.3 collective-permute-start.3
  42.2 2.5 %collective-permute-start.4 = (bf16[64,1024]{1,0:T(8,128)(2,1)S(1)}, bf16[64,1024]{1,0:T(8,128)(2,1)S(1)}, u32[]{:S(2)}, u32[]{:S(2)}) collective-permute-start(bf16[64,1024]{1,0:T(8,128)(2,1)S(1)} %get-tuple-element.36), channel_id=1, source_target_pairs={{0,32},{2,34},{4,36},{6,38},{8,40},{10,42},{12,44},{14,46},{16,48}... | collective-permute-start | bytes 393224 | tf_op jit(solution)/shard_map/ppermute | solution.py:379
  44.7 1.2 collective-permute-start.5
  45.9 1.3 collective-permute-start.6
  47.1 2.6 %collective-permute-start.7 = (bf16[64,1024]{1,0:T(8,128)(2,1)S(1)}, bf16[64,1024]{1,0:T(8,128)(2,1)S(1)}, u32[]{:S(2)}, u32[]{:S(2)}) collective-permute-start(bf16[64,1024]{1,0:T(8,128)(2,1)S(1)} %get-tuple-element.40), channel_id=1, source_target_pairs={{0,8},{2,10},{4,12},{6,14},{8,0},{10,2},{12,4},{14,6},{16,24},{18,... | collective-permute-start | bytes 393224 | tf_op jit(solution)/shard_map/ppermute | solution.py:379
  49.8 1.1 collective-permute-start.8
  51.3 3.6 %collective-permute-done.7 = bf16[64,1024]{1,0:T(8,128)(2,1)S(1)} collective-permute-done((bf16[64,1024]{1,0:T(8,128)(2,1)S(1)}, bf16[64,1024]{1,0:T(8,128)(2,1)S(1)}, u32[]{:S(2)}, u32[]{:S(2)}) %collective-permute-start.7) | collective-permute-done | bytes 131104 | tf_op jit(solution)/shard_map/ppermute | solution.py:379
  55.5 1.7 collective-permute-start.9
  57.4 0.9 collective-permute-start.11
  58.6 2.6 %collective-permute-start.15 = (bf16[256,1024]{1,0:T(8,128)(2,1)S(1)}, bf16[256,1024]{1,0:T(8,128)(2,1)}, u32[]{:S(2)}, u32[]{:S(2)}) collective-permute-start(bf16[256,1024]{1,0:T(8,128)(2,1)S(1)} %constant_dynamic-update-slice_fusion.refs_0_), channel_id=1, source_target_pairs={{0,8},{2,10},{4,12},{6,14},{8,0},{10,2},{12,4},{14,6},{16,24},{18,... | collective-permute-start | bytes 1572872 | tf_op jit(solution)/shard_map/ppermute | solution.py:379
  62.0 1.0 collective-permute-start.19
  63.0 8.8 %collective-permute-done.11.refs_4_ = bf16[256,1024]{1,0:T(8,128)(2,1)} collective-permute-done((bf16[256,1024]{1,0:T(8,128)(2,1)S(1)}, bf16[256,1024]{1,0:T(8,128)(2,1)}, u32[]{:S(2)}, u32[]{:S(2)}) %collective-permute-start.11) | collective-permute-done | bytes 524320 | tf_op jit(solution)/shard_map/ppermute | solution.py:379
  71.9 1.6 collective-permute-done.13.refs_6_
  73.5 0.8 copy-done.25
  74.3 11.6 %collective-permute-start.12 = (bf16[256,1024]{1,0:T(8,128)(2,1)}, bf16[256,1024]{1,0:T(8,128)(2,1)}, u32[]{:S(2)}, u32[]{:S(2)}) collective-permute-start(bf16[256,1024]{1,0:T(8,128)(2,1)} %collective-permute-done.11.refs_4_), channel_id=1, source_target_pairs={{0,2},{2,0},{4,6},{6,4},{8,10},{10,8},{12,14},{14,12},{16,18},{18,... | collective-permute-start | bytes 1572872 | tf_op jit(solution)/shard_map/ppermute | solution.py:379
  87.3 1.2 collective-permute-start.20
  88.9 0.7 collective-permute-done.16.refs_9_
  89.7 0.7 collective-permute-done.18.refs_11_
  90.4 0.7 collective-permute-done.20.refs_13_
  91.2 0.7 collective-permute-done.22.refs_15_
  91.9 8.3 %all-to-all-done.1.head_ref = bf16[8,320,512]{2,1,0:T(8,128)(2,1)} async-done(((bf16[8,320,512]{2,1,0:T(8,128)(2,1)}), bf16[8,320,512]{2,1,0:T(8,128)(2,1)}, u32[]{:S(2)}, u32[]{:S(2)}) %all-to-all-start.1) | async-done | bytes 2621472 | tf_op jit(solution)/shard_map/all_to_all | solution.py:437
  100.3 11.2 %shard_map.84 = (f32[320,1024]{1,0:T(8,128)}, f32[8,24,128]{2,1,0:T(8,128)}, bf16[512,1024]{1,0:T(8,128)(2,1)}) custom-call(s32[3]{0:T(128)} %pad_add_fusion.where_ref, bf16[8,320,512]{2,1,0:T(8,128)(2,1)} %all-to-all-done.1.head_ref, bf16[4,320,256]{2,1,0:T(8,128)(2,1)} %copy-done.19, bf16[256,1024]{1,0:T(8,128)(2,1)} %copy-done.20, ...), custom_call_target="tpu_custom_call" | custom-call | flops 2684354560 | bytes 12582912 | tf_op jit(solution)/shard_map/pallas_call | solution.py:118
  111.5 5.2 %all-to-all-start.2 = ((f32[8,24,128]{2,1,0:T(8,128)}), f32[8,24,128]{2,1,0:T(8,128)S(1)}, u32[]{:S(2)}, u32[]{:S(2)}) async-start(f32[8,24,128]{2,1,0:T(8,128)} %get-tuple-element.44), calls=%async_computation.2 | async-start | bytes 196608 | tf_op jit(solution)/shard_map/all_to_all | solution.py:446
  116.8 7.3 %all-to-all-done.2 = f32[8,24,128]{2,1,0:T(8,128)S(1)} async-done(((f32[8,24,128]{2,1,0:T(8,128)}), f32[8,24,128]{2,1,0:T(8,128)S(1)}, u32[]{:S(2)}, u32[]{:S(2)}) %all-to-all-start.2) | async-done | bytes 98336 | tf_op jit(solution)/shard_map/all_to_all | solution.py:446
  124.2 2.2 %collective-permute-start.23 = (f32[24,128]{1,0:T(8,128)S(1)}, f32[24,128]{1,0:T(8,128)S(1)}, u32[]{:S(2)}, u32[]{:S(2)}) collective-permute-start(f32[24,128]{1,0:T(8,128)S(1)} %get-tuple-element.71), channel_id=1, source_target_pairs={{0,2},{2,0},{4,6},{6,4},{8,10},{10,8},{12,14},{14,12},{16,18},{18,... | collective-permute-start | bytes 36872 | tf_op jit(solution)/shard_map/ppermute | solution.py:447
  126.5 0.7 collective-permute-done.23
  128.0 6.9 %all-to-all-start.3 = ((f32[16,24,128]{2,1,0:T(8,128)}), f32[16,24,128]{2,1,0:T(8,128)S(1)}, u32[]{:S(2)}, u32[]{:S(2)}) async-start(f32[16,24,128]{2,1,0:T(8,128)} %broadcast_in_dim.71), calls=%async_computation.3 | async-start | bytes 393216 | tf_op jit(solution)/shard_map/all_to_all | solution.py:449
  135.5 6.4 %all-to-all-done.3.stats_ref = f32[16,24,128]{2,1,0:T(8,128)S(1)} async-done(((f32[16,24,128]{2,1,0:T(8,128)}), f32[16,24,128]{2,1,0:T(8,128)S(1)}, u32[]{:S(2)}, u32[]{:S(2)}) %all-to-all-start.3) | async-done | bytes 196640 | tf_op jit(solution)/shard_map/all_to_all | solution.py:449
  142.7 2.8 %shard_map.85 = (bf16[160,1024]{1,0:T(8,128)(2,1)}, bf16[160,1024]{1,0:T(8,128)(2,1)}, f32[1,128]{1,0:T(1,128)}) custom-call(s32[3]{0:T(128)} %pad_add_fusion.where_ref, f32[16,24,128]{2,1,0:T(8,128)} %copy-done.22, f32[8,128]{1,0:T(8,128)} %divide_bitcast_fusion.weight_ref, f32[320,1024]{1,0:T(8,128)} %get-tuple-element.45.student_ref, ...), custom_call_target="tpu_custom_call" | custom-call | tf_op jit(solution)/shard_map/pallas_call | solution.py:165
  145.5 1.5 collective-permute-start.30
  147.2 2.4 %collective-permute-start.33 = (bf16[160,1024]{1,0:T(8,128)(2,1)}, bf16[160,1024]{1,0:T(8,128)(2,1)S(1)}, u32[]{:S(2)}, u32[]{:S(2)}) collective-permute-start(bf16[160,1024]{1,0:T(8,128)(2,1)} %get-tuple-element.47.refs_1_), channel_id=1, source_target_pairs={{0,193},{1,0},{64,1},{65,64},{128,65},{129,128},{192,129},{193,192... | collective-permute-start | bytes 983048 | tf_op jit(solution)/shard_map/ppermute | solution.py:344
  149.6 3.5 %collective-permute-done.27.refs_3_ = bf16[160,1024]{1,0:T(8,128)(2,1)S(1)} collective-permute-done((bf16[160,1024]{1,0:T(8,128)(2,1)}, bf16[160,1024]{1,0:T(8,128)(2,1)S(1)}, u32[]{:S(2)}, u32[]{:S(2)}) %collective-permute-start.27) | collective-permute-done | bytes 327712 | tf_op jit(solution)/shard_map/ppermute | solution.py:344
  153.1 1.5 collective-permute-start.28
  154.6 6.7 %collective-permute-done.24.refs_2_ = bf16[160,1024]{1,0:T(8,128)(2,1)S(1)} collective-permute-done((bf16[160,1024]{1,0:T(8,128)(2,1)}, bf16[160,1024]{1,0:T(8,128)(2,1)S(1)}, u32[]{:S(2)}, u32[]{:S(2)}) %collective-permute-start.24) | collective-permute-done | bytes 327712 | tf_op jit(solution)/shard_map/ppermute | solution.py:344
  161.3 2.7 %collective-permute-start.34 = (bf16[160,1024]{1,0:T(8,128)(2,1)S(1)}, bf16[160,1024]{1,0:T(8,128)(2,1)S(1)}, u32[]{:S(2)}, u32[]{:S(2)}) collective-permute-start(bf16[160,1024]{1,0:T(8,128)(2,1)S(1)} %collective-permute-done.33.refs_5_), channel_id=1, source_target_pairs={{0,193},{1,0},{64,1},{65,64},{128,65},{129,128},{192,129},{193,192... | collective-permute-start | bytes 983048 | tf_op jit(solution)/shard_map/ppermute | solution.py:344
  164.0 3.1 %collective-permute-done.28.refs_7_ = bf16[160,1024]{1,0:T(8,128)(2,1)S(1)} collective-permute-done((bf16[160,1024]{1,0:T(8,128)(2,1)S(1)}, bf16[160,1024]{1,0:T(8,128)(2,1)S(1)}, u32[]{:S(2)}, u32[]{:S(2)}) %collective-permute-start.28) | collective-permute-done | bytes 327712 | tf_op jit(solution)/shard_map/ppermute | solution.py:344
  167.1 1.5 collective-permute-start.29
  168.6 6.7 %collective-permute-done.25.refs_6_ = bf16[160,1024]{1,0:T(8,128)(2,1)S(1)} collective-permute-done((bf16[160,1024]{1,0:T(8,128)(2,1)S(1)}, bf16[160,1024]{1,0:T(8,128)(2,1)S(1)}, u32[]{:S(2)}, u32[]{:S(2)}) %collective-permute-start.25) | collective-permute-done | bytes 327712 | tf_op jit(solution)/shard_map/ppermute | solution.py:344
  175.4 2.7 %collective-permute-start.35 = (bf16[160,1024]{1,0:T(8,128)(2,1)S(1)}, bf16[160,1024]{1,0:T(8,128)(2,1)S(1)}, u32[]{:S(2)}, u32[]{:S(2)}) collective-permute-start(bf16[160,1024]{1,0:T(8,128)(2,1)S(1)} %collective-permute-done.34.refs_9_), channel_id=1, source_target_pairs={{0,193},{1,0},{64,1},{65,64},{128,65},{129,128},{192,129},{193,192... | collective-permute-start | bytes 983048 | tf_op jit(solution)/shard_map/ppermute | solution.py:344
  178.0 3.1 %collective-permute-done.29.refs_1_.refs_11_ = bf16[160,1024]{1,0:T(8,128)(2,1)S(1)} collective-permute-done((bf16[160,1024]{1,0:T(8,128)(2,1)S(1)}, bf16[160,1024]{1,0:T(8,128)(2,1)S(1)}, u32[]{:S(2)}, u32[]{:S(2)}) %collective-permute-start.29) | collective-permute-done | bytes 327712 | tf_op jit(solution)/shard_map/ppermute | solution.py:344
  181.6 0.8 collective-permute-done.32.refs_2_.refs_12_
  182.7 1.7 copy-done.1
  184.4 1.0 copy-done.9
  185.4 1.0 copy-done.10
  186.3 5.6 %shard_map.86.refs_7_ = f32[1024,512]{1,0:T(8,128)S(1)} custom-call(s32[3]{0:T(128)S(1)} %copy-done.8, bf16[160,1024]{1,0:T(8,128)(2,1)S(1)} %copy-done.9, bf16[160,1024]{1,0:T(8,128)(2,1)S(1)} %copy-done.10, bf16[160,1024]{1,0:T(8,128)(2,1)S(1)} %collective-permute-done.24.refs_2_, bf16[160,1024]{1,0:T(8,128)(2,1)S(1)} %collective-permute-done.27.refs_3_, ...), custom_call_target="tpu_custom_call" | custom-call | flops 2684354560 | bytes 8388608 | tf_op jit(solution)/shard_map/pallas_call | solution.py:222
  192.1 3.1 %collective-permute-done.36.refs_4_.refs_14_ = bf16[160,1024]{1,0:T(8,128)(2,1)S(1)} collective-permute-done((bf16[160,1024]{1,0:T(8,128)(2,1)S(1)}, bf16[160,1024]{1,0:T(8,128)(2,1)S(1)}, u32[]{:S(2)}, u32[]{:S(2)}) %collective-permute-start.36) | collective-permute-done | bytes 327712 | tf_op jit(solution)/shard_map/ppermute | solution.py:344
  195.2 1.2 collective-permute-done.37.refs_5_.refs_15_
  196.4 3.3 %shard_map.87 = (f32[16,32,512]{2,1,0:T(8,128)S(1)}, f32[16,32,512]{2,1,0:T(8,128)S(1)}) custom-call(s32[3]{0:T(128)S(1)} %copy-done.8, bf16[160,1024]{1,0:T(8,128)(2,1)S(1)} %collective-permute-done.26.refs_0_.refs_10_, bf16[160,1024]{1,0:T(8,128)(2,1)S(1)} %collective-permute-done.29.refs_1_.refs_11_, ...), custom_call_target="tpu_custom_call" | custom-call | flops 1207959552 | bytes 6291456 | tf_op jit(solution)/shard_map/pallas_call | solution.py:282
  199.7 2.8 %collective-permute-start.38 = (f32[16,32,512]{2,1,0:T(8,128)S(1)}, f32[16,32,512]{2,1,0:T(8,128)S(1)}, u32[]{:S(2)}, u32[]{:S(2)}) collective-permute-start(f32[16,32,512]{2,1,0:T(8,128)S(1)} %get-tuple-element.49), channel_id=1, source_target_pairs={{0,2},{2,0},{4,6},{6,4},{8,10},{10,8},{12,14},{14,12},{16,18},{18,... | collective-permute-start | bytes 3145736 | tf_op jit(solution)/shard_map/ppermute | solution.py:455
  202.6 2.3 %collective-permute-done.38 = f32[16,32,512]{2,1,0:T(8,128)S(1)} collective-permute-done((f32[16,32,512]{2,1,0:T(8,128)S(1)}, f32[16,32,512]{2,1,0:T(8,128)S(1)}, u32[]{:S(2)}, u32[]{:S(2)}) %collective-permute-start.38) | collective-permute-done | bytes 1048608 | tf_op jit(solution)/shard_map/ppermute | solution.py:455
  204.9 1.0 add_convert_fusion
  205.8 3.6 %all-to-all-start.4 = ((bf16[16,32,512]{2,1,0:T(8,128)(2,1)}), bf16[16,32,512]{2,1,0:T(8,128)(2,1)S(1)}, u32[]{:S(2)}, u32[]{:S(2)}) async-start(bf16[16,32,512]{2,1,0:T(8,128)(2,1)} %add_convert_fusion), calls=%async_computation.4 | async-start | bytes 1048576 | tf_op jit(solution)/shard_map/all_to_all | solution.py:457
  209.5 9.1 %shard_map.88 = (f32[512,2560]{1,0:T(8,128)}, bf16[128,2560]{1,0:T(8,128)(2,1)}) custom-call(s32[3]{0:T(128)} %pad_add_fusion.where_ref, bf16[160,1024]{1,0:T(8,128)(2,1)} %get-tuple-element.46.refs_0_, bf16[160,1024]{1,0:T(8,128)(2,1)} %get-tuple-element.47.refs_1_, bf16[160,1024]{1,0:T(8,128)(2,1)} %copy-done.13, bf16[160,1024]{1,0:T(8,128)(2,1)} %copy-done.11, ...), custom_call_target="tpu_custom_call" | custom-call | flops 2684354560 | bytes 12582912 | tf_op jit(solution)/shard_map/pallas_call | solution.py:320
  218.6 1.3 all-to-all-done.4
  (129 shorter events, 9.7 us)
Async XLA Ops:
  0.6 11.5 %copy-start = (bf16[512,1280]{1,0:T(8,128)(2,1)S(1)}, bf16[512,1280]{1,0:T(8,128)(2,1)}, u32[]{:S(2)}) copy-start(bf16[512,1280]{1,0:T(8,128)(2,1)} %param.7) | copy-start | bytes 3932164
  2.4 34.1 %all-to-all-start = ((bf16[8,128,128]{1,2,0:T(8,128)(2,1)}), bf16[8,128,128]{1,2,0:T(8,128)(2,1)S(1)}, u32[]{:S(2)}, u32[]{:S(2)}) async-start(bf16[8,128,128]{1,2,0:T(8,128)(2,1)} %broadcast_in_dim.65), calls=%async_computation | async-start | bytes 524288 | tf_op jit(solution)/shard_map/all_to_all | solution.py:368
  13.0 13.4 %collective-permute-start = (bf16[320,256]{1,0:T(8,128)(2,1)S(1)}, bf16[320,256]{1,0:T(8,128)(2,1)S(1)}, u32[]{:S(2)}, u32[]{:S(2)}) collective-permute-start(bf16[320,256]{1,0:T(8,128)(2,1)S(1)} %get-tuple-element.66), channel_id=1, source_target_pairs={{0,64},{64,128},{128,192},{192,0},{1,65},{65,129},{129,193},{193,1... | collective-permute-start | bytes 491528 | tf_op jit(solution)/shard_map/ppermute | solution.py:427
  15.4 18.7 %collective-permute-start.1 = (bf16[320,256]{1,0:T(8,128)(2,1)S(1)}, bf16[320,256]{1,0:T(8,128)(2,1)S(1)}, u32[]{:S(2)}, u32[]{:S(2)}) collective-permute-start(bf16[320,256]{1,0:T(8,128)(2,1)S(1)} %get-tuple-element.65), channel_id=1, source_target_pairs={{0,128},{64,192},{128,0},{192,64},{1,129},{65,193},{129,1},{193,65... | collective-permute-start | bytes 491528 | tf_op jit(solution)/shard_map/ppermute | solution.py:427
  18.7 17.8 %collective-permute-start.2 = (bf16[320,256]{1,0:T(8,128)(2,1)S(1)}, bf16[320,256]{1,0:T(8,128)(2,1)S(1)}, u32[]{:S(2)}, u32[]{:S(2)}) collective-permute-start(bf16[320,256]{1,0:T(8,128)(2,1)S(1)} %get-tuple-element.64), channel_id=1, source_target_pairs={{0,192},{64,0},{128,64},{192,128},{1,193},{65,1},{129,65},{193,129... | collective-permute-start | bytes 491528 | tf_op jit(solution)/shard_map/ppermute | solution.py:427
  36.5 20.7 %copy-start.26 = (bf16[320,256]{1,0:T(8,128)(2,1)}, bf16[320,256]{1,0:T(8,128)(2,1)S(1)}, u32[]{:S(2)}) copy-start(bf16[320,256]{1,0:T(8,128)(2,1)S(1)} %collective-permute-done.2) | copy-start | bytes 491524
  36.5 63.8 %all-to-all-start.1 = ((bf16[8,320,512]{2,1,0:T(8,128)(2,1)}), bf16[8,320,512]{2,1,0:T(8,128)(2,1)}, u32[]{:S(2)}, u32[]{:S(2)}) async-start(bf16[8,320,512]{2,1,0:T(8,128)(2,1)} %bitcast.39), calls=%async_computation.1 | async-start | bytes 5242880 | tf_op jit(solution)/shard_map/all_to_all | solution.py:437
  41.0 8.8 %collective-permute-start.3 = (bf16[64,1024]{1,0:T(8,128)(2,1)S(1)}, bf16[64,1024]{1,0:T(8,128)(2,1)S(1)}, u32[]{:S(2)}, u32[]{:S(2)}) collective-permute-start(bf16[64,1024]{1,0:T(8,128)(2,1)S(1)} %get-tuple-element.36), channel_id=1, source_target_pairs={{0,16},{2,18},{4,20},{6,22},{8,24},{10,26},{12,28},{14,30},{16,32}... | collective-permute-start | bytes 393224 | tf_op jit(solution)/shard_map/ppermute | solution.py:379
  42.2 8.6 %collective-permute-start.4 = (bf16[64,1024]{1,0:T(8,128)(2,1)S(1)}, bf16[64,1024]{1,0:T(8,128)(2,1)S(1)}, u32[]{:S(2)}, u32[]{:S(2)}) collective-permute-start(bf16[64,1024]{1,0:T(8,128)(2,1)S(1)} %get-tuple-element.36), channel_id=1, source_target_pairs={{0,32},{2,34},{4,36},{6,38},{8,40},{10,42},{12,44},{14,46},{16,48}... | collective-permute-start | bytes 393224 | tf_op jit(solution)/shard_map/ppermute | solution.py:379
  44.7 6.1 %collective-permute-start.5 = (bf16[64,1024]{1,0:T(8,128)(2,1)S(1)}, bf16[64,1024]{1,0:T(8,128)(2,1)S(1)}, u32[]{:S(2)}, u32[]{:S(2)}) collective-permute-start(bf16[64,1024]{1,0:T(8,128)(2,1)S(1)} %get-tuple-element.36), channel_id=1, source_target_pairs={{0,48},{2,50},{4,52},{6,54},{8,56},{10,58},{12,60},{14,62},{16,0},... | collective-permute-start | bytes 393224 | tf_op jit(solution)/shard_map/ppermute | solution.py:379
  45.9 5.5 %collective-permute-start.6 = (bf16[64,1024]{1,0:T(8,128)(2,1)S(1)}, bf16[64,1024]{1,0:T(8,128)(2,1)S(1)}, u32[]{:S(2)}, u32[]{:S(2)}) collective-permute-start(bf16[64,1024]{1,0:T(8,128)(2,1)S(1)} %get-tuple-element.40), channel_id=1, source_target_pairs={{0,4},{2,6},{4,8},{6,10},{8,12},{10,14},{12,0},{14,2},{16,20},{18,... | collective-permute-start | bytes 393224 | tf_op jit(solution)/shard_map/ppermute | solution.py:379
  47.1 7.8 %collective-permute-start.7 = (bf16[64,1024]{1,0:T(8,128)(2,1)S(1)}, bf16[64,1024]{1,0:T(8,128)(2,1)S(1)}, u32[]{:S(2)}, u32[]{:S(2)}) collective-permute-start(bf16[64,1024]{1,0:T(8,128)(2,1)S(1)} %get-tuple-element.40), channel_id=1, source_target_pairs={{0,8},{2,10},{4,12},{6,14},{8,0},{10,2},{12,4},{14,6},{16,24},{18,... | collective-permute-start | bytes 393224 | tf_op jit(solution)/shard_map/ppermute | solution.py:379
  49.8 5.6 %collective-permute-start.8 = (bf16[64,1024]{1,0:T(8,128)(2,1)S(1)}, bf16[64,1024]{1,0:T(8,128)(2,1)S(1)}, u32[]{:S(2)}, u32[]{:S(2)}) collective-permute-start(bf16[64,1024]{1,0:T(8,128)(2,1)S(1)} %get-tuple-element.40), channel_id=1, source_target_pairs={{0,12},{2,14},{4,0},{6,2},{8,4},{10,6},{12,8},{14,10},{16,28},{18,... | collective-permute-start | bytes 393224 | tf_op jit(solution)/shard_map/ppermute | solution.py:379
  55.5 33.0 %copy-start.20 = (bf16[256,1024]{1,0:T(8,128)(2,1)}, bf16[256,1024]{1,0:T(8,128)(2,1)S(1)}, u32[]{:S(2)}) copy-start(bf16[256,1024]{1,0:T(8,128)(2,1)S(1)} %constant_dynamic-update-slice_fusion.refs_0_) | copy-start | bytes 1572868
  55.5 5.8 %collective-permute-start.9 = (bf16[256,1024]{1,0:T(8,128)(2,1)S(1)}, bf16[256,1024]{1,0:T(8,128)(2,1)S(1)}, u32[]{:S(2)}, u32[]{:S(2)}) collective-permute-start(bf16[256,1024]{1,0:T(8,128)(2,1)S(1)} %constant_dynamic-update-slice_fusion.refs_0_), channel_id=1, source_target_pairs={{0,2},{2,0},{4,6},{6,4},{8,10},{10,8},{12,14},{14,12},{16,18},{18,... | collective-permute-start | bytes 1572872 | tf_op jit(solution)/shard_map/ppermute | solution.py:379
  57.3 43.0 %copy-start.21 = (bf16[256,1024]{1,0:T(8,128)(2,1)}, bf16[256,1024]{1,0:T(8,128)(2,1)S(1)}, u32[]{:S(2)}) copy-start(bf16[256,1024]{1,0:T(8,128)(2,1)S(1)} %constant_dynamic-update-slice_fusion.4.refs_2_) | copy-start | bytes 1572868
  57.3 4.7 %collective-permute-start.10 = (bf16[256,1024]{1,0:T(8,128)(2,1)S(1)}, bf16[256,1024]{1,0:T(8,128)(2,1)S(1)}, u32[]{:S(2)}, u32[]{:S(2)}) collective-permute-start(bf16[256,1024]{1,0:T(8,128)(2,1)S(1)} %constant_dynamic-update-slice_fusion.4.refs_2_), channel_id=1, source_target_pairs={{0,2},{2,0},{4,6},{6,4},{8,10},{10,8},{12,14},{14,12},{16,18},{18,... | collective-permute-start | bytes 1572872 | tf_op jit(solution)/shard_map/ppermute | solution.py:379
  57.4 14.5 %collective-permute-start.11 = (bf16[256,1024]{1,0:T(8,128)(2,1)S(1)}, bf16[256,1024]{1,0:T(8,128)(2,1)}, u32[]{:S(2)}, u32[]{:S(2)}) collective-permute-start(bf16[256,1024]{1,0:T(8,128)(2,1)S(1)} %constant_dynamic-update-slice_fusion.refs_0_), channel_id=1, source_target_pairs={{0,4},{2,6},{4,8},{6,10},{8,12},{10,14},{12,0},{14,2},{16,20},{18,... | collective-permute-start | bytes 1572872 | tf_op jit(solution)/shard_map/ppermute | solution.py:379
  58.3 15.2 %collective-permute-start.13 = (bf16[256,1024]{1,0:T(8,128)(2,1)S(1)}, bf16[256,1024]{1,0:T(8,128)(2,1)S(1)}, u32[]{:S(2)}, u32[]{:S(2)}) collective-permute-start(bf16[256,1024]{1,0:T(8,128)(2,1)S(1)} %constant_dynamic-update-slice_fusion.4.refs_2_), channel_id=1, source_target_pairs={{0,16},{2,18},{4,20},{6,22},{8,24},{10,26},{12,28},{14,30},{16,32}... | collective-permute-start | bytes 1572872 | tf_op jit(solution)/shard_map/ppermute | solution.py:379
  58.6 27.9 %collective-permute-start.15 = (bf16[256,1024]{1,0:T(8,128)(2,1)S(1)}, bf16[256,1024]{1,0:T(8,128)(2,1)}, u32[]{:S(2)}, u32[]{:S(2)}) collective-permute-start(bf16[256,1024]{1,0:T(8,128)(2,1)S(1)} %constant_dynamic-update-slice_fusion.refs_0_), channel_id=1, source_target_pairs={{0,8},{2,10},{4,12},{6,14},{8,0},{10,2},{12,4},{14,6},{16,24},{18,... | collective-permute-start | bytes 1572872 | tf_op jit(solution)/shard_map/ppermute | solution.py:379
  61.3 12.2 %copy-start.23 = (bf16[256,1024]{1,0:T(8,128)(2,1)}, bf16[256,1024]{1,0:T(8,128)(2,1)S(1)}, u32[]{:S(2)}) copy-start(bf16[256,1024]{1,0:T(8,128)(2,1)S(1)} %collective-permute-done.9.refs_1_) | copy-start | bytes 1572868
  61.3 25.4 %collective-permute-start.17 = (bf16[256,1024]{1,0:T(8,128)(2,1)S(1)}, bf16[256,1024]{1,0:T(8,128)(2,1)}, u32[]{:S(2)}, u32[]{:S(2)}) collective-permute-start(bf16[256,1024]{1,0:T(8,128)(2,1)S(1)} %constant_dynamic-update-slice_fusion.4.refs_2_), channel_id=1, source_target_pairs={{0,32},{2,34},{4,36},{6,38},{8,40},{10,42},{12,44},{14,46},{16,48}... | collective-permute-start | bytes 1572872 | tf_op jit(solution)/shard_map/ppermute | solution.py:379
  62.0 11.5 %copy-start.24 = (bf16[256,1024]{1,0:T(8,128)(2,1)}, bf16[256,1024]{1,0:T(8,128)(2,1)S(1)}, u32[]{:S(2)}) copy-start(bf16[256,1024]{1,0:T(8,128)(2,1)S(1)} %collective-permute-done.10.refs_3_) | copy-start | bytes 1572868
  62.0 25.2 %collective-permute-start.19 = (bf16[256,1024]{1,0:T(8,128)(2,1)S(1)}, bf16[256,1024]{1,0:T(8,128)(2,1)}, u32[]{:S(2)}, u32[]{:S(2)}) collective-permute-start(bf16[256,1024]{1,0:T(8,128)(2,1)S(1)} %constant_dynamic-update-slice_fusion.refs_0_), channel_id=1, source_target_pairs={{0,12},{2,14},{4,0},{6,2},{8,4},{10,6},{12,8},{14,10},{16,28},{18,... | collective-permute-start | bytes 1572872 | tf_op jit(solution)/shard_map/ppermute | solution.py:379
  71.9 15.4 %collective-permute-start.21 = (bf16[256,1024]{1,0:T(8,128)(2,1)S(1)}, bf16[256,1024]{1,0:T(8,128)(2,1)}, u32[]{:S(2)}, u32[]{:S(2)}) collective-permute-start(bf16[256,1024]{1,0:T(8,128)(2,1)S(1)} %constant_dynamic-update-slice_fusion.4.refs_2_), channel_id=1, source_target_pairs={{0,48},{2,50},{4,52},{6,54},{8,56},{10,58},{12,60},{14,62},{16,0},... | collective-permute-start | bytes 1572872 | tf_op jit(solution)/shard_map/ppermute | solution.py:379
  74.3 14.2 %collective-permute-start.12 = (bf16[256,1024]{1,0:T(8,128)(2,1)}, bf16[256,1024]{1,0:T(8,128)(2,1)}, u32[]{:S(2)}, u32[]{:S(2)}) collective-permute-start(bf16[256,1024]{1,0:T(8,128)(2,1)} %collective-permute-done.11.refs_4_), channel_id=1, source_target_pairs={{0,2},{2,0},{4,6},{6,4},{8,10},{10,8},{12,14},{14,12},{16,18},{18,... | collective-permute-start | bytes 1572872 | tf_op jit(solution)/shard_map/ppermute | solution.py:379
  86.6 2.3 %collective-permute-start.14 = (bf16[256,1024]{1,0:T(8,128)(2,1)}, bf16[256,1024]{1,0:T(8,128)(2,1)}, u32[]{:S(2)}, u32[]{:S(2)}) collective-permute-start(bf16[256,1024]{1,0:T(8,128)(2,1)} %copy-done.25), channel_id=1, source_target_pairs={{0,2},{2,0},{4,6},{6,4},{8,10},{10,8},{12,14},{14,12},{16,18},{18,... | collective-permute-start | bytes 1572872 | tf_op jit(solution)/shard_map/ppermute | solution.py:379
  86.7 3.0 %collective-permute-start.16 = (bf16[256,1024]{1,0:T(8,128)(2,1)}, bf16[256,1024]{1,0:T(8,128)(2,1)}, u32[]{:S(2)}, u32[]{:S(2)}) collective-permute-start(bf16[256,1024]{1,0:T(8,128)(2,1)} %collective-permute-done.15.refs_8_), channel_id=1, source_target_pairs={{0,2},{2,0},{4,6},{6,4},{8,10},{10,8},{12,14},{14,12},{16,18},{18,... | collective-permute-start | bytes 1572872 | tf_op jit(solution)/shard_map/ppermute | solution.py:379
  87.2 3.2 %collective-permute-start.18 = (bf16[256,1024]{1,0:T(8,128)(2,1)}, bf16[256,1024]{1,0:T(8,128)(2,1)}, u32[]{:S(2)}, u32[]{:S(2)}) collective-permute-start(bf16[256,1024]{1,0:T(8,128)(2,1)} %collective-permute-done.17.refs_10_), channel_id=1, source_target_pairs={{0,2},{2,0},{4,6},{6,4},{8,10},{10,8},{12,14},{14,12},{16,18},{18,... | collective-permute-start | bytes 1572872 | tf_op jit(solution)/shard_map/ppermute | solution.py:379
  87.3 3.9 %collective-permute-start.20 = (bf16[256,1024]{1,0:T(8,128)(2,1)}, bf16[256,1024]{1,0:T(8,128)(2,1)}, u32[]{:S(2)}, u32[]{:S(2)}) collective-permute-start(bf16[256,1024]{1,0:T(8,128)(2,1)} %collective-permute-done.19.refs_12_), channel_id=1, source_target_pairs={{0,2},{2,0},{4,6},{6,4},{8,10},{10,8},{12,14},{14,12},{16,18},{18,... | collective-permute-start | bytes 1572872 | tf_op jit(solution)/shard_map/ppermute | solution.py:379
  88.5 3.5 %collective-permute-start.22 = (bf16[256,1024]{1,0:T(8,128)(2,1)}, bf16[256,1024]{1,0:T(8,128)(2,1)}, u32[]{:S(2)}, u32[]{:S(2)}) collective-permute-start(bf16[256,1024]{1,0:T(8,128)(2,1)} %collective-permute-done.21.refs_14_), channel_id=1, source_target_pairs={{0,2},{2,0},{4,6},{6,4},{8,10},{10,8},{12,14},{14,12},{16,18},{18,... | collective-permute-start | bytes 1572872 | tf_op jit(solution)/shard_map/ppermute | solution.py:379
  88.6 11.7 %copy-start.19 = (bf16[4,320,256]{2,1,0:T(8,128)(2,1)}, bf16[4,320,256]{2,1,0:T(8,128)(2,1)S(1)}, u32[]{:S(2)}) copy-start(bf16[4,320,256]{2,1,0:T(8,128)(2,1)S(1)} %bitcast_dynamic-update-slice_fusion.teacher_ref) | copy-start | bytes 1966084
  88.6 28.1 %copy-start.28 = (s32[32]{0:T(128)S(1)}, s32[32]{0:T(128)}, u32[]{:S(2)}) copy-start(s32[32]{0:T(128)} %param.9) | copy-start | bytes 388
  111.5 12.6 %all-to-all-start.2 = ((f32[8,24,128]{2,1,0:T(8,128)}), f32[8,24,128]{2,1,0:T(8,128)S(1)}, u32[]{:S(2)}, u32[]{:S(2)}) async-start(f32[8,24,128]{2,1,0:T(8,128)} %get-tuple-element.44), calls=%async_computation.2 | async-start | bytes 196608 | tf_op jit(solution)/shard_map/all_to_all | solution.py:446
  124.2 3.1 %collective-permute-start.23 = (f32[24,128]{1,0:T(8,128)S(1)}, f32[24,128]{1,0:T(8,128)S(1)}, u32[]{:S(2)}, u32[]{:S(2)}) collective-permute-start(f32[24,128]{1,0:T(8,128)S(1)} %get-tuple-element.71), channel_id=1, source_target_pairs={{0,2},{2,0},{4,6},{6,4},{8,10},{10,8},{12,14},{14,12},{16,18},{18,... | collective-permute-start | bytes 36872 | tf_op jit(solution)/shard_map/ppermute | solution.py:447
  128.0 54.6 %copy-start.8 = (s32[3]{0:T(128)S(1)}, s32[3]{0:T(128)}, u32[]{:S(2)}) copy-start(s32[3]{0:T(128)} %pad_add_fusion.where_ref) | copy-start | bytes 40
  128.0 13.9 %all-to-all-start.3 = ((f32[16,24,128]{2,1,0:T(8,128)}), f32[16,24,128]{2,1,0:T(8,128)S(1)}, u32[]{:S(2)}, u32[]{:S(2)}) async-start(f32[16,24,128]{2,1,0:T(8,128)} %broadcast_in_dim.71), calls=%async_computation.3 | async-start | bytes 393216 | tf_op jit(solution)/shard_map/all_to_all | solution.py:449
  145.5 7.6 %collective-permute-start.27 = (bf16[160,1024]{1,0:T(8,128)(2,1)}, bf16[160,1024]{1,0:T(8,128)(2,1)S(1)}, u32[]{:S(2)}, u32[]{:S(2)}) collective-permute-start(bf16[160,1024]{1,0:T(8,128)(2,1)} %get-tuple-element.46.refs_0_), channel_id=1, source_target_pairs={{0,193},{1,0},{64,1},{65,64},{128,65},{129,128},{192,129},{193,192... | collective-permute-start | bytes 983048 | tf_op jit(solution)/shard_map/ppermute | solution.py:344
  145.5 9.1 %collective-permute-start.30 = (bf16[160,1024]{1,0:T(8,128)(2,1)}, bf16[160,1024]{1,0:T(8,128)(2,1)S(1)}, u32[]{:S(2)}, u32[]{:S(2)}) collective-permute-start(bf16[160,1024]{1,0:T(8,128)(2,1)} %get-tuple-element.47.refs_1_), channel_id=1, source_target_pairs={{0,1},{1,64},{64,65},{65,128},{128,129},{129,192},{192,193},{193,0... | collective-permute-start | bytes 983048 | tf_op jit(solution)/shard_map/ppermute | solution.py:344
  146.9 14.4 %collective-permute-start.24 = (bf16[160,1024]{1,0:T(8,128)(2,1)}, bf16[160,1024]{1,0:T(8,128)(2,1)S(1)}, u32[]{:S(2)}, u32[]{:S(2)}) collective-permute-start(bf16[160,1024]{1,0:T(8,128)(2,1)} %get-tuple-element.46.refs_0_), channel_id=1, source_target_pairs={{0,1},{1,64},{64,65},{65,128},{128,129},{129,192},{192,193},{193,0... | collective-permute-start | bytes 983048 | tf_op jit(solution)/shard_map/ppermute | solution.py:344
  147.2 14.1 %collective-permute-start.33 = (bf16[160,1024]{1,0:T(8,128)(2,1)}, bf16[160,1024]{1,0:T(8,128)(2,1)S(1)}, u32[]{:S(2)}, u32[]{:S(2)}) collective-permute-start(bf16[160,1024]{1,0:T(8,128)(2,1)} %get-tuple-element.47.refs_1_), channel_id=1, source_target_pairs={{0,193},{1,0},{64,1},{65,64},{128,65},{129,128},{192,129},{193,192... | collective-permute-start | bytes 983048 | tf_op jit(solution)/shard_map/ppermute | solution.py:344
  153.1 38.9 %copy-start.11 = (bf16[160,1024]{1,0:T(8,128)(2,1)}, bf16[160,1024]{1,0:T(8,128)(2,1)S(1)}, u32[]{:S(2)}) copy-start(bf16[160,1024]{1,0:T(8,128)(2,1)S(1)} %collective-permute-done.27.refs_3_) | copy-start | bytes 983044
  153.1 14.0 %collective-permute-start.28 = (bf16[160,1024]{1,0:T(8,128)(2,1)S(1)}, bf16[160,1024]{1,0:T(8,128)(2,1)S(1)}, u32[]{:S(2)}, u32[]{:S(2)}) collective-permute-start(bf16[160,1024]{1,0:T(8,128)(2,1)S(1)} %collective-permute-done.27.refs_3_), channel_id=1, source_target_pairs={{0,193},{1,0},{64,1},{65,64},{128,65},{129,128},{192,129},{193,192... | collective-permute-start | bytes 983048 | tf_op jit(solution)/shard_map/ppermute | solution.py:344
  154.6 37.4 %copy-start.12 = (bf16[160,1024]{1,0:T(8,128)(2,1)}, bf16[160,1024]{1,0:T(8,128)(2,1)S(1)}, u32[]{:S(2)}) copy-start(bf16[160,1024]{1,0:T(8,128)(2,1)S(1)} %collective-permute-done.30.refs_4_) | copy-start | bytes 983044
  154.6 14.0 %collective-permute-start.31 = (bf16[160,1024]{1,0:T(8,128)(2,1)S(1)}, bf16[160,1024]{1,0:T(8,128)(2,1)S(1)}, u32[]{:S(2)}, u32[]{:S(2)}) collective-permute-start(bf16[160,1024]{1,0:T(8,128)(2,1)S(1)} %collective-permute-done.30.refs_4_), channel_id=1, source_target_pairs={{0,1},{1,64},{64,65},{65,128},{128,129},{129,192},{192,193},{193,0... | collective-permute-start | bytes 983048 | tf_op jit(solution)/shard_map/ppermute | solution.py:344
  161.3 30.7 %copy-start.13 = (bf16[160,1024]{1,0:T(8,128)(2,1)}, bf16[160,1024]{1,0:T(8,128)(2,1)S(1)}, u32[]{:S(2)}) copy-start(bf16[160,1024]{1,0:T(8,128)(2,1)S(1)} %collective-permute-done.24.refs_2_) | copy-start | bytes 983044
  161.3 14.0 %collective-permute-start.25 = (bf16[160,1024]{1,0:T(8,128)(2,1)S(1)}, bf16[160,1024]{1,0:T(8,128)(2,1)S(1)}, u32[]{:S(2)}, u32[]{:S(2)}) collective-permute-start(bf16[160,1024]{1,0:T(8,128)(2,1)S(1)} %collective-permute-done.24.refs_2_), channel_id=1, source_target_pairs={{0,1},{1,64},{64,65},{65,128},{128,129},{129,192},{192,193},{193,0... | collective-permute-start | bytes 983048 | tf_op jit(solution)/shard_map/ppermute | solution.py:344
  161.3 30.7 %copy-start.14 = (bf16[160,1024]{1,0:T(8,128)(2,1)}, bf16[160,1024]{1,0:T(8,128)(2,1)S(1)}, u32[]{:S(2)}) copy-start(bf16[160,1024]{1,0:T(8,128)(2,1)S(1)} %collective-permute-done.33.refs_5_) | copy-start | bytes 983044
  161.3 14.0 %collective-permute-start.34 = (bf16[160,1024]{1,0:T(8,128)(2,1)S(1)}, bf16[160,1024]{1,0:T(8,128)(2,1)S(1)}, u32[]{:S(2)}, u32[]{:S(2)}) collective-permute-start(bf16[160,1024]{1,0:T(8,128)(2,1)S(1)} %collective-permute-done.33.refs_5_), channel_id=1, source_target_pairs={{0,193},{1,0},{64,1},{65,64},{128,65},{129,128},{192,129},{193,192... | collective-permute-start | bytes 983048 | tf_op jit(solution)/shard_map/ppermute | solution.py:344
  167.1 24.9 %copy-start.15 = (bf16[160,1024]{1,0:T(8,128)(2,1)}, bf16[160,1024]{1,0:T(8,128)(2,1)S(1)}, u32[]{:S(2)}) copy-start(bf16[160,1024]{1,0:T(8,128)(2,1)S(1)} %collective-permute-done.28.refs_7_) | copy-start | bytes 983044
  167.1 14.0 %collective-permute-start.29 = (bf16[160,1024]{1,0:T(8,128)(2,1)S(1)}, bf16[160,1024]{1,0:T(8,128)(2,1)S(1)}, u32[]{:S(2)}, u32[]{:S(2)}) collective-permute-start(bf16[160,1024]{1,0:T(8,128)(2,1)S(1)} %collective-permute-done.28.refs_7_), channel_id=1, source_target_pairs={{0,193},{1,0},{64,1},{65,64},{128,65},{129,128},{192,129},{193,192... | collective-permute-start | bytes 983048 | tf_op jit(solution)/shard_map/ppermute | solution.py:344
  168.6 23.4 %copy-start.16 = (bf16[160,1024]{1,0:T(8,128)(2,1)}, bf16[160,1024]{1,0:T(8,128)(2,1)S(1)}, u32[]{:S(2)}) copy-start(bf16[160,1024]{1,0:T(8,128)(2,1)S(1)} %collective-permute-done.31.refs_8_) | copy-start | bytes 983044
  168.6 13.8 %collective-permute-start.32 = (bf16[160,1024]{1,0:T(8,128)(2,1)S(1)}, bf16[160,1024]{1,0:T(8,128)(2,1)S(1)}, u32[]{:S(2)}, u32[]{:S(2)}) collective-permute-start(bf16[160,1024]{1,0:T(8,128)(2,1)S(1)} %collective-permute-done.31.refs_8_), channel_id=1, source_target_pairs={{0,1},{1,64},{64,65},{65,128},{128,129},{129,192},{192,193},{193,0... | collective-permute-start | bytes 983048 | tf_op jit(solution)/shard_map/ppermute | solution.py:344
  175.3 16.7 %copy-start.17 = (bf16[160,1024]{1,0:T(8,128)(2,1)}, bf16[160,1024]{1,0:T(8,128)(2,1)S(1)}, u32[]{:S(2)}) copy-start(bf16[160,1024]{1,0:T(8,128)(2,1)S(1)} %collective-permute-done.25.refs_6_) | copy-start | bytes 983044
  175.3 16.7 %collective-permute-start.26 = (bf16[160,1024]{1,0:T(8,128)(2,1)S(1)}, bf16[160,1024]{1,0:T(8,128)(2,1)S(1)}, u32[]{:S(2)}, u32[]{:S(2)}) collective-permute-start(bf16[160,1024]{1,0:T(8,128)(2,1)S(1)} %collective-permute-done.25.refs_6_), channel_id=1, source_target_pairs={{0,1},{1,64},{64,65},{65,128},{128,129},{129,192},{192,193},{193,0... | collective-permute-start | bytes 983048 | tf_op jit(solution)/shard_map/ppermute | solution.py:344
  175.4 16.7 %copy-start.18 = (bf16[160,1024]{1,0:T(8,128)(2,1)}, bf16[160,1024]{1,0:T(8,128)(2,1)S(1)}, u32[]{:S(2)}) copy-start(bf16[160,1024]{1,0:T(8,128)(2,1)S(1)} %collective-permute-done.34.refs_9_) | copy-start | bytes 983044
  175.4 16.7 %collective-permute-start.35 = (bf16[160,1024]{1,0:T(8,128)(2,1)S(1)}, bf16[160,1024]{1,0:T(8,128)(2,1)S(1)}, u32[]{:S(2)}, u32[]{:S(2)}) collective-permute-start(bf16[160,1024]{1,0:T(8,128)(2,1)S(1)} %collective-permute-done.34.refs_9_), channel_id=1, source_target_pairs={{0,193},{1,0},{64,1},{65,64},{128,65},{129,128},{192,129},{193,192... | collective-permute-start | bytes 983048 | tf_op jit(solution)/shard_map/ppermute | solution.py:344
  181.2 15.2 %copy-start.2 = (bf16[160,1024]{1,0:T(8,128)(2,1)}, bf16[160,1024]{1,0:T(8,128)(2,1)S(1)}, u32[]{:S(2)}) copy-start(bf16[160,1024]{1,0:T(8,128)(2,1)S(1)} %collective-permute-done.29.refs_1_.refs_11_) | copy-start | bytes 983044
  181.2 14.0 %collective-permute-start.36 = (bf16[160,1024]{1,0:T(8,128)(2,1)S(1)}, bf16[160,1024]{1,0:T(8,128)(2,1)S(1)}, u32[]{:S(2)}, u32[]{:S(2)}) collective-permute-start(bf16[160,1024]{1,0:T(8,128)(2,1)S(1)} %collective-permute-done.29.refs_1_.refs_11_), channel_id=1, source_target_pairs={{0,193},{1,0},{64,1},{65,64},{128,65},{129,128},{192,129},{193,192... | collective-permute-start | bytes 983048 | tf_op jit(solution)/shard_map/ppermute | solution.py:344
  182.4 14.0 %copy-start.3 = (bf16[160,1024]{1,0:T(8,128)(2,1)}, bf16[160,1024]{1,0:T(8,128)(2,1)S(1)}, u32[]{:S(2)}) copy-start(bf16[160,1024]{1,0:T(8,128)(2,1)S(1)} %collective-permute-done.32.refs_2_.refs_12_) | copy-start | bytes 983044
  182.4 14.0 %collective-permute-start.37 = (bf16[160,1024]{1,0:T(8,128)(2,1)S(1)}, bf16[160,1024]{1,0:T(8,128)(2,1)S(1)}, u32[]{:S(2)}, u32[]{:S(2)}) collective-permute-start(bf16[160,1024]{1,0:T(8,128)(2,1)S(1)} %collective-permute-done.32.refs_2_.refs_12_), channel_id=1, source_target_pairs={{0,1},{1,64},{64,65},{65,128},{128,129},{129,192},{192,193},{193,0... | collective-permute-start | bytes 983048 | tf_op jit(solution)/shard_map/ppermute | solution.py:344
  192.1 7.6 %copy-start.4 = (bf16[160,1024]{1,0:T(8,128)(2,1)}, bf16[160,1024]{1,0:T(8,128)(2,1)S(1)}, u32[]{:S(2)}) copy-start(bf16[160,1024]{1,0:T(8,128)(2,1)S(1)} %collective-permute-done.26.refs_0_.refs_10_) | copy-start | bytes 983044
  199.7 5.1 %collective-permute-start.38 = (f32[16,32,512]{2,1,0:T(8,128)S(1)}, f32[16,32,512]{2,1,0:T(8,128)S(1)}, u32[]{:S(2)}, u32[]{:S(2)}) collective-permute-start(f32[16,32,512]{2,1,0:T(8,128)S(1)} %get-tuple-element.49), channel_id=1, source_target_pairs={{0,2},{2,0},{4,6},{6,4},{8,10},{10,8},{12,14},{14,12},{16,18},{18,... | collective-permute-start | bytes 3145736 | tf_op jit(solution)/shard_map/ppermute | solution.py:455
  205.8 14.0 %all-to-all-start.4 = ((bf16[16,32,512]{2,1,0:T(8,128)(2,1)}), bf16[16,32,512]{2,1,0:T(8,128)(2,1)S(1)}, u32[]{:S(2)}, u32[]{:S(2)}) async-start(bf16[16,32,512]{2,1,0:T(8,128)(2,1)} %add_convert_fusion), calls=%async_computation.4 | async-start | bytes 1048576 | tf_op jit(solution)/shard_map/all_to_all | solution.py:457
  (9 other events, 23.2 us)

commit v4 on v3

--- a/solution.py
+++ b/solution.py
@@ -50,50 +50,89 @@
     return student_lse[0], teacher_lse[0], cross
 
 
+def stack_kernel(where_ref, *refs):
+    parts, out_ref = refs[:-1], refs[-1]
+    toks = len(parts)
+    for shift, part in enumerate(parts):
+        out_ref[lax.rem(where_ref[3] + toks - shift, toks)] = part[...]
+
+
+def stack_teachers(where, parts):
+    return pl.pallas_call(
+        stack_kernel,
+        in_specs=[SMEM] + [VMEM] * len(parts),
+        out_specs=VMEM,
+        out_shape=jax.ShapeDtypeStruct((len(parts),) + parts[0].shape, BF16),
+        compiler_params=params(24),
+        cost_estimate=pl.CostEstimate(
+            flops=40_000_000_000, bytes_accessed=2 * MIB, transcendentals=0
+        ),
+    )(where, *parts)
+
+
 def place_columns(voc, side, array_refs, origins, out_ref, sem):
     core, chip = lax.rem(voc, 2), voc // 2
     x, y = chip // side, lax.rem(chip, side)
     copies = []
-    for array_ref, (steps, other, which) in zip(array_refs, origins):
-        half = array_ref.shape[0] // len(steps)
+    for number, (array_ref, (steps, other, which)) in enumerate(zip(array_refs, origins)):
+        height, width = array_ref.shape[0] // len(steps), array_ref.shape[1]
         for index, (back_x, back_y) in enumerate(steps):
             from_x = lax.rem(x + side - back_x, side)
             from_y = lax.rem(y + side - back_y, side)
             from_core = 1 - core if other else core
-            start = ((from_x * side + from_y) * 2 + from_core) * (2 * half) + which * half
+            start = ((from_x * side + from_y) * 2 + from_core) * height
             copy = pltpu.make_async_copy(
-                array_ref.at[index * half : (index + 1) * half],
-                out_ref.at[pl.ds(pl.multiple_of(start, half), half)],
-                sem.at[len(copies)],
+                array_ref.at[index * height : (index + 1) * height],
+                out_ref.at[pl.ds(pl.multiple_of(start, height), height), which * width : (which + 1) * width],
+                sem.at[index, number],
             )
             copy.start()
-            copies.append(copy)
+            copies.append((which, copy))
     return copies
 
 
-def student_kernel(order, side, origins, where_ref, head_ref, teacher_ref, *refs):
-    arrays, rest = refs[: len(origins)], refs[len(origins) :]
-    student_ref, stats_ref, own_ref, features, sem = rest
-    depth = head_ref.shape[2]
-    for copy in place_columns(where_ref[2], side, arrays, origins, features, sem):
+def assemble_kernel(side, origins, where_ref, *refs):
+    arrays, (out_ref, own_ref, sem) = refs[: len(origins)], refs[len(origins) :]
+    for _, copy in place_columns(where_ref[2], side, arrays, origins, out_ref, sem):
         copy.wait()
-    mine = pl.multiple_of(where_ref[0] * depth, depth)
-    own_ref[...] = features[pl.ds(mine, depth), :]
+    depth = own_ref.shape[0]
+    own_ref[...] = out_ref[pl.ds(pl.multiple_of(where_ref[0] * depth, depth), depth), :]
+
+
+def assemble(where, arrays, origins, side, depth):
+    height = len(origins[0][0]) * len(arrays) // 2 * (arrays[0].shape[0] // len(origins[0][0]))
+    rows = 2 * arrays[0].shape[1]
+    return pl.pallas_call(
+        functools.partial(assemble_kernel, side, origins),
+        in_specs=[SMEM] + [HBM] * len(arrays),
+        out_specs=[VMEM] * 2,
+        out_shape=[
+            jax.ShapeDtypeStruct((height, rows), BF16),
+            jax.ShapeDtypeStruct((depth, rows), BF16),
+        ],
+        scratch_shapes=[pltpu.SemaphoreType.DMA((len(origins[0][0]), len(arrays)))],
+        compiler_params=params(40),
+        cost_estimate=pl.CostEstimate(flops=0, bytes_accessed=0, transcendentals=0),
+    )(where, *arrays)
+
+
+def student_kernel(order, head_hbm, features_ref, teacher_ref, student_ref, stats_ref, head_ref, sem):
+    depth = head_hbm.shape[2]
+    head_copies = [
+        pltpu.make_async_copy(
+            head_hbm.at[index], head_ref.at[:, block * depth : (block + 1) * depth], sem.at[index]
+        )
+        for index, block in enumerate(order)
+    ]
+    for copy in head_copies:
+        copy.start()
+    for copy in head_copies:
+        copy.wait()
+    student_ref[...] = jnp.dot(head_ref[...], features_ref[...], preferred_element_type=F32)
     copies, height, lanes = stats_ref.shape
     toks, _, width = teacher_ref.shape
-
-    @pl.loop(0, toks)
-    def _(i):
-        cols = pl.ds(pl.multiple_of(i * width, width), width)
-        student = None
-        for index, block in enumerate(order):
-            part = jnp.dot(
-                head_ref[index],
-                features[block * depth : (block + 1) * depth, cols],
-                preferred_element_type=F32,
-            )
-            student = part if student is None else student + part
-        student_ref[:, cols] = student
+    for i in range(toks):
+        student = student_ref[:, i * width : (i + 1) * width]
         teacher = teacher_ref[i].astype(F32)
         student_lse, teacher_lse = log_sum_exp(student), log_sum_exp(teacher)
         cross = jnp.sum(
@@ -104,32 +143,30 @@
             for piece in range(pieces):
                 place = index * (height // 3) + i * pieces + piece
                 values = row[:, piece * lanes : (piece + 1) * lanes]
-                stats_ref[:, pl.ds(place, 1), :] = jnp.broadcast_to(
+                stats_ref[:, place : place + 1, :] = jnp.broadcast_to(
                     values[None], (copies, 1, lanes)
                 )
 
 
-def student_logits(where, head, teachers, arrays, origins, side, subs):
+def student_logits(head, features, teachers, subs):
     blocks, v, d = head.shape
-    toks, _, width = teachers.shape
-    r = toks * width
+    toks = teachers.shape[0]
+    r = features.shape[1]
     order = [i % toks * subs + i // toks for i in range(blocks)]
-    count = sum(len(steps) for steps, _, _ in origins)
-    return pl.pallas_call(
-        functools.partial(student_kernel, order, side, origins),
-        in_specs=[SMEM] + [VMEM] * 2 + [HBM] * len(arrays),
-        out_specs=[VMEM] * 3,
+    return pl.pallas_call(
+        functools.partial(student_kernel, order),
+        in_specs=[HBM, VMEM, VMEM],
+        out_specs=[VMEM] * 2,
         out_shape=[
             jax.ShapeDtypeStruct((v, r), F32),
-            jax.ShapeDtypeStruct((blocks, 3 * r // 128, 128), F32),
-            jax.ShapeDtypeStruct((d, r), BF16),
-        ],
-        scratch_shapes=[pltpu.VMEM((blocks * d, r), BF16), pltpu.SemaphoreType.DMA((count,))],
-        compiler_params=params(58),
+            jax.ShapeDtypeStruct((2 * blocks, 3 * r // 128, 128), F32),
+        ],
+        scratch_shapes=[pltpu.VMEM((v, blocks * d), BF16), pltpu.SemaphoreType.DMA((blocks,))],
+        compiler_params=params(20),
         cost_estimate=pl.CostEstimate(
             flops=2 * r * v * d * blocks, bytes_accessed=12 * MIB, transcendentals=0
         ),
-    )(where, head, teachers, *arrays)
+    )(head, features, teachers)
 
 
 def merge(stats):
@@ -171,7 +208,7 @@
             jax.ShapeDtypeStruct((v // 2, r), BF16),
             jax.ShapeDtypeStruct((1, 128), F32),
         ],
-        compiler_params=params(58),
+        compiler_params=params(20),
     )(where, stats, weights, student, teachers)
 
 
@@ -378,8 +415,8 @@
                     pairs.append(((i * chips_y + j) * 2 + c, target))
         return lax.ppermute(values, "voc", pairs)
 
-    half = column.shape[0] // 2
-    first, second = column[:half], column[half:]
+    half = column.shape[1] // 2
+    first, second = column[:, :half], column[:, half:]
     along_x = [first] + [shift(first, k, 0, 0) for k in range(1, chips_x)]
     along_y = [second] + [shift(second, 0, k, 0) for k in range(1, chips_y)]
     along_x, along_y = lax.optimization_barrier((along_x, along_y))
@@ -390,9 +427,10 @@
             arrays.append((shift(first, 0, k, 0), [(i, k) for i in range(chips_x)], 0))
         if k < chips_x:
             arrays.append((shift(second, k, 0, 0), [(k, i) for i in range(chips_y)], 1))
+    values = lax.optimization_barrier([array for array, _, _ in arrays])
     out, origins = [], []
-    for values, steps, which in arrays:
-        out += [values, shift(values, 0, 0, 1)]
+    for (_, steps, which), value in zip(arrays, values):
+        out += [value, shift(value, 0, 0, 1)]
         origins += [(steps, 0, which), (steps, 1, which)]
     return out, origins
 
@@ -409,7 +447,7 @@
     tok = lax.axis_index("tok")
     place = lax.axis_index(RING)
     voc = lax.axis_index("voc")
-    where = jnp.stack([place, voc % 2, voc])
+    where = jnp.stack([place, voc % 2, voc, tok])
     cores = [(i, i ^ 1) for i in range(vocs)]
     groups = [[2 * i + c for i in range(chips)] for c in range(2)]
 
@@ -431,20 +469,20 @@
     own = lax.dynamic_slice_in_dim(hidden, voc * piece, piece, 1)
     column = to_all(own, RING)
     slices = head.T.reshape(ring, cut, depth)
-    slices, column, *parts = lax.optimization_barrier((slices, column, *parts))
+    teachers = stack_teachers(where, parts)
+    slices, column, teachers = lax.optimization_barrier((slices, column, teachers))
     side = math.isqrt(chips)
     arrays, origins = spread(column.reshape(rows, piece).T, side, side)
+    features, own_features = assemble(where, arrays, origins, side, depth)
     head_cut = lax.all_to_all(slices, ("sub", "tok"), 0, 0)
-    teachers = jnp.zeros((toks, cut, kept), BF16)
-    for shift, part in enumerate(parts):
-        teachers = lax.dynamic_update_index_in_dim(teachers, part, (tok + toks - shift) % toks, 0)
     weights = row_weights(sizes, rows).reshape(rows // 128, 128)
 
-    student, stats, features = student_logits(
-        where, head_cut, teachers, arrays, origins, side, subs
-    )
-    stats = merge(lax.all_to_all(stats, RING, 0, 0))
-    stats = merge(jnp.stack([stats, lax.ppermute(stats, "voc", cores)]))
+    student, stats = student_logits(head_cut, features, teachers, subs)
+    mixed = [
+        [(t * vocs + 2 * i + c) * subs + u for t in range(toks) for c in range(2) for u in range(subs)]
+        for i in range(chips)
+    ]
+    stats = merge(lax.all_to_all(stats, ("tok", "voc", "sub"), 0, 0, axis_index_groups=mixed))
     stats = jnp.broadcast_to(stats[None], (chips,) + stats.shape)
     stats = lax.all_to_all(stats, "voc", 0, 0, axis_index_groups=groups)
     low, high, divergence = logit_grads(where, stats, weights, student, teachers)
@@ -457,7 +495,7 @@
     sums = lax.all_to_all(sums, "voc", 0, 0, axis_index_groups=groups)
     feature_grad = jnp.sum(sums.astype(F32), axis=0)
 
-    head_grad, local_grad = head_parts(where, blocks, hops, features, vocab, share)
+    head_grad, local_grad = head_parts(where, blocks, hops, own_features, vocab, share)
     return head_grad, feature_grad, local_grad, divergence.reshape(share)
 
 

time: 221 us -> 217 us (0.982)
    ppermute x20, waiting for transfers between devices: 18.4 us -> 28.8 us  [shift(): return lax.ppermute(values, 'voc', pairs)]
    all_to_all x1, waiting for transfers between devices: 8.34 us -> 0.01 us  [on_device(): head_cut = lax.all_to_all(slices, ('sub', 'tok'), 0, 0)]
    ppermute x14, starting transfers between devices: 13.1 us -> 19.9 us  [ring_shift(): lax.ppermute(values, RING, [(i, (i + step) % size) for i in range(size)])]
    all_to_all x1, starting transfers between devices: 9.01 us -> 3.41 us  [to_all(): lax.all_to_all(jnp.broadcast_to(values[None], (size,) + values.shape), ax...]
    ppermute x3, waiting for transfers between devices: 10.1 us -> 5.11 us  [on_device(): lax.ppermute(part, 'tok', [(i, (i + shift) % toks) for i in range(toks)])]
    all_to_all x1, starting transfers between devices: 6.88 us -> 3.52 us  [on_device(): stats = lax.all_to_all(stats, 'voc', 0, 0, axis_index_groups=groups)]
    ppermute x14, waiting for transfers between devices: 28.3 us -> 25.2 us  [ring_shift(): lax.ppermute(values, RING, [(i, (i + step) % size) for i in range(size)])]
    all_to_all x1, waiting for transfers between devices: 0.01 us -> 2.82 us  [to_all(): lax.all_to_all(jnp.broadcast_to(values[None], (size,) + values.shape), ax...]
  transfers between devices with their start and end apart: 44 -> 43, of which waited for: 26 -> 29; matrix products, arithmetic and copies ran while one was open for 3% -> 3% of each run, Pallas kernels for 7% -> 10%
where the time goes in v4:
time: 217 us; the launch traced here: 216 us
  starting transfers between devices  85.7 us (39%)
  waiting for transfers between devices  81.1 us (37%)
  Pallas kernels  31.1 us (14%)
  local copies, waits for them, and re-layouts  13.9 us (6%)
  other arithmetic  2.81 us (1%)
    ppermute x20, waiting for transfers between devices, shift(): return lax.ppermute(values, 'voc', pairs)  28.8 us
    ppermute x20, starting transfers between devices, shift(): return lax.ppermute(values, 'voc', pairs)  28.2 us
    ppermute x14, waiting for transfers between devices, ring_shift(): lax.ppermute(values, RING, [(i, (i + step) % size) for i in range(size)])  25.2 us
    ppermute x14, starting transfers between devices, ring_shift(): lax.ppermute(values, RING, [(i, (i + step) % size) for i in range(size)])  19.9 us
    ppermute x3, starting transfers between devices, on_device(): lax.ppermute(part, 'tok', [(i, (i + shift) % toks) for i in range(toks)])  11.4 us
    pallas_call x1, Pallas kernels, head_parts(): pl.pallas_call(functools.partial(head_kernel, hops), grid=(vocab // tile,...  9.08 us
    all_to_all x1, waiting for transfers between devices, on_device(): lax.all_to_all(stats, ('tok', 'voc', 'sub'), 0, 0, axis_index_groups=mixed)  8.65 us
    all_to_all x1, starting transfers between devices, on_device(): lax.all_to_all(stats, ('tok', 'voc', 'sub'), 0, 0, axis_index_groups=mixed)  7.32 us
  transfers between devices with their start and end apart: 43, of which 29 were waited for; matrix products, arithmetic and copies ran while one was open for 3% of the time, Pallas kernels for 10%

profile of v4, /device:TPU:1, one launch (start us, length us, event | category | flops | bytes accessed | tf_op | source)
XLA Modules:
  0.0 216.3 jit_solution(3571277414490010785)
XLA Ops:
  0.7 0.8 broadcast_subtract_fusion
  2.9 3.9 %collective-permute-start = (bf16[320,256]{1,0:T(8,128)(2,1)S(1)}, bf16[320,256]{1,0:T(8,128)(2,1)S(1)}, u32[]{:S(2)}, u32[]{:S(2)}) collective-permute-start(bf16[320,256]{1,0:T(8,128)(2,1)S(1)} %get-tuple-element.74), channel_id=1, source_target_pairs={{0,64},{64,128},{128,192},{192,0},{1,65},{65,129},{129,193},{193,1... | collective-permute-start | bytes 491528 | tf_op jit(solution)/shard_map/ppermute | solution.py:465
  6.7 5.1 %collective-permute-start.1 = (bf16[320,256]{1,0:T(8,128)(2,1)S(1)}, bf16[320,256]{1,0:T(8,128)(2,1)S(1)}, u32[]{:S(2)}, u32[]{:S(2)}) collective-permute-start(bf16[320,256]{1,0:T(8,128)(2,1)S(1)} %get-tuple-element.73), channel_id=1, source_target_pairs={{0,128},{64,192},{128,0},{192,64},{1,129},{65,193},{129,1},{193,65... | collective-permute-start | bytes 491528 | tf_op jit(solution)/shard_map/ppermute | solution.py:465
  11.9 2.4 %collective-permute-start.2 = (bf16[320,256]{1,0:T(8,128)(2,1)S(1)}, bf16[320,256]{1,0:T(8,128)(2,1)S(1)}, u32[]{:S(2)}, u32[]{:S(2)}) collective-permute-start(bf16[320,256]{1,0:T(8,128)(2,1)S(1)} %get-tuple-element.72), channel_id=1, source_target_pairs={{0,192},{64,0},{128,64},{192,128},{1,193},{65,1},{129,65},{193,129... | collective-permute-start | bytes 491528 | tf_op jit(solution)/shard_map/ppermute | solution.py:465
  14.2 0.8 constant_dynamic-slice_fusion
  15.9 3.4 %all-to-all-start = ((bf16[8,128,128]{1,2,0:T(8,128)(2,1)}), bf16[8,128,128]{1,2,0:T(8,128)(2,1)S(1)}, u32[]{:S(2)}, u32[]{:S(2)}) async-start(bf16[8,128,128]{1,2,0:T(8,128)(2,1)} %broadcast_in_dim.28), calls=%async_computation | async-start | bytes 524288 | tf_op jit(solution)/shard_map/all_to_all | solution.py:405
  19.3 4.4 %copy.22 = bf16[2560,512]{1,0:T(8,128)(2,1)} copy(bf16[2560,512]{0,1:T(8,128)(2,1)} %bitcast.28) | data formatting | bytes 5242880 | tf_op jit(solution)/shard_map/transpose | solution.py:471
  23.8 5.1 %collective-permute-done.2.refs_3_ = bf16[320,256]{1,0:T(8,128)(2,1)S(1)} collective-permute-done((bf16[320,256]{1,0:T(8,128)(2,1)S(1)}, bf16[320,256]{1,0:T(8,128)(2,1)S(1)}, u32[]{:S(2)}, u32[]{:S(2)}) %collective-permute-start.2) | collective-permute-done | bytes 163872 | tf_op jit(solution)/shard_map/ppermute | solution.py:465
  29.5 2.8 %all-to-all-done = bf16[8,128,128]{1,2,0:T(8,128)(2,1)S(1)} async-done(((bf16[8,128,128]{1,2,0:T(8,128)(2,1)}), bf16[8,128,128]{1,2,0:T(8,128)(2,1)S(1)}, u32[]{:S(2)}, u32[]{:S(2)}) %all-to-all-start) | async-done | bytes 262176 | tf_op jit(solution)/shard_map/all_to_all | solution.py:405
  32.3 5.1 %all-to-all-start.1 = ((bf16[8,320,512]{2,1,0:T(8,128)(2,1)}), bf16[8,320,512]{2,1,0:T(8,128)(2,1)}, u32[]{:S(2)}, u32[]{:S(2)}) async-start(bf16[8,320,512]{2,1,0:T(8,128)(2,1)} %bitcast.29), calls=%async_computation.1 | async-start | bytes 5242880 | tf_op jit(solution)/shard_map/all_to_all | solution.py:477
  37.4 1.3 collective-permute-start.3
  38.7 2.5 %collective-permute-start.4 = (bf16[128,512]{1,0:T(8,128)(2,1)S(1)}, bf16[128,512]{1,0:T(8,128)(2,1)S(1)}, u32[]{:S(2)}, u32[]{:S(2)}) collective-permute-start(bf16[128,512]{1,0:T(8,128)(2,1)S(1)} %get-tuple-element.38), channel_id=1, source_target_pairs={{0,32},{2,34},{4,36},{6,38},{8,40},{10,42},{12,44},{14,46},{16,48}... | collective-permute-start | bytes 393224 | tf_op jit(solution)/shard_map/ppermute | solution.py:416
  41.2 1.1 collective-permute-start.5
  42.3 1.3 collective-permute-start.6
  43.6 2.6 %collective-permute-start.7 = (bf16[128,512]{1,0:T(8,128)(2,1)S(1)}, bf16[128,512]{1,0:T(8,128)(2,1)S(1)}, u32[]{:S(2)}, u32[]{:S(2)}) collective-permute-start(bf16[128,512]{1,0:T(8,128)(2,1)S(1)} %get-tuple-element.42), channel_id=1, source_target_pairs={{0,8},{2,10},{4,12},{6,14},{8,0},{10,2},{12,4},{14,6},{16,24},{18,... | collective-permute-start | bytes 393224 | tf_op jit(solution)/shard_map/ppermute | solution.py:416
  46.3 1.1 collective-permute-start.8
  47.7 2.7 %collective-permute-done.7 = bf16[128,512]{1,0:T(8,128)(2,1)S(1)} collective-permute-done((bf16[128,512]{1,0:T(8,128)(2,1)S(1)}, bf16[128,512]{1,0:T(8,128)(2,1)S(1)}, u32[]{:S(2)}, u32[]{:S(2)}) %collective-permute-start.7) | collective-permute-done | bytes 131104 | tf_op jit(solution)/shard_map/ppermute | solution.py:416
  50.9 1.0 collective-permute-start.12
  51.9 1.5 collective-permute-start.14
  53.5 2.3 %collective-permute-start.11 = (bf16[512,512]{1,0:T(8,128)(2,1)S(1)}, bf16[512,512]{1,0:T(8,128)(2,1)S(1)}, u32[]{:S(2)}, u32[]{:S(2)}) collective-permute-start(bf16[512,512]{1,0:T(8,128)(2,1)S(1)} %constant_dynamic-update-slice_fusion.refs_0_), channel_id=1, source_target_pairs={{0,8},{2,10},{4,12},{6,14},{8,0},{10,2},{12,4},{14,6},{16,24},{18,... | collective-permute-start | bytes 1572872 | tf_op jit(solution)/shard_map/ppermute | solution.py:416
  55.8 1.0 collective-permute-start.13
  56.8 5.3 %collective-permute-done.10.refs_6_ = bf16[512,512]{1,0:T(8,128)(2,1)S(1)} collective-permute-done((bf16[512,512]{1,0:T(8,128)(2,1)S(1)}, bf16[512,512]{1,0:T(8,128)(2,1)S(1)}, u32[]{:S(2)}, u32[]{:S(2)}) %collective-permute-start.10) | collective-permute-done | bytes 524320 | tf_op jit(solution)/shard_map/ppermute | solution.py:416
  62.1 1.0 collective-permute-start.9
  63.1 8.2 %collective-permute-done.12.refs_10_ = bf16[512,512]{1,0:T(8,128)(2,1)S(1)} collective-permute-done((bf16[512,512]{1,0:T(8,128)(2,1)S(1)}, bf16[512,512]{1,0:T(8,128)(2,1)S(1)}, u32[]{:S(2)}, u32[]{:S(2)}) %collective-permute-start.12) | collective-permute-done | bytes 524320 | tf_op jit(solution)/shard_map/ppermute | solution.py:416
  71.3 4.8 %collective-permute-done.14.refs_14_ = bf16[512,512]{1,0:T(8,128)(2,1)S(1)} collective-permute-done((bf16[512,512]{1,0:T(8,128)(2,1)S(1)}, bf16[512,512]{1,0:T(8,128)(2,1)S(1)}, u32[]{:S(2)}, u32[]{:S(2)}) %collective-permute-start.14) | collective-permute-done | bytes 524320 | tf_op jit(solution)/shard_map/ppermute | solution.py:416
  76.2 2.7 %collective-permute-done.13.refs_12_ = bf16[512,512]{1,0:T(8,128)(2,1)S(1)} collective-permute-done((bf16[512,512]{1,0:T(8,128)(2,1)S(1)}, bf16[512,512]{1,0:T(8,128)(2,1)S(1)}, u32[]{:S(2)}, u32[]{:S(2)}) %collective-permute-start.13) | collective-permute-done | bytes 524320 | tf_op jit(solution)/shard_map/ppermute | solution.py:416
  78.8 9.0 %collective-permute-start.15 = (bf16[512,512]{1,0:T(8,128)(2,1)S(1)}, bf16[512,512]{1,0:T(8,128)(2,1)S(1)}, u32[]{:S(2)}, u32[]{:S(2)}) collective-permute-start(bf16[512,512]{1,0:T(8,128)(2,1)S(1)} %constant_dynamic-update-slice_fusion.refs_0_), channel_id=1, source_target_pairs={{0,2},{2,0},{4,6},{6,4},{8,10},{10,8},{12,14},{14,12},{16,18},{18,... | collective-permute-start | bytes 1572872 | tf_op jit(solution)/shard_map/ppermute | solution.py:416
  91.6 0.7 collective-permute-done.19.refs_9_
  92.3 0.7 collective-permute-done.20.refs_11_
  93.1 0.7 collective-permute-done.21.refs_13_
  93.8 0.7 collective-permute-done.22.refs_15_
  94.6 5.5 %shard_map.85 = (bf16[4096,1024]{1,0:T(8,128)(2,1)}, bf16[512,1024]{1,0:T(8,128)(2,1)S(1)}) custom-call(s32[4]{0:T(128)S(1)} %pad_add_fusion.where_ref, bf16[512,512]{1,0:T(8,128)(2,1)S(1)} %constant_dynamic-update-slice_fusion.refs_0_, bf16[512,512]{1,0:T(8,128)(2,1)S(1)} %collective-permute-done.15.refs_1_, ...), custom_call_target="tpu_custom_call" | custom-call | tf_op jit(solution)/shard_map/pallas_call | solution.py:105
  100.1 1.0 copy-done.10
  101.1 3.4 %copy-done.2 = bf16[4096,1024]{1,0:T(8,128)(2,1)S(1)} copy-done((bf16[4096,1024]{1,0:T(8,128)(2,1)S(1)}, bf16[4096,1024]{1,0:T(8,128)(2,1)}, u32[]{:S(2)}) %copy-start.2) | copy-done | bytes 8388632
  104.5 5.8 %shard_map.86 = (f32[320,1024]{1,0:T(8,128)S(1)}, f32[16,24,128]{2,1,0:T(8,128)}) custom-call(bf16[8,320,512]{2,1,0:T(8,128)(2,1)} %all-to-all-done.1.head_hbm, bf16[4096,1024]{1,0:T(8,128)(2,1)S(1)} %copy-done.2, bf16[4,320,256]{2,1,0:T(8,128)(2,1)S(1)} %shard_map.84.teacher_ref), custom_call_target="tpu_custom_call" | custom-call | flops 2684354560 | bytes 12582912 | tf_op jit(solution)/shard_map/pallas_call | solution.py:156
  110.3 7.3 %all-to-all-start.2 = ((f32[16,24,128]{2,1,0:T(8,128)}), f32[16,24,128]{2,1,0:T(8,128)S(1)}, u32[]{:S(2)}, u32[]{:S(2)}) async-start(f32[16,24,128]{2,1,0:T(8,128)} %get-tuple-element.56), calls=%async_computation.2 | async-start | bytes 393216 | tf_op jit(solution)/shard_map/all_to_all | solution.py:485
  117.9 8.7 %all-to-all-done.2 = f32[16,24,128]{2,1,0:T(8,128)S(1)} async-done(((f32[16,24,128]{2,1,0:T(8,128)}), f32[16,24,128]{2,1,0:T(8,128)S(1)}, u32[]{:S(2)}, u32[]{:S(2)}) %all-to-all-start.2) | async-done | bytes 196640 | tf_op jit(solution)/shard_map/all_to_all | solution.py:485
  127.3 3.5 %all-to-all-start.3 = ((f32[16,24,128]{2,1,0:T(8,128)}), f32[16,24,128]{2,1,0:T(8,128)S(1)}, u32[]{:S(2)}, u32[]{:S(2)}) async-start(f32[16,24,128]{2,1,0:T(8,128)} %broadcast_in_dim.29), calls=%async_computation.3 | async-start | bytes 393216 | tf_op jit(solution)/shard_map/all_to_all | solution.py:487
  130.9 6.9 %all-to-all-done.3.stats_ref = f32[16,24,128]{2,1,0:T(8,128)S(1)} async-done(((f32[16,24,128]{2,1,0:T(8,128)}), f32[16,24,128]{2,1,0:T(8,128)S(1)}, u32[]{:S(2)}, u32[]{:S(2)}) %all-to-all-start.3) | async-done | bytes 196640 | tf_op jit(solution)/shard_map/all_to_all | solution.py:487
  137.8 1.1 shard_map.87
  138.9 2.2 %collective-permute-start.26 = (bf16[160,1024]{1,0:T(8,128)(2,1)S(1)}, bf16[160,1024]{1,0:T(8,128)(2,1)S(1)}, u32[]{:S(2)}, u32[]{:S(2)}) collective-permute-start(bf16[160,1024]{1,0:T(8,128)(2,1)S(1)} %get-tuple-element.58.refs_0_), channel_id=1, source_target_pairs={{0,193},{1,0},{64,1},{65,64},{128,65},{129,128},{192,129},{193,192... | collective-permute-start | bytes 983048 | tf_op jit(solution)/shard_map/ppermute | solution.py:381
  141.8 2.1 collective-permute-start.32
  143.8 2.6 %collective-permute-done.26.refs_3_ = bf16[160,1024]{1,0:T(8,128)(2,1)S(1)} collective-permute-done((bf16[160,1024]{1,0:T(8,128)(2,1)S(1)}, bf16[160,1024]{1,0:T(8,128)(2,1)S(1)}, u32[]{:S(2)}, u32[]{:S(2)}) %collective-permute-start.26) | collective-permute-done | bytes 327712 | tf_op jit(solution)/shard_map/ppermute | solution.py:381
  146.4 3.4 %collective-permute-start.27 = (bf16[160,1024]{1,0:T(8,128)(2,1)S(1)}, bf16[160,1024]{1,0:T(8,128)(2,1)S(1)}, u32[]{:S(2)}, u32[]{:S(2)}) collective-permute-start(bf16[160,1024]{1,0:T(8,128)(2,1)S(1)} %collective-permute-done.26.refs_3_), channel_id=1, source_target_pairs={{0,193},{1,0},{64,1},{65,64},{128,65},{129,128},{192,129},{193,192... | collective-permute-start | bytes 983048 | tf_op jit(solution)/shard_map/ppermute | solution.py:381
  149.9 6.7 %collective-permute-done.23.refs_2_ = bf16[160,1024]{1,0:T(8,128)(2,1)S(1)} collective-permute-done((bf16[160,1024]{1,0:T(8,128)(2,1)S(1)}, bf16[160,1024]{1,0:T(8,128)(2,1)S(1)}, u32[]{:S(2)}, u32[]{:S(2)}) %collective-permute-start.23) | collective-permute-done | bytes 327712 | tf_op jit(solution)/shard_map/ppermute | solution.py:381
  156.6 2.7 %collective-permute-start.33 = (bf16[160,1024]{1,0:T(8,128)(2,1)S(1)}, bf16[160,1024]{1,0:T(8,128)(2,1)S(1)}, u32[]{:S(2)}, u32[]{:S(2)}) collective-permute-start(bf16[160,1024]{1,0:T(8,128)(2,1)S(1)} %collective-permute-done.32.refs_5_), channel_id=1, source_target_pairs={{0,193},{1,0},{64,1},{65,64},{128,65},{129,128},{192,129},{193,192... | collective-permute-start | bytes 983048 | tf_op jit(solution)/shard_map/ppermute | solution.py:381
  159.3 1.2 collective-permute-done.27.refs_7_
  160.5 3.4 %collective-permute-start.28 = (bf16[160,1024]{1,0:T(8,128)(2,1)S(1)}, bf16[160,1024]{1,0:T(8,128)(2,1)S(1)}, u32[]{:S(2)}, u32[]{:S(2)}) collective-permute-start(bf16[160,1024]{1,0:T(8,128)(2,1)S(1)} %collective-permute-done.27.refs_7_), channel_id=1, source_target_pairs={{0,193},{1,0},{64,1},{65,64},{128,65},{129,128},{192,129},{193,192... | collective-permute-start | bytes 983048 | tf_op jit(solution)/shard_map/ppermute | solution.py:381
  163.9 6.7 %collective-permute-done.24.refs_6_ = bf16[160,1024]{1,0:T(8,128)(2,1)S(1)} collective-permute-done((bf16[160,1024]{1,0:T(8,128)(2,1)S(1)}, bf16[160,1024]{1,0:T(8,128)(2,1)S(1)}, u32[]{:S(2)}, u32[]{:S(2)}) %collective-permute-start.24) | collective-permute-done | bytes 327712 | tf_op jit(solution)/shard_map/ppermute | solution.py:381
  170.7 2.7 %collective-permute-start.34 = (bf16[160,1024]{1,0:T(8,128)(2,1)S(1)}, bf16[160,1024]{1,0:T(8,128)(2,1)S(1)}, u32[]{:S(2)}, u32[]{:S(2)}) collective-permute-start(bf16[160,1024]{1,0:T(8,128)(2,1)S(1)} %collective-permute-done.33.refs_9_), channel_id=1, source_target_pairs={{0,193},{1,0},{64,1},{65,64},{128,65},{129,128},{192,129},{193,192... | collective-permute-start | bytes 983048 | tf_op jit(solution)/shard_map/ppermute | solution.py:381
  173.3 0.8 collective-permute-done.28.refs_1_.refs_11_
  174.1 2.8 %collective-permute-start.35 = (bf16[160,1024]{1,0:T(8,128)(2,1)S(1)}, bf16[160,1024]{1,0:T(8,128)(2,1)S(1)}, u32[]{:S(2)}, u32[]{:S(2)}) collective-permute-start(bf16[160,1024]{1,0:T(8,128)(2,1)S(1)} %collective-permute-done.28.refs_1_.refs_11_), channel_id=1, source_target_pairs={{0,193},{1,0},{64,1},{65,64},{128,65},{129,128},{192,129},{193,192... | collective-permute-start | bytes 983048 | tf_op jit(solution)/shard_map/ppermute | solution.py:381
  176.9 0.8 collective-permute-done.31.refs_2_.refs_12_
  177.7 1.9 copy-done.1
  179.5 5.6 %shard_map.88.refs_7_ = f32[1024,512]{1,0:T(8,128)S(1)} custom-call(s32[4]{0:T(128)S(1)} %pad_add_fusion.where_ref, bf16[160,1024]{1,0:T(8,128)(2,1)S(1)} %get-tuple-element.58.refs_0_, bf16[160,1024]{1,0:T(8,128)(2,1)S(1)} %get-tuple-element.59.refs_1_, bf16[160,1024]{1,0:T(8,128)(2,1)S(1)} %collective-permute-done.23.refs_2_, ...), custom_call_target="tpu_custom_call" | custom-call | flops 2684354560 | bytes 8388608 | tf_op jit(solution)/shard_map/pallas_call | solution.py:259
  185.3 2.8 %collective-permute-done.35.refs_4_.refs_14_ = bf16[160,1024]{1,0:T(8,128)(2,1)S(1)} collective-permute-done((bf16[160,1024]{1,0:T(8,128)(2,1)S(1)}, bf16[160,1024]{1,0:T(8,128)(2,1)S(1)}, u32[]{:S(2)}, u32[]{:S(2)}) %collective-permute-start.35) | collective-permute-done | bytes 327712 | tf_op jit(solution)/shard_map/ppermute | solution.py:381
  188.1 3.6 %collective-permute-done.36.refs_5_.refs_15_ = bf16[160,1024]{1,0:T(8,128)(2,1)S(1)} collective-permute-done((bf16[160,1024]{1,0:T(8,128)(2,1)S(1)}, bf16[160,1024]{1,0:T(8,128)(2,1)S(1)}, u32[]{:S(2)}, u32[]{:S(2)}) %collective-permute-start.36) | collective-permute-done | bytes 327712 | tf_op jit(solution)/shard_map/ppermute | solution.py:381
  191.7 3.3 %shard_map.89 = (f32[16,32,512]{2,1,0:T(8,128)S(1)}, f32[16,32,512]{2,1,0:T(8,128)S(1)}) custom-call(s32[4]{0:T(128)S(1)} %pad_add_fusion.where_ref, bf16[160,1024]{1,0:T(8,128)(2,1)S(1)} %collective-permute-done.25.refs_0_.refs_10_, bf16[160,1024]{1,0:T(8,128)(2,1)S(1)} %collective-permute-done.28.refs_1_.refs_11_, ...), custom_call_target="tpu_custom_call" | custom-call | flops 1207959552 | bytes 6291456 | tf_op jit(solution)/shard_map/pallas_call | solution.py:319
  195.1 3.0 %collective-permute-start.37 = (f32[16,32,512]{2,1,0:T(8,128)S(1)}, f32[16,32,512]{2,1,0:T(8,128)S(1)}, u32[]{:S(2)}, u32[]{:S(2)}) collective-permute-start(f32[16,32,512]{2,1,0:T(8,128)S(1)} %get-tuple-element.61), channel_id=1, source_target_pairs={{0,2},{2,0},{4,6},{6,4},{8,10},{10,8},{12,14},{14,12},{16,18},{18,... | collective-permute-start | bytes 3145736 | tf_op jit(solution)/shard_map/ppermute | solution.py:493
  198.0 2.3 %collective-permute-done.37 = f32[16,32,512]{2,1,0:T(8,128)S(1)} collective-permute-done((f32[16,32,512]{2,1,0:T(8,128)S(1)}, f32[16,32,512]{2,1,0:T(8,128)S(1)}, u32[]{:S(2)}, u32[]{:S(2)}) %collective-permute-start.37) | collective-permute-done | bytes 1048608 | tf_op jit(solution)/shard_map/ppermute | solution.py:493
  200.3 1.0 add_convert_fusion
  201.3 4.0 %all-to-all-start.4 = ((bf16[16,32,512]{2,1,0:T(8,128)(2,1)}), bf16[16,32,512]{2,1,0:T(8,128)(2,1)S(1)}, u32[]{:S(2)}, u32[]{:S(2)}) async-start(bf16[16,32,512]{2,1,0:T(8,128)(2,1)} %add_convert_fusion), calls=%async_computation.4 | async-start | bytes 1048576 | tf_op jit(solution)/shard_map/all_to_all | solution.py:495
  205.3 9.1 %shard_map.90 = (f32[512,2560]{1,0:T(8,128)}, bf16[128,2560]{1,0:T(8,128)(2,1)}) custom-call(s32[4]{0:T(128)} %copy-done.9, bf16[160,1024]{1,0:T(8,128)(2,1)} %copy-done.11, bf16[160,1024]{1,0:T(8,128)(2,1)} %copy-done.12, bf16[160,1024]{1,0:T(8,128)(2,1)} %copy-done.15, bf16[160,1024]{1,0:T(8,128)(2,1)} %copy-done.13, bf16[160,1024]{1,0:T(8,128)(2,1)} %copy-done.14, ...), custom_call_target="tpu_custom_call" | custom-call | flops 2684354560 | bytes 12582912 | tf_op jit(solution)/shard_map/pallas_call | solution.py:357
  214.4 1.3 all-to-all-done.4
  (104 shorter events, 10.1 us)
Async XLA Ops:
  0.6 1.3 copy-start
  2.9 20.9 %collective-permute-start = (bf16[320,256]{1,0:T(8,128)(2,1)S(1)}, bf16[320,256]{1,0:T(8,128)(2,1)S(1)}, u32[]{:S(2)}, u32[]{:S(2)}) collective-permute-start(bf16[320,256]{1,0:T(8,128)(2,1)S(1)} %get-tuple-element.74), channel_id=1, source_target_pairs={{0,64},{64,128},{128,192},{192,0},{1,65},{65,129},{129,193},{193,1... | collective-permute-start | bytes 491528 | tf_op jit(solution)/shard_map/ppermute | solution.py:465
  6.7 17.0 %collective-permute-start.1 = (bf16[320,256]{1,0:T(8,128)(2,1)S(1)}, bf16[320,256]{1,0:T(8,128)(2,1)S(1)}, u32[]{:S(2)}, u32[]{:S(2)}) collective-permute-start(bf16[320,256]{1,0:T(8,128)(2,1)S(1)} %get-tuple-element.73), channel_id=1, source_target_pairs={{0,128},{64,192},{128,0},{192,64},{1,129},{65,193},{129,1},{193,65... | collective-permute-start | bytes 491528 | tf_op jit(solution)/shard_map/ppermute | solution.py:465
  11.9 17.0 %collective-permute-start.2 = (bf16[320,256]{1,0:T(8,128)(2,1)S(1)}, bf16[320,256]{1,0:T(8,128)(2,1)S(1)}, u32[]{:S(2)}, u32[]{:S(2)}) collective-permute-start(bf16[320,256]{1,0:T(8,128)(2,1)S(1)} %get-tuple-element.72), channel_id=1, source_target_pairs={{0,192},{64,0},{128,64},{192,128},{1,193},{65,1},{129,65},{193,129... | collective-permute-start | bytes 491528 | tf_op jit(solution)/shard_map/ppermute | solution.py:465
  15.9 16.4 %all-to-all-start = ((bf16[8,128,128]{1,2,0:T(8,128)(2,1)}), bf16[8,128,128]{1,2,0:T(8,128)(2,1)S(1)}, u32[]{:S(2)}, u32[]{:S(2)}) async-start(bf16[8,128,128]{1,2,0:T(8,128)(2,1)} %broadcast_in_dim.28), calls=%async_computation | async-start | bytes 524288 | tf_op jit(solution)/shard_map/all_to_all | solution.py:405
  23.8 167.9 %copy-start.9 = (s32[4]{0:T(128)}, s32[4]{0:T(128)S(1)}, u32[]{:S(2)}) copy-start(s32[4]{0:T(128)S(1)} %pad_add_fusion.where_ref) | copy-start | bytes 52
  32.3 68.8 %all-to-all-start.1 = ((bf16[8,320,512]{2,1,0:T(8,128)(2,1)}), bf16[8,320,512]{2,1,0:T(8,128)(2,1)}, u32[]{:S(2)}, u32[]{:S(2)}) async-start(bf16[8,320,512]{2,1,0:T(8,128)(2,1)} %bitcast.29), calls=%async_computation.1 | async-start | bytes 5242880 | tf_op jit(solution)/shard_map/all_to_all | solution.py:477
  37.4 8.8 %collective-permute-start.3 = (bf16[128,512]{1,0:T(8,128)(2,1)S(1)}, bf16[128,512]{1,0:T(8,128)(2,1)S(1)}, u32[]{:S(2)}, u32[]{:S(2)}) collective-permute-start(bf16[128,512]{1,0:T(8,128)(2,1)S(1)} %get-tuple-element.38), channel_id=1, source_target_pairs={{0,16},{2,18},{4,20},{6,22},{8,24},{10,26},{12,28},{14,30},{16,32}... | collective-permute-start | bytes 393224 | tf_op jit(solution)/shard_map/ppermute | solution.py:416
  38.7 8.6 %collective-permute-start.4 = (bf16[128,512]{1,0:T(8,128)(2,1)S(1)}, bf16[128,512]{1,0:T(8,128)(2,1)S(1)}, u32[]{:S(2)}, u32[]{:S(2)}) collective-permute-start(bf16[128,512]{1,0:T(8,128)(2,1)S(1)} %get-tuple-element.38), channel_id=1, source_target_pairs={{0,32},{2,34},{4,36},{6,38},{8,40},{10,42},{12,44},{14,46},{16,48}... | collective-permute-start | bytes 393224 | tf_op jit(solution)/shard_map/ppermute | solution.py:416
  41.2 6.1 %collective-permute-start.5 = (bf16[128,512]{1,0:T(8,128)(2,1)S(1)}, bf16[128,512]{1,0:T(8,128)(2,1)S(1)}, u32[]{:S(2)}, u32[]{:S(2)}) collective-permute-start(bf16[128,512]{1,0:T(8,128)(2,1)S(1)} %get-tuple-element.38), channel_id=1, source_target_pairs={{0,48},{2,50},{4,52},{6,54},{8,56},{10,58},{12,60},{14,62},{16,0},... | collective-permute-start | bytes 393224 | tf_op jit(solution)/shard_map/ppermute | solution.py:416
  42.3 5.4 %collective-permute-start.6 = (bf16[128,512]{1,0:T(8,128)(2,1)S(1)}, bf16[128,512]{1,0:T(8,128)(2,1)S(1)}, u32[]{:S(2)}, u32[]{:S(2)}) collective-permute-start(bf16[128,512]{1,0:T(8,128)(2,1)S(1)} %get-tuple-element.42), channel_id=1, source_target_pairs={{0,4},{2,6},{4,8},{6,10},{8,12},{10,14},{12,0},{14,2},{16,20},{18,... | collective-permute-start | bytes 393224 | tf_op jit(solution)/shard_map/ppermute | solution.py:416
  43.6 6.8 %collective-permute-start.7 = (bf16[128,512]{1,0:T(8,128)(2,1)S(1)}, bf16[128,512]{1,0:T(8,128)(2,1)S(1)}, u32[]{:S(2)}, u32[]{:S(2)}) collective-permute-start(bf16[128,512]{1,0:T(8,128)(2,1)S(1)} %get-tuple-element.42), channel_id=1, source_target_pairs={{0,8},{2,10},{4,12},{6,14},{8,0},{10,2},{12,4},{14,6},{16,24},{18,... | collective-permute-start | bytes 393224 | tf_op jit(solution)/shard_map/ppermute | solution.py:416
  46.3 4.2 %collective-permute-start.8 = (bf16[128,512]{1,0:T(8,128)(2,1)S(1)}, bf16[128,512]{1,0:T(8,128)(2,1)S(1)}, u32[]{:S(2)}, u32[]{:S(2)}) collective-permute-start(bf16[128,512]{1,0:T(8,128)(2,1)S(1)} %get-tuple-element.42), channel_id=1, source_target_pairs={{0,12},{2,14},{4,0},{6,2},{8,4},{10,6},{12,8},{14,10},{16,28},{18,... | collective-permute-start | bytes 393224 | tf_op jit(solution)/shard_map/ppermute | solution.py:416
  50.5 11.6 %collective-permute-start.10 = (bf16[512,512]{1,0:T(8,128)(2,1)S(1)}, bf16[512,512]{1,0:T(8,128)(2,1)S(1)}, u32[]{:S(2)}, u32[]{:S(2)}) collective-permute-start(bf16[512,512]{1,0:T(8,128)(2,1)S(1)} %constant_dynamic-update-slice_fusion.4.refs_2_), channel_id=1, source_target_pairs={{0,16},{2,18},{4,20},{6,22},{8,24},{10,26},{12,28},{14,30},{16,32}... | collective-permute-start | bytes 1572872 | tf_op jit(solution)/shard_map/ppermute | solution.py:416
  50.9 20.4 %collective-permute-start.12 = (bf16[512,512]{1,0:T(8,128)(2,1)S(1)}, bf16[512,512]{1,0:T(8,128)(2,1)S(1)}, u32[]{:S(2)}, u32[]{:S(2)}) collective-permute-start(bf16[512,512]{1,0:T(8,128)(2,1)S(1)} %constant_dynamic-update-slice_fusion.4.refs_2_), channel_id=1, source_target_pairs={{0,32},{2,34},{4,36},{6,38},{8,40},{10,42},{12,44},{14,46},{16,48}... | collective-permute-start | bytes 1572872 | tf_op jit(solution)/shard_map/ppermute | solution.py:416
  51.9 24.3 %collective-permute-start.14 = (bf16[512,512]{1,0:T(8,128)(2,1)S(1)}, bf16[512,512]{1,0:T(8,128)(2,1)S(1)}, u32[]{:S(2)}, u32[]{:S(2)}) collective-permute-start(bf16[512,512]{1,0:T(8,128)(2,1)S(1)} %constant_dynamic-update-slice_fusion.4.refs_2_), channel_id=1, source_target_pairs={{0,48},{2,50},{4,52},{6,54},{8,56},{10,58},{12,60},{14,62},{16,0},... | collective-permute-start | bytes 1572872 | tf_op jit(solution)/shard_map/ppermute | solution.py:416
  53.5 22.6 %collective-permute-start.11 = (bf16[512,512]{1,0:T(8,128)(2,1)S(1)}, bf16[512,512]{1,0:T(8,128)(2,1)S(1)}, u32[]{:S(2)}, u32[]{:S(2)}) collective-permute-start(bf16[512,512]{1,0:T(8,128)(2,1)S(1)} %constant_dynamic-update-slice_fusion.refs_0_), channel_id=1, source_target_pairs={{0,8},{2,10},{4,12},{6,14},{8,0},{10,2},{12,4},{14,6},{16,24},{18,... | collective-permute-start | bytes 1572872 | tf_op jit(solution)/shard_map/ppermute | solution.py:416
  55.8 23.0 %collective-permute-start.13 = (bf16[512,512]{1,0:T(8,128)(2,1)S(1)}, bf16[512,512]{1,0:T(8,128)(2,1)S(1)}, u32[]{:S(2)}, u32[]{:S(2)}) collective-permute-start(bf16[512,512]{1,0:T(8,128)(2,1)S(1)} %constant_dynamic-update-slice_fusion.refs_0_), channel_id=1, source_target_pairs={{0,12},{2,14},{4,0},{6,2},{8,4},{10,6},{12,8},{14,10},{16,28},{18,... | collective-permute-start | bytes 1572872 | tf_op jit(solution)/shard_map/ppermute | solution.py:416
  62.1 16.7 %collective-permute-start.9 = (bf16[512,512]{1,0:T(8,128)(2,1)S(1)}, bf16[512,512]{1,0:T(8,128)(2,1)S(1)}, u32[]{:S(2)}, u32[]{:S(2)}) collective-permute-start(bf16[512,512]{1,0:T(8,128)(2,1)S(1)} %constant_dynamic-update-slice_fusion.refs_0_), channel_id=1, source_target_pairs={{0,4},{2,6},{4,8},{6,10},{8,12},{10,14},{12,0},{14,2},{16,20},{18,... | collective-permute-start | bytes 1572872 | tf_op jit(solution)/shard_map/ppermute | solution.py:416
  78.8 10.5 %collective-permute-start.15 = (bf16[512,512]{1,0:T(8,128)(2,1)S(1)}, bf16[512,512]{1,0:T(8,128)(2,1)S(1)}, u32[]{:S(2)}, u32[]{:S(2)}) collective-permute-start(bf16[512,512]{1,0:T(8,128)(2,1)S(1)} %constant_dynamic-update-slice_fusion.refs_0_), channel_id=1, source_target_pairs={{0,2},{2,0},{4,6},{6,4},{8,10},{10,8},{12,14},{14,12},{16,18},{18,... | collective-permute-start | bytes 1572872 | tf_op jit(solution)/shard_map/ppermute | solution.py:416
  87.8 2.3 %collective-permute-start.16 = (bf16[512,512]{1,0:T(8,128)(2,1)S(1)}, bf16[512,512]{1,0:T(8,128)(2,1)S(1)}, u32[]{:S(2)}, u32[]{:S(2)}) collective-permute-start(bf16[512,512]{1,0:T(8,128)(2,1)S(1)} %constant_dynamic-update-slice_fusion.4.refs_2_), channel_id=1, source_target_pairs={{0,2},{2,0},{4,6},{6,4},{8,10},{10,8},{12,14},{14,12},{16,18},{18,... | collective-permute-start | bytes 1572872 | tf_op jit(solution)/shard_map/ppermute | solution.py:416
  87.8 3.0 %collective-permute-start.17 = (bf16[512,512]{1,0:T(8,128)(2,1)S(1)}, bf16[512,512]{1,0:T(8,128)(2,1)S(1)}, u32[]{:S(2)}, u32[]{:S(2)}) collective-permute-start(bf16[512,512]{1,0:T(8,128)(2,1)S(1)} %collective-permute-done.9.refs_4_), channel_id=1, source_target_pairs={{0,2},{2,0},{4,6},{6,4},{8,10},{10,8},{12,14},{14,12},{16,18},{18,... | collective-permute-start | bytes 1572872 | tf_op jit(solution)/shard_map/ppermute | solution.py:416
  88.3 3.3 %collective-permute-start.18 = (bf16[512,512]{1,0:T(8,128)(2,1)S(1)}, bf16[512,512]{1,0:T(8,128)(2,1)S(1)}, u32[]{:S(2)}, u32[]{:S(2)}) collective-permute-start(bf16[512,512]{1,0:T(8,128)(2,1)S(1)} %collective-permute-done.10.refs_6_), channel_id=1, source_target_pairs={{0,2},{2,0},{4,6},{6,4},{8,10},{10,8},{12,14},{14,12},{16,18},{18,... | collective-permute-start | bytes 1572872 | tf_op jit(solution)/shard_map/ppermute | solution.py:416
  88.3 4.0 %collective-permute-start.19 = (bf16[512,512]{1,0:T(8,128)(2,1)S(1)}, bf16[512,512]{1,0:T(8,128)(2,1)S(1)}, u32[]{:S(2)}, u32[]{:S(2)}) collective-permute-start(bf16[512,512]{1,0:T(8,128)(2,1)S(1)} %collective-permute-done.11.refs_8_), channel_id=1, source_target_pairs={{0,2},{2,0},{4,6},{6,4},{8,10},{10,8},{12,14},{14,12},{16,18},{18,... | collective-permute-start | bytes 1572872 | tf_op jit(solution)/shard_map/ppermute | solution.py:416
  89.3 3.7 %collective-permute-start.20 = (bf16[512,512]{1,0:T(8,128)(2,1)S(1)}, bf16[512,512]{1,0:T(8,128)(2,1)S(1)}, u32[]{:S(2)}, u32[]{:S(2)}) collective-permute-start(bf16[512,512]{1,0:T(8,128)(2,1)S(1)} %collective-permute-done.12.refs_10_), channel_id=1, source_target_pairs={{0,2},{2,0},{4,6},{6,4},{8,10},{10,8},{12,14},{14,12},{16,18},{18,... | collective-permute-start | bytes 1572872 | tf_op jit(solution)/shard_map/ppermute | solution.py:416
  90.1 3.7 %collective-permute-start.21 = (bf16[512,512]{1,0:T(8,128)(2,1)S(1)}, bf16[512,512]{1,0:T(8,128)(2,1)S(1)}, u32[]{:S(2)}, u32[]{:S(2)}) collective-permute-start(bf16[512,512]{1,0:T(8,128)(2,1)S(1)} %collective-permute-done.13.refs_12_), channel_id=1, source_target_pairs={{0,2},{2,0},{4,6},{6,4},{8,10},{10,8},{12,14},{14,12},{16,18},{18,... | collective-permute-start | bytes 1572872 | tf_op jit(solution)/shard_map/ppermute | solution.py:416
  90.8 3.7 %collective-permute-start.22 = (bf16[512,512]{1,0:T(8,128)(2,1)S(1)}, bf16[512,512]{1,0:T(8,128)(2,1)S(1)}, u32[]{:S(2)}, u32[]{:S(2)}) collective-permute-start(bf16[512,512]{1,0:T(8,128)(2,1)S(1)} %collective-permute-done.14.refs_14_), channel_id=1, source_target_pairs={{0,2},{2,0},{4,6},{6,4},{8,10},{10,8},{12,14},{14,12},{16,18},{18,... | collective-permute-start | bytes 1572872 | tf_op jit(solution)/shard_map/ppermute | solution.py:416
  101.1 3.4 %copy-start.2 = (bf16[4096,1024]{1,0:T(8,128)(2,1)S(1)}, bf16[4096,1024]{1,0:T(8,128)(2,1)}, u32[]{:S(2)}) copy-start(bf16[4096,1024]{1,0:T(8,128)(2,1)} %get-tuple-element.54.features_ref) | copy-start | bytes 25165828
  104.5 13.1 %copy-start.21 = (s32[32]{0:T(128)S(1)}, s32[32]{0:T(128)}, u32[]{:S(2)}) copy-start(s32[32]{0:T(128)} %param.9) | copy-start | bytes 388
  110.3 16.2 %all-to-all-start.2 = ((f32[16,24,128]{2,1,0:T(8,128)}), f32[16,24,128]{2,1,0:T(8,128)S(1)}, u32[]{:S(2)}, u32[]{:S(2)}) async-start(f32[16,24,128]{2,1,0:T(8,128)} %get-tuple-element.56), calls=%async_computation.2 | async-start | bytes 393216 | tf_op jit(solution)/shard_map/all_to_all | solution.py:485
  127.3 10.4 %all-to-all-start.3 = ((f32[16,24,128]{2,1,0:T(8,128)}), f32[16,24,128]{2,1,0:T(8,128)S(1)}, u32[]{:S(2)}, u32[]{:S(2)}) async-start(f32[16,24,128]{2,1,0:T(8,128)} %broadcast_in_dim.29), calls=%async_computation.3 | async-start | bytes 393216 | tf_op jit(solution)/shard_map/all_to_all | solution.py:487
  138.9 46.3 %copy-start.11 = (bf16[160,1024]{1,0:T(8,128)(2,1)}, bf16[160,1024]{1,0:T(8,128)(2,1)S(1)}, u32[]{:S(2)}) copy-start(bf16[160,1024]{1,0:T(8,128)(2,1)S(1)} %get-tuple-element.58.refs_0_) | copy-start | bytes 983044
  138.9 46.3 %copy-start.12 = (bf16[160,1024]{1,0:T(8,128)(2,1)}, bf16[160,1024]{1,0:T(8,128)(2,1)S(1)}, u32[]{:S(2)}) copy-start(bf16[160,1024]{1,0:T(8,128)(2,1)S(1)} %get-tuple-element.59.refs_1_) | copy-start | bytes 983044
  138.9 7.5 %collective-permute-start.26 = (bf16[160,1024]{1,0:T(8,128)(2,1)S(1)}, bf16[160,1024]{1,0:T(8,128)(2,1)S(1)}, u32[]{:S(2)}, u32[]{:S(2)}) collective-permute-start(bf16[160,1024]{1,0:T(8,128)(2,1)S(1)} %get-tuple-element.58.refs_0_), channel_id=1, source_target_pairs={{0,193},{1,0},{64,1},{65,64},{128,65},{129,128},{192,129},{193,192... | collective-permute-start | bytes 983048 | tf_op jit(solution)/shard_map/ppermute | solution.py:381
  141.1 8.7 %collective-permute-start.29 = (bf16[160,1024]{1,0:T(8,128)(2,1)S(1)}, bf16[160,1024]{1,0:T(8,128)(2,1)S(1)}, u32[]{:S(2)}, u32[]{:S(2)}) collective-permute-start(bf16[160,1024]{1,0:T(8,128)(2,1)S(1)} %get-tuple-element.59.refs_1_), channel_id=1, source_target_pairs={{0,1},{1,64},{64,65},{65,128},{128,129},{129,192},{192,193},{193,0... | collective-permute-start | bytes 983048 | tf_op jit(solution)/shard_map/ppermute | solution.py:381
  141.1 15.5 %collective-permute-start.23 = (bf16[160,1024]{1,0:T(8,128)(2,1)S(1)}, bf16[160,1024]{1,0:T(8,128)(2,1)S(1)}, u32[]{:S(2)}, u32[]{:S(2)}) collective-permute-start(bf16[160,1024]{1,0:T(8,128)(2,1)S(1)} %get-tuple-element.58.refs_0_), channel_id=1, source_target_pairs={{0,1},{1,64},{64,65},{65,128},{128,129},{129,192},{192,193},{193,0... | collective-permute-start | bytes 983048 | tf_op jit(solution)/shard_map/ppermute | solution.py:381
  141.8 14.8 %collective-permute-start.32 = (bf16[160,1024]{1,0:T(8,128)(2,1)S(1)}, bf16[160,1024]{1,0:T(8,128)(2,1)S(1)}, u32[]{:S(2)}, u32[]{:S(2)}) collective-permute-start(bf16[160,1024]{1,0:T(8,128)(2,1)S(1)} %get-tuple-element.59.refs_1_), channel_id=1, source_target_pairs={{0,193},{1,0},{64,1},{65,64},{128,65},{129,128},{192,129},{193,192... | collective-permute-start | bytes 983048 | tf_op jit(solution)/shard_map/ppermute | solution.py:381
  146.4 38.8 %copy-start.13 = (bf16[160,1024]{1,0:T(8,128)(2,1)}, bf16[160,1024]{1,0:T(8,128)(2,1)S(1)}, u32[]{:S(2)}) copy-start(bf16[160,1024]{1,0:T(8,128)(2,1)S(1)} %collective-permute-done.26.refs_3_) | copy-start | bytes 983044
  146.4 14.0 %collective-permute-start.27 = (bf16[160,1024]{1,0:T(8,128)(2,1)S(1)}, bf16[160,1024]{1,0:T(8,128)(2,1)S(1)}, u32[]{:S(2)}, u32[]{:S(2)}) collective-permute-start(bf16[160,1024]{1,0:T(8,128)(2,1)S(1)} %collective-permute-done.26.refs_3_), channel_id=1, source_target_pairs={{0,193},{1,0},{64,1},{65,64},{128,65},{129,128},{192,129},{193,192... | collective-permute-start | bytes 983048 | tf_op jit(solution)/shard_map/ppermute | solution.py:381
  149.9 35.3 %copy-start.14 = (bf16[160,1024]{1,0:T(8,128)(2,1)}, bf16[160,1024]{1,0:T(8,128)(2,1)S(1)}, u32[]{:S(2)}) copy-start(bf16[160,1024]{1,0:T(8,128)(2,1)S(1)} %collective-permute-done.29.refs_4_) | copy-start | bytes 983044
  149.9 14.0 %collective-permute-start.30 = (bf16[160,1024]{1,0:T(8,128)(2,1)S(1)}, bf16[160,1024]{1,0:T(8,128)(2,1)S(1)}, u32[]{:S(2)}, u32[]{:S(2)}) collective-permute-start(bf16[160,1024]{1,0:T(8,128)(2,1)S(1)} %collective-permute-done.29.refs_4_), channel_id=1, source_target_pairs={{0,1},{1,64},{64,65},{65,128},{128,129},{129,192},{192,193},{193,0... | collective-permute-start | bytes 983048 | tf_op jit(solution)/shard_map/ppermute | solution.py:381
  156.6 28.6 %copy-start.15 = (bf16[160,1024]{1,0:T(8,128)(2,1)}, bf16[160,1024]{1,0:T(8,128)(2,1)S(1)}, u32[]{:S(2)}) copy-start(bf16[160,1024]{1,0:T(8,128)(2,1)S(1)} %collective-permute-done.23.refs_2_) | copy-start | bytes 983044
  156.6 14.0 %collective-permute-start.24 = (bf16[160,1024]{1,0:T(8,128)(2,1)S(1)}, bf16[160,1024]{1,0:T(8,128)(2,1)S(1)}, u32[]{:S(2)}, u32[]{:S(2)}) collective-permute-start(bf16[160,1024]{1,0:T(8,128)(2,1)S(1)} %collective-permute-done.23.refs_2_), channel_id=1, source_target_pairs={{0,1},{1,64},{64,65},{65,128},{128,129},{129,192},{192,193},{193,0... | collective-permute-start | bytes 983048 | tf_op jit(solution)/shard_map/ppermute | solution.py:381
  156.6 28.6 %copy-start.16 = (bf16[160,1024]{1,0:T(8,128)(2,1)}, bf16[160,1024]{1,0:T(8,128)(2,1)S(1)}, u32[]{:S(2)}) copy-start(bf16[160,1024]{1,0:T(8,128)(2,1)S(1)} %collective-permute-done.32.refs_5_) | copy-start | bytes 983044
  156.6 14.0 %collective-permute-start.33 = (bf16[160,1024]{1,0:T(8,128)(2,1)S(1)}, bf16[160,1024]{1,0:T(8,128)(2,1)S(1)}, u32[]{:S(2)}, u32[]{:S(2)}) collective-permute-start(bf16[160,1024]{1,0:T(8,128)(2,1)S(1)} %collective-permute-done.32.refs_5_), channel_id=1, source_target_pairs={{0,193},{1,0},{64,1},{65,64},{128,65},{129,128},{192,129},{193,192... | collective-permute-start | bytes 983048 | tf_op jit(solution)/shard_map/ppermute | solution.py:381
  160.5 24.8 %copy-start.17 = (bf16[160,1024]{1,0:T(8,128)(2,1)}, bf16[160,1024]{1,0:T(8,128)(2,1)S(1)}, u32[]{:S(2)}) copy-start(bf16[160,1024]{1,0:T(8,128)(2,1)S(1)} %collective-permute-done.27.refs_7_) | copy-start | bytes 983044
  160.5 13.6 %collective-permute-start.28 = (bf16[160,1024]{1,0:T(8,128)(2,1)S(1)}, bf16[160,1024]{1,0:T(8,128)(2,1)S(1)}, u32[]{:S(2)}, u32[]{:S(2)}) collective-permute-start(bf16[160,1024]{1,0:T(8,128)(2,1)S(1)} %collective-permute-done.27.refs_7_), channel_id=1, source_target_pairs={{0,193},{1,0},{64,1},{65,64},{128,65},{129,128},{192,129},{193,192... | collective-permute-start | bytes 983048 | tf_op jit(solution)/shard_map/ppermute | solution.py:381
  163.9 21.3 %copy-start.18 = (bf16[160,1024]{1,0:T(8,128)(2,1)}, bf16[160,1024]{1,0:T(8,128)(2,1)S(1)}, u32[]{:S(2)}) copy-start(bf16[160,1024]{1,0:T(8,128)(2,1)S(1)} %collective-permute-done.30.refs_8_) | copy-start | bytes 983044
  163.9 13.8 %collective-permute-start.31 = (bf16[160,1024]{1,0:T(8,128)(2,1)S(1)}, bf16[160,1024]{1,0:T(8,128)(2,1)S(1)}, u32[]{:S(2)}, u32[]{:S(2)}) collective-permute-start(bf16[160,1024]{1,0:T(8,128)(2,1)S(1)} %collective-permute-done.30.refs_8_), channel_id=1, source_target_pairs={{0,1},{1,64},{64,65},{65,128},{128,129},{129,192},{192,193},{193,0... | collective-permute-start | bytes 983048 | tf_op jit(solution)/shard_map/ppermute | solution.py:381
  170.6 14.6 %copy-start.19 = (bf16[160,1024]{1,0:T(8,128)(2,1)}, bf16[160,1024]{1,0:T(8,128)(2,1)S(1)}, u32[]{:S(2)}) copy-start(bf16[160,1024]{1,0:T(8,128)(2,1)S(1)} %collective-permute-done.24.refs_6_) | copy-start | bytes 983044
  170.6 14.6 %collective-permute-start.25 = (bf16[160,1024]{1,0:T(8,128)(2,1)S(1)}, bf16[160,1024]{1,0:T(8,128)(2,1)S(1)}, u32[]{:S(2)}, u32[]{:S(2)}) collective-permute-start(bf16[160,1024]{1,0:T(8,128)(2,1)S(1)} %collective-permute-done.24.refs_6_), channel_id=1, source_target_pairs={{0,1},{1,64},{64,65},{65,128},{128,129},{129,192},{192,193},{193,0... | collective-permute-start | bytes 983048 | tf_op jit(solution)/shard_map/ppermute | solution.py:381
  170.6 14.6 %copy-start.20 = (bf16[160,1024]{1,0:T(8,128)(2,1)}, bf16[160,1024]{1,0:T(8,128)(2,1)S(1)}, u32[]{:S(2)}) copy-start(bf16[160,1024]{1,0:T(8,128)(2,1)S(1)} %collective-permute-done.33.refs_9_) | copy-start | bytes 983044
  170.7 14.6 %collective-permute-start.34 = (bf16[160,1024]{1,0:T(8,128)(2,1)S(1)}, bf16[160,1024]{1,0:T(8,128)(2,1)S(1)}, u32[]{:S(2)}, u32[]{:S(2)}) collective-permute-start(bf16[160,1024]{1,0:T(8,128)(2,1)S(1)} %collective-permute-done.33.refs_9_), channel_id=1, source_target_pairs={{0,193},{1,0},{64,1},{65,64},{128,65},{129,128},{192,129},{193,192... | collective-permute-start | bytes 983048 | tf_op jit(solution)/shard_map/ppermute | solution.py:381
  174.1 17.6 %copy-start.3 = (bf16[160,1024]{1,0:T(8,128)(2,1)}, bf16[160,1024]{1,0:T(8,128)(2,1)S(1)}, u32[]{:S(2)}) copy-start(bf16[160,1024]{1,0:T(8,128)(2,1)S(1)} %collective-permute-done.28.refs_1_.refs_11_) | copy-start | bytes 983044
  174.1 14.0 %collective-permute-start.35 = (bf16[160,1024]{1,0:T(8,128)(2,1)S(1)}, bf16[160,1024]{1,0:T(8,128)(2,1)S(1)}, u32[]{:S(2)}, u32[]{:S(2)}) collective-permute-start(bf16[160,1024]{1,0:T(8,128)(2,1)S(1)} %collective-permute-done.28.refs_1_.refs_11_), channel_id=1, source_target_pairs={{0,193},{1,0},{64,1},{65,64},{128,65},{129,128},{192,129},{193,192... | collective-permute-start | bytes 983048 | tf_op jit(solution)/shard_map/ppermute | solution.py:381
  177.7 14.1 %copy-start.4 = (bf16[160,1024]{1,0:T(8,128)(2,1)}, bf16[160,1024]{1,0:T(8,128)(2,1)S(1)}, u32[]{:S(2)}) copy-start(bf16[160,1024]{1,0:T(8,128)(2,1)S(1)} %collective-permute-done.31.refs_2_.refs_12_) | copy-start | bytes 983044
  177.7 14.0 %collective-permute-start.36 = (bf16[160,1024]{1,0:T(8,128)(2,1)S(1)}, bf16[160,1024]{1,0:T(8,128)(2,1)S(1)}, u32[]{:S(2)}, u32[]{:S(2)}) collective-permute-start(bf16[160,1024]{1,0:T(8,128)(2,1)S(1)} %collective-permute-done.31.refs_2_.refs_12_), channel_id=1, source_target_pairs={{0,1},{1,64},{64,65},{65,128},{128,129},{129,192},{192,193},{193,0... | collective-permute-start | bytes 983048 | tf_op jit(solution)/shard_map/ppermute | solution.py:381
  177.7 1.9 copy-start.1
  185.3 9.7 %copy-start.5 = (bf16[160,1024]{1,0:T(8,128)(2,1)}, bf16[160,1024]{1,0:T(8,128)(2,1)S(1)}, u32[]{:S(2)}) copy-start(bf16[160,1024]{1,0:T(8,128)(2,1)S(1)} %collective-permute-done.25.refs_0_.refs_10_) | copy-start | bytes 983044
  185.3 9.7 %copy-start.6 = (bf16[160,1024]{1,0:T(8,128)(2,1)}, bf16[160,1024]{1,0:T(8,128)(2,1)S(1)}, u32[]{:S(2)}) copy-start(bf16[160,1024]{1,0:T(8,128)(2,1)S(1)} %collective-permute-done.34.refs_3_.refs_13_) | copy-start | bytes 983044
  188.1 6.9 %copy-start.7 = (bf16[160,1024]{1,0:T(8,128)(2,1)}, bf16[160,1024]{1,0:T(8,128)(2,1)S(1)}, u32[]{:S(2)}) copy-start(bf16[160,1024]{1,0:T(8,128)(2,1)S(1)} %collective-permute-done.35.refs_4_.refs_14_) | copy-start | bytes 983044
  191.7 3.3 %copy-start.8 = (bf16[160,1024]{1,0:T(8,128)(2,1)}, bf16[160,1024]{1,0:T(8,128)(2,1)S(1)}, u32[]{:S(2)}) copy-start(bf16[160,1024]{1,0:T(8,128)(2,1)S(1)} %collective-permute-done.36.refs_5_.refs_15_) | copy-start | bytes 983044
  195.1 5.3 %collective-permute-start.37 = (f32[16,32,512]{2,1,0:T(8,128)S(1)}, f32[16,32,512]{2,1,0:T(8,128)S(1)}, u32[]{:S(2)}, u32[]{:S(2)}) collective-permute-start(f32[16,32,512]{2,1,0:T(8,128)S(1)} %get-tuple-element.61), channel_id=1, source_target_pairs={{0,2},{2,0},{4,6},{6,4},{8,10},{10,8},{12,14},{14,12},{16,18},{18,... | collective-permute-start | bytes 3145736 | tf_op jit(solution)/shard_map/ppermute | solution.py:493
  201.3 14.3 %all-to-all-start.4 = ((bf16[16,32,512]{2,1,0:T(8,128)(2,1)}), bf16[16,32,512]{2,1,0:T(8,128)(2,1)S(1)}, u32[]{:S(2)}, u32[]{:S(2)}) async-start(bf16[16,32,512]{2,1,0:T(8,128)(2,1)} %add_convert_fusion), calls=%async_computation.4 | async-start | bytes 1048576 | tf_op jit(solution)/shard_map/all_to_all | solution.py:495
  (1 other events, 1.0 us)

commit v5 on v4

--- a/solution.py
+++ b/solution.py
@@ -92,24 +92,19 @@
 
 
 def assemble_kernel(side, origins, where_ref, *refs):
-    arrays, (out_ref, own_ref, sem) = refs[: len(origins)], refs[len(origins) :]
+    arrays, (out_ref, sem) = refs[: len(origins)], refs[len(origins) :]
     for _, copy in place_columns(where_ref[2], side, arrays, origins, out_ref, sem):
         copy.wait()
-    depth = own_ref.shape[0]
-    own_ref[...] = out_ref[pl.ds(pl.multiple_of(where_ref[0] * depth, depth), depth), :]
-
-
-def assemble(where, arrays, origins, side, depth):
+
+
+def assemble(where, arrays, origins, side):
     height = len(origins[0][0]) * len(arrays) // 2 * (arrays[0].shape[0] // len(origins[0][0]))
     rows = 2 * arrays[0].shape[1]
     return pl.pallas_call(
         functools.partial(assemble_kernel, side, origins),
         in_specs=[SMEM] + [HBM] * len(arrays),
-        out_specs=[VMEM] * 2,
-        out_shape=[
-            jax.ShapeDtypeStruct((height, rows), BF16),
-            jax.ShapeDtypeStruct((depth, rows), BF16),
-        ],
+        out_specs=VMEM,
+        out_shape=jax.ShapeDtypeStruct((height, rows), BF16),
         scratch_shapes=[pltpu.SemaphoreType.DMA((len(origins[0][0]), len(arrays)))],
         compiler_params=params(40),
         cost_estimate=pl.CostEstimate(flops=0, bytes_accessed=0, transcendentals=0),
@@ -307,7 +302,7 @@
         part = part.reshape(chips, 2, per, part.shape[1])
         even, odd = part[:, 0], part[:, 1]
         keep_ref[pl.ds(i * chips, chips)] = jnp.where(first, even, odd)
-        give_ref[pl.ds(i * chips, chips)] = jnp.where(first, odd, even)
+        give_ref[pl.ds(i * chips, chips)] = jnp.where(first, odd, even).astype(BF16)
 
 
 def late_features(where, blocks, hops, head, part, ring, per):
@@ -315,12 +310,12 @@
     height, rows = blocks[0].shape
     count = len({back for back, _ in hops})
     span = -(-2 * height // 128) * 128
-    shape = jax.ShapeDtypeStruct((rows // (2 * per), per, depth), F32)
+    shape = (rows // (2 * per), per, depth)
     return pl.pallas_call(
         functools.partial(late_kernel, ring, hops),
         in_specs=[SMEM] + [VMEM] * len(blocks) + [HBM, VMEM],
         out_specs=[VMEM] * 2,
-        out_shape=[shape, shape],
+        out_shape=[jax.ShapeDtypeStruct(shape, F32), jax.ShapeDtypeStruct(shape, BF16)],
         scratch_shapes=[
             pltpu.VMEM((depth, count * span), BF16),
             pltpu.VMEM((count * span, rows), BF16),
@@ -335,29 +330,34 @@
 
 def head_kernel(hops, where_ref, *refs):
     blocks, rest = refs[: len(hops)], refs[len(hops) :]
-    features_ref, out_ref, own_ref, all_ref, sem = rest
+    features_hbm, out_ref, own_ref, all_ref, own_features, sem, own_sem = rest
+    depth = own_features.shape[0]
     step = pl.program_id(0)
 
     @pl.when(step == 0)
     def _():
+        mine = pl.ds(pl.multiple_of(where_ref[0] * depth, depth), depth)
+        copy = pltpu.make_async_copy(features_hbm.at[mine], own_features, own_sem)
+        copy.start()
         fetch_blocks(where_ref, blocks, hops, all_ref, sem)
+        copy.wait()
 
     share, tile = own_ref.shape
     own_cols = pl.ds(pl.multiple_of(where_ref[0] * share, share), share)
     rows = pl.ds(pl.multiple_of(step * tile, tile), tile)
     out_ref[...] = lax.dot_general(
-        features_ref[...], all_ref[rows, :], (((1,), (1,)), ((), ())), preferred_element_type=F32
+        own_features[...], all_ref[rows, :], (((1,), (1,)), ((), ())), preferred_element_type=F32
     )
     own_ref[...] = all_ref[rows, own_cols].astype(F32).T.astype(BF16)
 
 
-def head_parts(where, blocks, hops, features, vocab, share):
-    depth, rows = features.shape
+def head_parts(where, blocks, hops, features, depth, vocab, share):
+    rows = blocks[0].shape[1]
     tile = 512
     return pl.pallas_call(
         functools.partial(head_kernel, hops),
         grid=(vocab // tile,),
-        in_specs=[SMEM] + [HBM] * len(blocks) + [pl.BlockSpec((depth, rows), lambda i: (0, 0))],
+        in_specs=[SMEM] + [HBM] * (len(blocks) + 1),
         out_specs=[
             pl.BlockSpec((depth, tile), lambda i: (0, i)),
             pl.BlockSpec((share, tile), lambda i: (0, i)),
@@ -368,7 +368,9 @@
         ],
         scratch_shapes=[
             pltpu.VMEM((vocab, rows), BF16),
+            pltpu.VMEM((depth, rows), BF16),
             pltpu.SemaphoreType.DMA((len(blocks),)),
+            pltpu.SemaphoreType.DMA,
         ],
         compiler_params=params(58),
         cost_estimate=pl.CostEstimate(
@@ -473,7 +475,7 @@
     slices, column, teachers = lax.optimization_barrier((slices, column, teachers))
     side = math.isqrt(chips)
     arrays, origins = spread(column.reshape(rows, piece).T, side, side)
-    features, own_features = assemble(where, arrays, origins, side, depth)
+    features = assemble(where, arrays, origins, side)
     head_cut = lax.all_to_all(slices, ("sub", "tok"), 0, 0)
     weights = row_weights(sizes, rows).reshape(rows // 128, 128)
 
@@ -491,11 +493,11 @@
     part = early_features(where, blocks[:-6], hops[:-6], head)
     keep, give = late_features(where, blocks[-6:], hops[-6:], head, part, ring, rows // vocs)
     given = lax.ppermute(give, "voc", cores)
-    sums, where = lax.optimization_barrier(((keep + given).astype(BF16), where))
+    sums, where = lax.optimization_barrier(((keep + given.astype(F32)).astype(BF16), where))
     sums = lax.all_to_all(sums, "voc", 0, 0, axis_index_groups=groups)
     feature_grad = jnp.sum(sums.astype(F32), axis=0)
 
-    head_grad, local_grad = head_parts(where, blocks, hops, own_features, vocab, share)
+    head_grad, local_grad = head_parts(where, blocks, hops, features, depth, vocab, share)
     return head_grad, feature_grad, local_grad, divergence.reshape(share)
 
 

time: 217 us -> 215 us (level)
    unnamed x50 -> x48, local copies, waits for them, and re-layouts: 6.87 us -> 5.87 us
where the time goes in v5:
time: 215 us
  starting transfers between devices  85.7 us (40%)
  waiting for transfers between devices  80.6 us (37%)
  Pallas kernels  30.8 us (14%)
  local copies, waits for them, and re-layouts  12.9 us (6%)
  other arithmetic  2.81 us (1%)
    ppermute x20, waiting for transfers between devices, shift(): return lax.ppermute(values, 'voc', pairs)  28.8 us
    ppermute x20, starting transfers between devices, shift(): return lax.ppermute(values, 'voc', pairs)  28.2 us
    ppermute x14, waiting for transfers between devices, ring_shift(): lax.ppermute(values, RING, [(i, (i + step) % size) for i in range(size)])  25.2 us
    ppermute x14, starting transfers between devices, ring_shift(): lax.ppermute(values, RING, [(i, (i + step) % size) for i in range(size)])  19.9 us
    ppermute x3, starting transfers between devices, on_device(): lax.ppermute(part, 'tok', [(i, (i + shift) % toks) for i in range(toks)])  11.4 us
    pallas_call x1, Pallas kernels, head_parts(): pl.pallas_call(functools.partial(head_kernel, hops), grid=(vocab // tile,...  8.83 us
    all_to_all x1, waiting for transfers between devices, on_device(): lax.all_to_all(stats, ('tok', 'voc', 'sub'), 0, 0, axis_index_groups=mixed)  8.65 us
    all_to_all x1, starting transfers between devices, on_device(): lax.all_to_all(stats, ('tok', 'voc', 'sub'), 0, 0, axis_index_groups=mixed)  7.32 us
  transfers between devices with their start and end apart: 43, of which 29 were waited for; matrix products, arithmetic and copies ran while one was open for 3% of the time, Pallas kernels for 10%

profile of v5, /device:TPU:1, one launch (start us, length us, event | category | flops | bytes accessed | tf_op | source)
XLA Modules:
  0.0 214.5 jit_solution(13094497623838476931)
XLA Ops:
  0.7 0.8 broadcast_subtract_fusion
  2.9 3.9 %collective-permute-start = (bf16[320,256]{1,0:T(8,128)(2,1)S(1)}, bf16[320,256]{1,0:T(8,128)(2,1)S(1)}, u32[]{:S(2)}, u32[]{:S(2)}) collective-permute-start(bf16[320,256]{1,0:T(8,128)(2,1)S(1)} %get-tuple-element.70), channel_id=1, source_target_pairs={{0,64},{64,128},{128,192},{192,0},{1,65},{65,129},{129,193},{193,1... | collective-permute-start | bytes 491528 | tf_op jit(solution)/shard_map/ppermute | solution.py:467
  6.7 5.1 %collective-permute-start.1 = (bf16[320,256]{1,0:T(8,128)(2,1)S(1)}, bf16[320,256]{1,0:T(8,128)(2,1)S(1)}, u32[]{:S(2)}, u32[]{:S(2)}) collective-permute-start(bf16[320,256]{1,0:T(8,128)(2,1)S(1)} %get-tuple-element.69), channel_id=1, source_target_pairs={{0,128},{64,192},{128,0},{192,64},{1,129},{65,193},{129,1},{193,65... | collective-permute-start | bytes 491528 | tf_op jit(solution)/shard_map/ppermute | solution.py:467
  11.9 2.4 %collective-permute-start.2 = (bf16[320,256]{1,0:T(8,128)(2,1)S(1)}, bf16[320,256]{1,0:T(8,128)(2,1)S(1)}, u32[]{:S(2)}, u32[]{:S(2)}) collective-permute-start(bf16[320,256]{1,0:T(8,128)(2,1)S(1)} %get-tuple-element.68), channel_id=1, source_target_pairs={{0,192},{64,0},{128,64},{192,128},{1,193},{65,1},{129,65},{193,129... | collective-permute-start | bytes 491528 | tf_op jit(solution)/shard_map/ppermute | solution.py:467
  14.2 0.8 constant_dynamic-slice_fusion
  15.1 0.7 broadcast_in_dim.28
  15.9 3.4 %all-to-all-start = ((bf16[8,128,128]{1,2,0:T(8,128)(2,1)}), bf16[8,128,128]{1,2,0:T(8,128)(2,1)S(1)}, u32[]{:S(2)}, u32[]{:S(2)}) async-start(bf16[8,128,128]{1,2,0:T(8,128)(2,1)} %broadcast_in_dim.28), calls=%async_computation | async-start | bytes 524288 | tf_op jit(solution)/shard_map/all_to_all | solution.py:407
  19.3 4.4 %copy.22 = bf16[2560,512]{1,0:T(8,128)(2,1)} copy(bf16[2560,512]{0,1:T(8,128)(2,1)} %bitcast.28) | data formatting | bytes 5242880 | tf_op jit(solution)/shard_map/transpose | solution.py:473
  23.8 5.1 %collective-permute-done.2.refs_3_ = bf16[320,256]{1,0:T(8,128)(2,1)S(1)} collective-permute-done((bf16[320,256]{1,0:T(8,128)(2,1)S(1)}, bf16[320,256]{1,0:T(8,128)(2,1)S(1)}, u32[]{:S(2)}, u32[]{:S(2)}) %collective-permute-start.2) | collective-permute-done | bytes 163872 | tf_op jit(solution)/shard_map/ppermute | solution.py:467
  29.5 2.8 %all-to-all-done = bf16[8,128,128]{1,2,0:T(8,128)(2,1)S(1)} async-done(((bf16[8,128,128]{1,2,0:T(8,128)(2,1)}), bf16[8,128,128]{1,2,0:T(8,128)(2,1)S(1)}, u32[]{:S(2)}, u32[]{:S(2)}) %all-to-all-start) | async-done | bytes 262176 | tf_op jit(solution)/shard_map/all_to_all | solution.py:407
  32.3 5.1 %all-to-all-start.1 = ((bf16[8,320,512]{2,1,0:T(8,128)(2,1)}), bf16[8,320,512]{2,1,0:T(8,128)(2,1)}, u32[]{:S(2)}, u32[]{:S(2)}) async-start(bf16[8,320,512]{2,1,0:T(8,128)(2,1)} %bitcast.29), calls=%async_computation.1 | async-start | bytes 5242880 | tf_op jit(solution)/shard_map/all_to_all | solution.py:479
  37.4 1.3 collective-permute-start.3
  38.7 2.5 %collective-permute-start.4 = (bf16[128,512]{1,0:T(8,128)(2,1)S(1)}, bf16[128,512]{1,0:T(8,128)(2,1)S(1)}, u32[]{:S(2)}, u32[]{:S(2)}) collective-permute-start(bf16[128,512]{1,0:T(8,128)(2,1)S(1)} %get-tuple-element.36), channel_id=1, source_target_pairs={{0,32},{2,34},{4,36},{6,38},{8,40},{10,42},{12,44},{14,46},{16,48}... | collective-permute-start | bytes 393224 | tf_op jit(solution)/shard_map/ppermute | solution.py:418
  41.2 1.1 collective-permute-start.5
  42.3 1.3 collective-permute-start.6
  43.6 2.6 %collective-permute-start.7 = (bf16[128,512]{1,0:T(8,128)(2,1)S(1)}, bf16[128,512]{1,0:T(8,128)(2,1)S(1)}, u32[]{:S(2)}, u32[]{:S(2)}) collective-permute-start(bf16[128,512]{1,0:T(8,128)(2,1)S(1)} %get-tuple-element.40), channel_id=1, source_target_pairs={{0,8},{2,10},{4,12},{6,14},{8,0},{10,2},{12,4},{14,6},{16,24},{18,... | collective-permute-start | bytes 393224 | tf_op jit(solution)/shard_map/ppermute | solution.py:418
  46.3 1.1 collective-permute-start.8
  47.7 2.7 %collective-permute-done.7 = bf16[128,512]{1,0:T(8,128)(2,1)S(1)} collective-permute-done((bf16[128,512]{1,0:T(8,128)(2,1)S(1)}, bf16[128,512]{1,0:T(8,128)(2,1)S(1)}, u32[]{:S(2)}, u32[]{:S(2)}) %collective-permute-start.7) | collective-permute-done | bytes 131104 | tf_op jit(solution)/shard_map/ppermute | solution.py:418
  50.9 1.0 collective-permute-start.12
  51.9 1.5 collective-permute-start.14
  53.5 2.3 %collective-permute-start.11 = (bf16[512,512]{1,0:T(8,128)(2,1)S(1)}, bf16[512,512]{1,0:T(8,128)(2,1)S(1)}, u32[]{:S(2)}, u32[]{:S(2)}) collective-permute-start(bf16[512,512]{1,0:T(8,128)(2,1)S(1)} %constant_dynamic-update-slice_fusion.refs_0_), channel_id=1, source_target_pairs={{0,8},{2,10},{4,12},{6,14},{8,0},{10,2},{12,4},{14,6},{16,24},{18,... | collective-permute-start | bytes 1572872 | tf_op jit(solution)/shard_map/ppermute | solution.py:418
  55.8 1.0 collective-permute-start.13
  56.8 5.3 %collective-permute-done.10.refs_6_ = bf16[512,512]{1,0:T(8,128)(2,1)S(1)} collective-permute-done((bf16[512,512]{1,0:T(8,128)(2,1)S(1)}, bf16[512,512]{1,0:T(8,128)(2,1)S(1)}, u32[]{:S(2)}, u32[]{:S(2)}) %collective-permute-start.10) | collective-permute-done | bytes 524320 | tf_op jit(solution)/shard_map/ppermute | solution.py:418
  62.1 1.0 collective-permute-start.9
  63.1 8.2 %collective-permute-done.12.refs_10_ = bf16[512,512]{1,0:T(8,128)(2,1)S(1)} collective-permute-done((bf16[512,512]{1,0:T(8,128)(2,1)S(1)}, bf16[512,512]{1,0:T(8,128)(2,1)S(1)}, u32[]{:S(2)}, u32[]{:S(2)}) %collective-permute-start.12) | collective-permute-done | bytes 524320 | tf_op jit(solution)/shard_map/ppermute | solution.py:418
  71.3 4.8 %collective-permute-done.14.refs_14_ = bf16[512,512]{1,0:T(8,128)(2,1)S(1)} collective-permute-done((bf16[512,512]{1,0:T(8,128)(2,1)S(1)}, bf16[512,512]{1,0:T(8,128)(2,1)S(1)}, u32[]{:S(2)}, u32[]{:S(2)}) %collective-permute-start.14) | collective-permute-done | bytes 524320 | tf_op jit(solution)/shard_map/ppermute | solution.py:418
  76.2 2.7 %collective-permute-done.13.refs_12_ = bf16[512,512]{1,0:T(8,128)(2,1)S(1)} collective-permute-done((bf16[512,512]{1,0:T(8,128)(2,1)S(1)}, bf16[512,512]{1,0:T(8,128)(2,1)S(1)}, u32[]{:S(2)}, u32[]{:S(2)}) %collective-permute-start.13) | collective-permute-done | bytes 524320 | tf_op jit(solution)/shard_map/ppermute | solution.py:418
  78.8 9.0 %collective-permute-start.15 = (bf16[512,512]{1,0:T(8,128)(2,1)S(1)}, bf16[512,512]{1,0:T(8,128)(2,1)S(1)}, u32[]{:S(2)}, u32[]{:S(2)}) collective-permute-start(bf16[512,512]{1,0:T(8,128)(2,1)S(1)} %constant_dynamic-update-slice_fusion.refs_0_), channel_id=1, source_target_pairs={{0,2},{2,0},{4,6},{6,4},{8,10},{10,8},{12,14},{14,12},{16,18},{18,... | collective-permute-start | bytes 1572872 | tf_op jit(solution)/shard_map/ppermute | solution.py:418
  91.6 0.7 collective-permute-done.19.refs_9_
  92.3 0.7 collective-permute-done.20.refs_11_
  93.1 0.7 collective-permute-done.21.refs_13_
  93.8 0.7 collective-permute-done.22.refs_15_
  94.6 5.5 %shard_map.85.features_ref.refs_16_ = bf16[4096,1024]{1,0:T(8,128)(2,1)} custom-call(s32[4]{0:T(128)S(1)} %pad_add_fusion.where_ref, bf16[512,512]{1,0:T(8,128)(2,1)S(1)} %constant_dynamic-update-slice_fusion.refs_0_, bf16[512,512]{1,0:T(8,128)(2,1)S(1)} %collective-permute-done.15.refs_1_, bf16[512,512]{1,0:T(8,128)(2,1)S(1)} %constant_dynamic-update-slice_fusion.4.refs_2_, ...), custom_call_target="tpu_custom_call" | custom-call | tf_op jit(solution)/shard_map/pallas_call | solution.py:103
  100.1 3.4 %copy-done.1 = bf16[4096,1024]{1,0:T(8,128)(2,1)S(1)} copy-done((bf16[4096,1024]{1,0:T(8,128)(2,1)S(1)}, bf16[4096,1024]{1,0:T(8,128)(2,1)}, u32[]{:S(2)}) %copy-start.1) | copy-done | bytes 8388632
  103.5 5.8 %shard_map.86 = (f32[320,1024]{1,0:T(8,128)S(1)}, f32[16,24,128]{2,1,0:T(8,128)}) custom-call(bf16[8,320,512]{2,1,0:T(8,128)(2,1)} %all-to-all-done.1.head_hbm, bf16[4096,1024]{1,0:T(8,128)(2,1)S(1)} %copy-done.1, bf16[4,320,256]{2,1,0:T(8,128)(2,1)S(1)} %shard_map.84.teacher_ref), custom_call_target="tpu_custom_call" | custom-call | flops 2684354560 | bytes 12582912 | tf_op jit(solution)/shard_map/pallas_call | solution.py:151
  109.3 7.3 %all-to-all-start.2 = ((f32[16,24,128]{2,1,0:T(8,128)}), f32[16,24,128]{2,1,0:T(8,128)S(1)}, u32[]{:S(2)}, u32[]{:S(2)}) async-start(f32[16,24,128]{2,1,0:T(8,128)} %get-tuple-element.53), calls=%async_computation.2 | async-start | bytes 393216 | tf_op jit(solution)/shard_map/all_to_all | solution.py:487
  116.8 8.7 %all-to-all-done.2 = f32[16,24,128]{2,1,0:T(8,128)S(1)} async-done(((f32[16,24,128]{2,1,0:T(8,128)}), f32[16,24,128]{2,1,0:T(8,128)S(1)}, u32[]{:S(2)}, u32[]{:S(2)}) %all-to-all-start.2) | async-done | bytes 196640 | tf_op jit(solution)/shard_map/all_to_all | solution.py:487
  126.3 3.5 %all-to-all-start.3 = ((f32[16,24,128]{2,1,0:T(8,128)}), f32[16,24,128]{2,1,0:T(8,128)S(1)}, u32[]{:S(2)}, u32[]{:S(2)}) async-start(f32[16,24,128]{2,1,0:T(8,128)} %broadcast_in_dim.29), calls=%async_computation.3 | async-start | bytes 393216 | tf_op jit(solution)/shard_map/all_to_all | solution.py:489
  129.9 6.9 %all-to-all-done.3.stats_ref = f32[16,24,128]{2,1,0:T(8,128)S(1)} async-done(((f32[16,24,128]{2,1,0:T(8,128)}), f32[16,24,128]{2,1,0:T(8,128)S(1)}, u32[]{:S(2)}, u32[]{:S(2)}) %all-to-all-start.3) | async-done | bytes 196640 | tf_op jit(solution)/shard_map/all_to_all | solution.py:489
  136.8 1.1 shard_map.87
  137.9 2.2 %collective-permute-start.26 = (bf16[160,1024]{1,0:T(8,128)(2,1)S(1)}, bf16[160,1024]{1,0:T(8,128)(2,1)S(1)}, u32[]{:S(2)}, u32[]{:S(2)}) collective-permute-start(bf16[160,1024]{1,0:T(8,128)(2,1)S(1)} %get-tuple-element.55.refs_0_), channel_id=1, source_target_pairs={{0,193},{1,0},{64,1},{65,64},{128,65},{129,128},{192,129},{193,192... | collective-permute-start | bytes 983048 | tf_op jit(solution)/shard_map/ppermute | solution.py:383
  140.8 2.1 collective-permute-start.32
  142.8 2.6 %collective-permute-done.26.refs_3_ = bf16[160,1024]{1,0:T(8,128)(2,1)S(1)} collective-permute-done((bf16[160,1024]{1,0:T(8,128)(2,1)S(1)}, bf16[160,1024]{1,0:T(8,128)(2,1)S(1)}, u32[]{:S(2)}, u32[]{:S(2)}) %collective-permute-start.26) | collective-permute-done | bytes 327712 | tf_op jit(solution)/shard_map/ppermute | solution.py:383
  145.4 3.4 %collective-permute-start.27 = (bf16[160,1024]{1,0:T(8,128)(2,1)S(1)}, bf16[160,1024]{1,0:T(8,128)(2,1)S(1)}, u32[]{:S(2)}, u32[]{:S(2)}) collective-permute-start(bf16[160,1024]{1,0:T(8,128)(2,1)S(1)} %collective-permute-done.26.refs_3_), channel_id=1, source_target_pairs={{0,193},{1,0},{64,1},{65,64},{128,65},{129,128},{192,129},{193,192... | collective-permute-start | bytes 983048 | tf_op jit(solution)/shard_map/ppermute | solution.py:383
  148.8 6.7 %collective-permute-done.23.refs_2_ = bf16[160,1024]{1,0:T(8,128)(2,1)S(1)} collective-permute-done((bf16[160,1024]{1,0:T(8,128)(2,1)S(1)}, bf16[160,1024]{1,0:T(8,128)(2,1)S(1)}, u32[]{:S(2)}, u32[]{:S(2)}) %collective-permute-start.23) | collective-permute-done | bytes 327712 | tf_op jit(solution)/shard_map/ppermute | solution.py:383
  155.6 2.7 %collective-permute-start.33 = (bf16[160,1024]{1,0:T(8,128)(2,1)S(1)}, bf16[160,1024]{1,0:T(8,128)(2,1)S(1)}, u32[]{:S(2)}, u32[]{:S(2)}) collective-permute-start(bf16[160,1024]{1,0:T(8,128)(2,1)S(1)} %collective-permute-done.32.refs_5_), channel_id=1, source_target_pairs={{0,193},{1,0},{64,1},{65,64},{128,65},{129,128},{192,129},{193,192... | collective-permute-start | bytes 983048 | tf_op jit(solution)/shard_map/ppermute | solution.py:383
  158.3 1.2 collective-permute-done.27.refs_7_
  159.5 3.4 %collective-permute-start.28 = (bf16[160,1024]{1,0:T(8,128)(2,1)S(1)}, bf16[160,1024]{1,0:T(8,128)(2,1)S(1)}, u32[]{:S(2)}, u32[]{:S(2)}) collective-permute-start(bf16[160,1024]{1,0:T(8,128)(2,1)S(1)} %collective-permute-done.27.refs_7_), channel_id=1, source_target_pairs={{0,193},{1,0},{64,1},{65,64},{128,65},{129,128},{192,129},{193,192... | collective-permute-start | bytes 983048 | tf_op jit(solution)/shard_map/ppermute | solution.py:383
  162.9 6.7 %collective-permute-done.24.refs_6_ = bf16[160,1024]{1,0:T(8,128)(2,1)S(1)} collective-permute-done((bf16[160,1024]{1,0:T(8,128)(2,1)S(1)}, bf16[160,1024]{1,0:T(8,128)(2,1)S(1)}, u32[]{:S(2)}, u32[]{:S(2)}) %collective-permute-start.24) | collective-permute-done | bytes 327712 | tf_op jit(solution)/shard_map/ppermute | solution.py:383
  169.6 2.7 %collective-permute-start.34 = (bf16[160,1024]{1,0:T(8,128)(2,1)S(1)}, bf16[160,1024]{1,0:T(8,128)(2,1)S(1)}, u32[]{:S(2)}, u32[]{:S(2)}) collective-permute-start(bf16[160,1024]{1,0:T(8,128)(2,1)S(1)} %collective-permute-done.33.refs_9_), channel_id=1, source_target_pairs={{0,193},{1,0},{64,1},{65,64},{128,65},{129,128},{192,129},{193,192... | collective-permute-start | bytes 983048 | tf_op jit(solution)/shard_map/ppermute | solution.py:383
  172.3 0.8 collective-permute-done.28.refs_1_.refs_11_
  173.1 2.8 %collective-permute-start.35 = (bf16[160,1024]{1,0:T(8,128)(2,1)S(1)}, bf16[160,1024]{1,0:T(8,128)(2,1)S(1)}, u32[]{:S(2)}, u32[]{:S(2)}) collective-permute-start(bf16[160,1024]{1,0:T(8,128)(2,1)S(1)} %collective-permute-done.28.refs_1_.refs_11_), channel_id=1, source_target_pairs={{0,193},{1,0},{64,1},{65,64},{128,65},{129,128},{192,129},{193,192... | collective-permute-start | bytes 983048 | tf_op jit(solution)/shard_map/ppermute | solution.py:383
  175.9 0.8 collective-permute-done.31.refs_2_.refs_12_
  176.7 1.9 copy-done.2
  178.5 5.6 %shard_map.88.refs_7_ = f32[1024,512]{1,0:T(8,128)S(1)} custom-call(s32[4]{0:T(128)S(1)} %pad_add_fusion.where_ref, bf16[160,1024]{1,0:T(8,128)(2,1)S(1)} %get-tuple-element.55.refs_0_, bf16[160,1024]{1,0:T(8,128)(2,1)S(1)} %get-tuple-element.56.refs_1_, bf16[160,1024]{1,0:T(8,128)(2,1)S(1)} %collective-permute-done.23.refs_2_, ...), custom_call_target="tpu_custom_call" | custom-call | flops 2684354560 | bytes 8388608 | tf_op jit(solution)/shard_map/pallas_call | solution.py:254
  184.3 2.8 %collective-permute-done.35.refs_4_.refs_14_ = bf16[160,1024]{1,0:T(8,128)(2,1)S(1)} collective-permute-done((bf16[160,1024]{1,0:T(8,128)(2,1)S(1)}, bf16[160,1024]{1,0:T(8,128)(2,1)S(1)}, u32[]{:S(2)}, u32[]{:S(2)}) %collective-permute-start.35) | collective-permute-done | bytes 327712 | tf_op jit(solution)/shard_map/ppermute | solution.py:383
  187.1 3.6 %collective-permute-done.36.refs_5_.refs_15_ = bf16[160,1024]{1,0:T(8,128)(2,1)S(1)} collective-permute-done((bf16[160,1024]{1,0:T(8,128)(2,1)S(1)}, bf16[160,1024]{1,0:T(8,128)(2,1)S(1)}, u32[]{:S(2)}, u32[]{:S(2)}) %collective-permute-start.36) | collective-permute-done | bytes 327712 | tf_op jit(solution)/shard_map/ppermute | solution.py:383
  190.7 3.3 %shard_map.89 = (f32[16,32,512]{2,1,0:T(8,128)S(1)}, bf16[16,32,512]{2,1,0:T(8,128)(2,1)S(1)}) custom-call(s32[4]{0:T(128)S(1)} %pad_add_fusion.where_ref, bf16[160,1024]{1,0:T(8,128)(2,1)S(1)} %collective-permute-done.25.refs_0_.refs_10_, bf16[160,1024]{1,0:T(8,128)(2,1)S(1)} %collective-permute-done.28.refs_1_.refs_11_, ...), custom_call_target="tpu_custom_call" | custom-call | flops 1207959552 | bytes 6291456 | tf_op jit(solution)/shard_map/pallas_call | solution.py:314
  194.0 3.0 %collective-permute-start.37 = (bf16[16,32,512]{2,1,0:T(8,128)(2,1)S(1)}, bf16[16,32,512]{2,1,0:T(8,128)(2,1)S(1)}, u32[]{:S(2)}, u32[]{:S(2)}) collective-permute-start(bf16[16,32,512]{2,1,0:T(8,128)(2,1)S(1)} %get-tuple-element.58), channel_id=1, source_target_pairs={{0,2},{2,0},{4,6},{6,4},{8,10},{10,8},{12,14},{14,12},{16,18},{18,... | collective-permute-start | bytes 1572872 | tf_op jit(solution)/shard_map/ppermute | solution.py:495
  197.0 1.5 collective-permute-done.37
  198.5 1.0 add_convert_fusion
  199.5 4.0 %all-to-all-start.4 = ((bf16[16,32,512]{2,1,0:T(8,128)(2,1)}), bf16[16,32,512]{2,1,0:T(8,128)(2,1)S(1)}, u32[]{:S(2)}, u32[]{:S(2)}) async-start(bf16[16,32,512]{2,1,0:T(8,128)(2,1)} %add_convert_fusion), calls=%async_computation.4 | async-start | bytes 1048576 | tf_op jit(solution)/shard_map/all_to_all | solution.py:497
  203.5 8.8 %shard_map.90 = (f32[512,2560]{1,0:T(8,128)}, bf16[128,2560]{1,0:T(8,128)(2,1)}) custom-call(s32[4]{0:T(128)} %copy-done.19, bf16[160,1024]{1,0:T(8,128)(2,1)} %copy-done.9, bf16[160,1024]{1,0:T(8,128)(2,1)} %copy-done.10, bf16[160,1024]{1,0:T(8,128)(2,1)} %copy-done.13, bf16[160,1024]{1,0:T(8,128)(2,1)} %copy-done.11, bf16[160,1024]{1,0:T(8,128)(2,1)} %copy-done.12, ...), custom_call_target="tpu_custom_call" | custom-call | flops 2684354560 | bytes 12582912 | tf_op jit(solution)/shard_map/pallas_call | solution.py:357
  212.3 1.5 all-to-all-done.4
  (102 shorter events, 9.3 us)
Async XLA Ops:
  0.6 1.3 copy-start
  2.9 20.9 %collective-permute-start = (bf16[320,256]{1,0:T(8,128)(2,1)S(1)}, bf16[320,256]{1,0:T(8,128)(2,1)S(1)}, u32[]{:S(2)}, u32[]{:S(2)}) collective-permute-start(bf16[320,256]{1,0:T(8,128)(2,1)S(1)} %get-tuple-element.70), channel_id=1, source_target_pairs={{0,64},{64,128},{128,192},{192,0},{1,65},{65,129},{129,193},{193,1... | collective-permute-start | bytes 491528 | tf_op jit(solution)/shard_map/ppermute | solution.py:467
  6.7 17.0 %collective-permute-start.1 = (bf16[320,256]{1,0:T(8,128)(2,1)S(1)}, bf16[320,256]{1,0:T(8,128)(2,1)S(1)}, u32[]{:S(2)}, u32[]{:S(2)}) collective-permute-start(bf16[320,256]{1,0:T(8,128)(2,1)S(1)} %get-tuple-element.69), channel_id=1, source_target_pairs={{0,128},{64,192},{128,0},{192,64},{1,129},{65,193},{129,1},{193,65... | collective-permute-start | bytes 491528 | tf_op jit(solution)/shard_map/ppermute | solution.py:467
  11.9 17.0 %collective-permute-start.2 = (bf16[320,256]{1,0:T(8,128)(2,1)S(1)}, bf16[320,256]{1,0:T(8,128)(2,1)S(1)}, u32[]{:S(2)}, u32[]{:S(2)}) collective-permute-start(bf16[320,256]{1,0:T(8,128)(2,1)S(1)} %get-tuple-element.68), channel_id=1, source_target_pairs={{0,192},{64,0},{128,64},{192,128},{1,193},{65,1},{129,65},{193,129... | collective-permute-start | bytes 491528 | tf_op jit(solution)/shard_map/ppermute | solution.py:467
  15.9 16.4 %all-to-all-start = ((bf16[8,128,128]{1,2,0:T(8,128)(2,1)}), bf16[8,128,128]{1,2,0:T(8,128)(2,1)S(1)}, u32[]{:S(2)}, u32[]{:S(2)}) async-start(bf16[8,128,128]{1,2,0:T(8,128)(2,1)} %broadcast_in_dim.28), calls=%async_computation | async-start | bytes 524288 | tf_op jit(solution)/shard_map/all_to_all | solution.py:407
  23.8 166.9 %copy-start.19 = (s32[4]{0:T(128)}, s32[4]{0:T(128)S(1)}, u32[]{:S(2)}) copy-start(s32[4]{0:T(128)S(1)} %pad_add_fusion.where_ref) | copy-start | bytes 52
  32.3 67.8 %all-to-all-start.1 = ((bf16[8,320,512]{2,1,0:T(8,128)(2,1)}), bf16[8,320,512]{2,1,0:T(8,128)(2,1)}, u32[]{:S(2)}, u32[]{:S(2)}) async-start(bf16[8,320,512]{2,1,0:T(8,128)(2,1)} %bitcast.29), calls=%async_computation.1 | async-start | bytes 5242880 | tf_op jit(solution)/shard_map/all_to_all | solution.py:479
  37.4 8.8 %collective-permute-start.3 = (bf16[128,512]{1,0:T(8,128)(2,1)S(1)}, bf16[128,512]{1,0:T(8,128)(2,1)S(1)}, u32[]{:S(2)}, u32[]{:S(2)}) collective-permute-start(bf16[128,512]{1,0:T(8,128)(2,1)S(1)} %get-tuple-element.36), channel_id=1, source_target_pairs={{0,16},{2,18},{4,20},{6,22},{8,24},{10,26},{12,28},{14,30},{16,32}... | collective-permute-start | bytes 393224 | tf_op jit(solution)/shard_map/ppermute | solution.py:418
  38.7 8.6 %collective-permute-start.4 = (bf16[128,512]{1,0:T(8,128)(2,1)S(1)}, bf16[128,512]{1,0:T(8,128)(2,1)S(1)}, u32[]{:S(2)}, u32[]{:S(2)}) collective-permute-start(bf16[128,512]{1,0:T(8,128)(2,1)S(1)} %get-tuple-element.36), channel_id=1, source_target_pairs={{0,32},{2,34},{4,36},{6,38},{8,40},{10,42},{12,44},{14,46},{16,48}... | collective-permute-start | bytes 393224 | tf_op jit(solution)/shard_map/ppermute | solution.py:418
  41.2 6.1 %collective-permute-start.5 = (bf16[128,512]{1,0:T(8,128)(2,1)S(1)}, bf16[128,512]{1,0:T(8,128)(2,1)S(1)}, u32[]{:S(2)}, u32[]{:S(2)}) collective-permute-start(bf16[128,512]{1,0:T(8,128)(2,1)S(1)} %get-tuple-element.36), channel_id=1, source_target_pairs={{0,48},{2,50},{4,52},{6,54},{8,56},{10,58},{12,60},{14,62},{16,0},... | collective-permute-start | bytes 393224 | tf_op jit(solution)/shard_map/ppermute | solution.py:418
  42.3 5.4 %collective-permute-start.6 = (bf16[128,512]{1,0:T(8,128)(2,1)S(1)}, bf16[128,512]{1,0:T(8,128)(2,1)S(1)}, u32[]{:S(2)}, u32[]{:S(2)}) collective-permute-start(bf16[128,512]{1,0:T(8,128)(2,1)S(1)} %get-tuple-element.40), channel_id=1, source_target_pairs={{0,4},{2,6},{4,8},{6,10},{8,12},{10,14},{12,0},{14,2},{16,20},{18,... | collective-permute-start | bytes 393224 | tf_op jit(solution)/shard_map/ppermute | solution.py:418
  43.6 6.8 %collective-permute-start.7 = (bf16[128,512]{1,0:T(8,128)(2,1)S(1)}, bf16[128,512]{1,0:T(8,128)(2,1)S(1)}, u32[]{:S(2)}, u32[]{:S(2)}) collective-permute-start(bf16[128,512]{1,0:T(8,128)(2,1)S(1)} %get-tuple-element.40), channel_id=1, source_target_pairs={{0,8},{2,10},{4,12},{6,14},{8,0},{10,2},{12,4},{14,6},{16,24},{18,... | collective-permute-start | bytes 393224 | tf_op jit(solution)/shard_map/ppermute | solution.py:418
  46.3 4.2 %collective-permute-start.8 = (bf16[128,512]{1,0:T(8,128)(2,1)S(1)}, bf16[128,512]{1,0:T(8,128)(2,1)S(1)}, u32[]{:S(2)}, u32[]{:S(2)}) collective-permute-start(bf16[128,512]{1,0:T(8,128)(2,1)S(1)} %get-tuple-element.40), channel_id=1, source_target_pairs={{0,12},{2,14},{4,0},{6,2},{8,4},{10,6},{12,8},{14,10},{16,28},{18,... | collective-permute-start | bytes 393224 | tf_op jit(solution)/shard_map/ppermute | solution.py:418
  50.5 11.6 %collective-permute-start.10 = (bf16[512,512]{1,0:T(8,128)(2,1)S(1)}, bf16[512,512]{1,0:T(8,128)(2,1)S(1)}, u32[]{:S(2)}, u32[]{:S(2)}) collective-permute-start(bf16[512,512]{1,0:T(8,128)(2,1)S(1)} %constant_dynamic-update-slice_fusion.4.refs_2_), channel_id=1, source_target_pairs={{0,16},{2,18},{4,20},{6,22},{8,24},{10,26},{12,28},{14,30},{16,32}... | collective-permute-start | bytes 1572872 | tf_op jit(solution)/shard_map/ppermute | solution.py:418
  50.9 20.4 %collective-permute-start.12 = (bf16[512,512]{1,0:T(8,128)(2,1)S(1)}, bf16[512,512]{1,0:T(8,128)(2,1)S(1)}, u32[]{:S(2)}, u32[]{:S(2)}) collective-permute-start(bf16[512,512]{1,0:T(8,128)(2,1)S(1)} %constant_dynamic-update-slice_fusion.4.refs_2_), channel_id=1, source_target_pairs={{0,32},{2,34},{4,36},{6,38},{8,40},{10,42},{12,44},{14,46},{16,48}... | collective-permute-start | bytes 1572872 | tf_op jit(solution)/shard_map/ppermute | solution.py:418
  51.9 24.3 %collective-permute-start.14 = (bf16[512,512]{1,0:T(8,128)(2,1)S(1)}, bf16[512,512]{1,0:T(8,128)(2,1)S(1)}, u32[]{:S(2)}, u32[]{:S(2)}) collective-permute-start(bf16[512,512]{1,0:T(8,128)(2,1)S(1)} %constant_dynamic-update-slice_fusion.4.refs_2_), channel_id=1, source_target_pairs={{0,48},{2,50},{4,52},{6,54},{8,56},{10,58},{12,60},{14,62},{16,0},... | collective-permute-start | bytes 1572872 | tf_op jit(solution)/shard_map/ppermute | solution.py:418
  53.5 22.6 %collective-permute-start.11 = (bf16[512,512]{1,0:T(8,128)(2,1)S(1)}, bf16[512,512]{1,0:T(8,128)(2,1)S(1)}, u32[]{:S(2)}, u32[]{:S(2)}) collective-permute-start(bf16[512,512]{1,0:T(8,128)(2,1)S(1)} %constant_dynamic-update-slice_fusion.refs_0_), channel_id=1, source_target_pairs={{0,8},{2,10},{4,12},{6,14},{8,0},{10,2},{12,4},{14,6},{16,24},{18,... | collective-permute-start | bytes 1572872 | tf_op jit(solution)/shard_map/ppermute | solution.py:418
  55.8 23.0 %collective-permute-start.13 = (bf16[512,512]{1,0:T(8,128)(2,1)S(1)}, bf16[512,512]{1,0:T(8,128)(2,1)S(1)}, u32[]{:S(2)}, u32[]{:S(2)}) collective-permute-start(bf16[512,512]{1,0:T(8,128)(2,1)S(1)} %constant_dynamic-update-slice_fusion.refs_0_), channel_id=1, source_target_pairs={{0,12},{2,14},{4,0},{6,2},{8,4},{10,6},{12,8},{14,10},{16,28},{18,... | collective-permute-start | bytes 1572872 | tf_op jit(solution)/shard_map/ppermute | solution.py:418
  62.1 16.7 %collective-permute-start.9 = (bf16[512,512]{1,0:T(8,128)(2,1)S(1)}, bf16[512,512]{1,0:T(8,128)(2,1)S(1)}, u32[]{:S(2)}, u32[]{:S(2)}) collective-permute-start(bf16[512,512]{1,0:T(8,128)(2,1)S(1)} %constant_dynamic-update-slice_fusion.refs_0_), channel_id=1, source_target_pairs={{0,4},{2,6},{4,8},{6,10},{8,12},{10,14},{12,0},{14,2},{16,20},{18,... | collective-permute-start | bytes 1572872 | tf_op jit(solution)/shard_map/ppermute | solution.py:418
  78.8 10.5 %collective-permute-start.15 = (bf16[512,512]{1,0:T(8,128)(2,1)S(1)}, bf16[512,512]{1,0:T(8,128)(2,1)S(1)}, u32[]{:S(2)}, u32[]{:S(2)}) collective-permute-start(bf16[512,512]{1,0:T(8,128)(2,1)S(1)} %constant_dynamic-update-slice_fusion.refs_0_), channel_id=1, source_target_pairs={{0,2},{2,0},{4,6},{6,4},{8,10},{10,8},{12,14},{14,12},{16,18},{18,... | collective-permute-start | bytes 1572872 | tf_op jit(solution)/shard_map/ppermute | solution.py:418
  87.8 2.3 %collective-permute-start.16 = (bf16[512,512]{1,0:T(8,128)(2,1)S(1)}, bf16[512,512]{1,0:T(8,128)(2,1)S(1)}, u32[]{:S(2)}, u32[]{:S(2)}) collective-permute-start(bf16[512,512]{1,0:T(8,128)(2,1)S(1)} %constant_dynamic-update-slice_fusion.4.refs_2_), channel_id=1, source_target_pairs={{0,2},{2,0},{4,6},{6,4},{8,10},{10,8},{12,14},{14,12},{16,18},{18,... | collective-permute-start | bytes 1572872 | tf_op jit(solution)/shard_map/ppermute | solution.py:418
  87.8 3.0 %collective-permute-start.17 = (bf16[512,512]{1,0:T(8,128)(2,1)S(1)}, bf16[512,512]{1,0:T(8,128)(2,1)S(1)}, u32[]{:S(2)}, u32[]{:S(2)}) collective-permute-start(bf16[512,512]{1,0:T(8,128)(2,1)S(1)} %collective-permute-done.9.refs_4_), channel_id=1, source_target_pairs={{0,2},{2,0},{4,6},{6,4},{8,10},{10,8},{12,14},{14,12},{16,18},{18,... | collective-permute-start | bytes 1572872 | tf_op jit(solution)/shard_map/ppermute | solution.py:418
  88.3 3.3 %collective-permute-start.18 = (bf16[512,512]{1,0:T(8,128)(2,1)S(1)}, bf16[512,512]{1,0:T(8,128)(2,1)S(1)}, u32[]{:S(2)}, u32[]{:S(2)}) collective-permute-start(bf16[512,512]{1,0:T(8,128)(2,1)S(1)} %collective-permute-done.10.refs_6_), channel_id=1, source_target_pairs={{0,2},{2,0},{4,6},{6,4},{8,10},{10,8},{12,14},{14,12},{16,18},{18,... | collective-permute-start | bytes 1572872 | tf_op jit(solution)/shard_map/ppermute | solution.py:418
  88.3 4.0 %collective-permute-start.19 = (bf16[512,512]{1,0:T(8,128)(2,1)S(1)}, bf16[512,512]{1,0:T(8,128)(2,1)S(1)}, u32[]{:S(2)}, u32[]{:S(2)}) collective-permute-start(bf16[512,512]{1,0:T(8,128)(2,1)S(1)} %collective-permute-done.11.refs_8_), channel_id=1, source_target_pairs={{0,2},{2,0},{4,6},{6,4},{8,10},{10,8},{12,14},{14,12},{16,18},{18,... | collective-permute-start | bytes 1572872 | tf_op jit(solution)/shard_map/ppermute | solution.py:418
  89.3 3.7 %collective-permute-start.20 = (bf16[512,512]{1,0:T(8,128)(2,1)S(1)}, bf16[512,512]{1,0:T(8,128)(2,1)S(1)}, u32[]{:S(2)}, u32[]{:S(2)}) collective-permute-start(bf16[512,512]{1,0:T(8,128)(2,1)S(1)} %collective-permute-done.12.refs_10_), channel_id=1, source_target_pairs={{0,2},{2,0},{4,6},{6,4},{8,10},{10,8},{12,14},{14,12},{16,18},{18,... | collective-permute-start | bytes 1572872 | tf_op jit(solution)/shard_map/ppermute | solution.py:418
  90.1 3.7 %collective-permute-start.21 = (bf16[512,512]{1,0:T(8,128)(2,1)S(1)}, bf16[512,512]{1,0:T(8,128)(2,1)S(1)}, u32[]{:S(2)}, u32[]{:S(2)}) collective-permute-start(bf16[512,512]{1,0:T(8,128)(2,1)S(1)} %collective-permute-done.13.refs_12_), channel_id=1, source_target_pairs={{0,2},{2,0},{4,6},{6,4},{8,10},{10,8},{12,14},{14,12},{16,18},{18,... | collective-permute-start | bytes 1572872 | tf_op jit(solution)/shard_map/ppermute | solution.py:418
  90.8 3.7 %collective-permute-start.22 = (bf16[512,512]{1,0:T(8,128)(2,1)S(1)}, bf16[512,512]{1,0:T(8,128)(2,1)S(1)}, u32[]{:S(2)}, u32[]{:S(2)}) collective-permute-start(bf16[512,512]{1,0:T(8,128)(2,1)S(1)} %collective-permute-done.14.refs_14_), channel_id=1, source_target_pairs={{0,2},{2,0},{4,6},{6,4},{8,10},{10,8},{12,14},{14,12},{16,18},{18,... | collective-permute-start | bytes 1572872 | tf_op jit(solution)/shard_map/ppermute | solution.py:418
  100.1 3.4 %copy-start.1 = (bf16[4096,1024]{1,0:T(8,128)(2,1)S(1)}, bf16[4096,1024]{1,0:T(8,128)(2,1)}, u32[]{:S(2)}) copy-start(bf16[4096,1024]{1,0:T(8,128)(2,1)} %shard_map.85.features_ref.refs_16_) | copy-start | bytes 25165828
  103.5 13.1 %copy-start.20 = (s32[32]{0:T(128)S(1)}, s32[32]{0:T(128)}, u32[]{:S(2)}) copy-start(s32[32]{0:T(128)} %param.9) | copy-start | bytes 388
  109.3 16.2 %all-to-all-start.2 = ((f32[16,24,128]{2,1,0:T(8,128)}), f32[16,24,128]{2,1,0:T(8,128)S(1)}, u32[]{:S(2)}, u32[]{:S(2)}) async-start(f32[16,24,128]{2,1,0:T(8,128)} %get-tuple-element.53), calls=%async_computation.2 | async-start | bytes 393216 | tf_op jit(solution)/shard_map/all_to_all | solution.py:487
  126.3 10.4 %all-to-all-start.3 = ((f32[16,24,128]{2,1,0:T(8,128)}), f32[16,24,128]{2,1,0:T(8,128)S(1)}, u32[]{:S(2)}, u32[]{:S(2)}) async-start(f32[16,24,128]{2,1,0:T(8,128)} %broadcast_in_dim.29), calls=%async_computation.3 | async-start | bytes 393216 | tf_op jit(solution)/shard_map/all_to_all | solution.py:489
  137.9 46.3 %copy-start.9 = (bf16[160,1024]{1,0:T(8,128)(2,1)}, bf16[160,1024]{1,0:T(8,128)(2,1)S(1)}, u32[]{:S(2)}) copy-start(bf16[160,1024]{1,0:T(8,128)(2,1)S(1)} %get-tuple-element.55.refs_0_) | copy-start | bytes 983044
  137.9 46.3 %copy-start.10 = (bf16[160,1024]{1,0:T(8,128)(2,1)}, bf16[160,1024]{1,0:T(8,128)(2,1)S(1)}, u32[]{:S(2)}) copy-start(bf16[160,1024]{1,0:T(8,128)(2,1)S(1)} %get-tuple-element.56.refs_1_) | copy-start | bytes 983044
  137.9 7.5 %collective-permute-start.26 = (bf16[160,1024]{1,0:T(8,128)(2,1)S(1)}, bf16[160,1024]{1,0:T(8,128)(2,1)S(1)}, u32[]{:S(2)}, u32[]{:S(2)}) collective-permute-start(bf16[160,1024]{1,0:T(8,128)(2,1)S(1)} %get-tuple-element.55.refs_0_), channel_id=1, source_target_pairs={{0,193},{1,0},{64,1},{65,64},{128,65},{129,128},{192,129},{193,192... | collective-permute-start | bytes 983048 | tf_op jit(solution)/shard_map/ppermute | solution.py:383
  140.1 8.7 %collective-permute-start.29 = (bf16[160,1024]{1,0:T(8,128)(2,1)S(1)}, bf16[160,1024]{1,0:T(8,128)(2,1)S(1)}, u32[]{:S(2)}, u32[]{:S(2)}) collective-permute-start(bf16[160,1024]{1,0:T(8,128)(2,1)S(1)} %get-tuple-element.56.refs_1_), channel_id=1, source_target_pairs={{0,1},{1,64},{64,65},{65,128},{128,129},{129,192},{192,193},{193,0... | collective-permute-start | bytes 983048 | tf_op jit(solution)/shard_map/ppermute | solution.py:383
  140.1 15.5 %collective-permute-start.23 = (bf16[160,1024]{1,0:T(8,128)(2,1)S(1)}, bf16[160,1024]{1,0:T(8,128)(2,1)S(1)}, u32[]{:S(2)}, u32[]{:S(2)}) collective-permute-start(bf16[160,1024]{1,0:T(8,128)(2,1)S(1)} %get-tuple-element.55.refs_0_), channel_id=1, source_target_pairs={{0,1},{1,64},{64,65},{65,128},{128,129},{129,192},{192,193},{193,0... | collective-permute-start | bytes 983048 | tf_op jit(solution)/shard_map/ppermute | solution.py:383
  140.8 14.8 %collective-permute-start.32 = (bf16[160,1024]{1,0:T(8,128)(2,1)S(1)}, bf16[160,1024]{1,0:T(8,128)(2,1)S(1)}, u32[]{:S(2)}, u32[]{:S(2)}) collective-permute-start(bf16[160,1024]{1,0:T(8,128)(2,1)S(1)} %get-tuple-element.56.refs_1_), channel_id=1, source_target_pairs={{0,193},{1,0},{64,1},{65,64},{128,65},{129,128},{192,129},{193,192... | collective-permute-start | bytes 983048 | tf_op jit(solution)/shard_map/ppermute | solution.py:383
  145.4 38.8 %copy-start.11 = (bf16[160,1024]{1,0:T(8,128)(2,1)}, bf16[160,1024]{1,0:T(8,128)(2,1)S(1)}, u32[]{:S(2)}) copy-start(bf16[160,1024]{1,0:T(8,128)(2,1)S(1)} %collective-permute-done.26.refs_3_) | copy-start | bytes 983044
  145.4 14.0 %collective-permute-start.27 = (bf16[160,1024]{1,0:T(8,128)(2,1)S(1)}, bf16[160,1024]{1,0:T(8,128)(2,1)S(1)}, u32[]{:S(2)}, u32[]{:S(2)}) collective-permute-start(bf16[160,1024]{1,0:T(8,128)(2,1)S(1)} %collective-permute-done.26.refs_3_), channel_id=1, source_target_pairs={{0,193},{1,0},{64,1},{65,64},{128,65},{129,128},{192,129},{193,192... | collective-permute-start | bytes 983048 | tf_op jit(solution)/shard_map/ppermute | solution.py:383
  148.8 35.3 %copy-start.12 = (bf16[160,1024]{1,0:T(8,128)(2,1)}, bf16[160,1024]{1,0:T(8,128)(2,1)S(1)}, u32[]{:S(2)}) copy-start(bf16[160,1024]{1,0:T(8,128)(2,1)S(1)} %collective-permute-done.29.refs_4_) | copy-start | bytes 983044
  148.8 14.0 %collective-permute-start.30 = (bf16[160,1024]{1,0:T(8,128)(2,1)S(1)}, bf16[160,1024]{1,0:T(8,128)(2,1)S(1)}, u32[]{:S(2)}, u32[]{:S(2)}) collective-permute-start(bf16[160,1024]{1,0:T(8,128)(2,1)S(1)} %collective-permute-done.29.refs_4_), channel_id=1, source_target_pairs={{0,1},{1,64},{64,65},{65,128},{128,129},{129,192},{192,193},{193,0... | collective-permute-start | bytes 983048 | tf_op jit(solution)/shard_map/ppermute | solution.py:383
  155.6 28.6 %copy-start.13 = (bf16[160,1024]{1,0:T(8,128)(2,1)}, bf16[160,1024]{1,0:T(8,128)(2,1)S(1)}, u32[]{:S(2)}) copy-start(bf16[160,1024]{1,0:T(8,128)(2,1)S(1)} %collective-permute-done.23.refs_2_) | copy-start | bytes 983044
  155.6 14.0 %collective-permute-start.24 = (bf16[160,1024]{1,0:T(8,128)(2,1)S(1)}, bf16[160,1024]{1,0:T(8,128)(2,1)S(1)}, u32[]{:S(2)}, u32[]{:S(2)}) collective-permute-start(bf16[160,1024]{1,0:T(8,128)(2,1)S(1)} %collective-permute-done.23.refs_2_), channel_id=1, source_target_pairs={{0,1},{1,64},{64,65},{65,128},{128,129},{129,192},{192,193},{193,0... | collective-permute-start | bytes 983048 | tf_op jit(solution)/shard_map/ppermute | solution.py:383
  155.6 28.6 %copy-start.14 = (bf16[160,1024]{1,0:T(8,128)(2,1)}, bf16[160,1024]{1,0:T(8,128)(2,1)S(1)}, u32[]{:S(2)}) copy-start(bf16[160,1024]{1,0:T(8,128)(2,1)S(1)} %collective-permute-done.32.refs_5_) | copy-start | bytes 983044
  155.6 14.0 %collective-permute-start.33 = (bf16[160,1024]{1,0:T(8,128)(2,1)S(1)}, bf16[160,1024]{1,0:T(8,128)(2,1)S(1)}, u32[]{:S(2)}, u32[]{:S(2)}) collective-permute-start(bf16[160,1024]{1,0:T(8,128)(2,1)S(1)} %collective-permute-done.32.refs_5_), channel_id=1, source_target_pairs={{0,193},{1,0},{64,1},{65,64},{128,65},{129,128},{192,129},{193,192... | collective-permute-start | bytes 983048 | tf_op jit(solution)/shard_map/ppermute | solution.py:383
  159.5 24.8 %copy-start.15 = (bf16[160,1024]{1,0:T(8,128)(2,1)}, bf16[160,1024]{1,0:T(8,128)(2,1)S(1)}, u32[]{:S(2)}) copy-start(bf16[160,1024]{1,0:T(8,128)(2,1)S(1)} %collective-permute-done.27.refs_7_) | copy-start | bytes 983044
  159.5 13.6 %collective-permute-start.28 = (bf16[160,1024]{1,0:T(8,128)(2,1)S(1)}, bf16[160,1024]{1,0:T(8,128)(2,1)S(1)}, u32[]{:S(2)}, u32[]{:S(2)}) collective-permute-start(bf16[160,1024]{1,0:T(8,128)(2,1)S(1)} %collective-permute-done.27.refs_7_), channel_id=1, source_target_pairs={{0,193},{1,0},{64,1},{65,64},{128,65},{129,128},{192,129},{193,192... | collective-permute-start | bytes 983048 | tf_op jit(solution)/shard_map/ppermute | solution.py:383
  162.9 21.3 %copy-start.16 = (bf16[160,1024]{1,0:T(8,128)(2,1)}, bf16[160,1024]{1,0:T(8,128)(2,1)S(1)}, u32[]{:S(2)}) copy-start(bf16[160,1024]{1,0:T(8,128)(2,1)S(1)} %collective-permute-done.30.refs_8_) | copy-start | bytes 983044
  162.9 13.8 %collective-permute-start.31 = (bf16[160,1024]{1,0:T(8,128)(2,1)S(1)}, bf16[160,1024]{1,0:T(8,128)(2,1)S(1)}, u32[]{:S(2)}, u32[]{:S(2)}) collective-permute-start(bf16[160,1024]{1,0:T(8,128)(2,1)S(1)} %collective-permute-done.30.refs_8_), channel_id=1, source_target_pairs={{0,1},{1,64},{64,65},{65,128},{128,129},{129,192},{192,193},{193,0... | collective-permute-start | bytes 983048 | tf_op jit(solution)/shard_map/ppermute | solution.py:383
  169.6 14.6 %copy-start.17 = (bf16[160,1024]{1,0:T(8,128)(2,1)}, bf16[160,1024]{1,0:T(8,128)(2,1)S(1)}, u32[]{:S(2)}) copy-start(bf16[160,1024]{1,0:T(8,128)(2,1)S(1)} %collective-permute-done.24.refs_6_) | copy-start | bytes 983044
  169.6 14.6 %collective-permute-start.25 = (bf16[160,1024]{1,0:T(8,128)(2,1)S(1)}, bf16[160,1024]{1,0:T(8,128)(2,1)S(1)}, u32[]{:S(2)}, u32[]{:S(2)}) collective-permute-start(bf16[160,1024]{1,0:T(8,128)(2,1)S(1)} %collective-permute-done.24.refs_6_), channel_id=1, source_target_pairs={{0,1},{1,64},{64,65},{65,128},{128,129},{129,192},{192,193},{193,0... | collective-permute-start | bytes 983048 | tf_op jit(solution)/shard_map/ppermute | solution.py:383
  169.6 14.6 %copy-start.18 = (bf16[160,1024]{1,0:T(8,128)(2,1)}, bf16[160,1024]{1,0:T(8,128)(2,1)S(1)}, u32[]{:S(2)}) copy-start(bf16[160,1024]{1,0:T(8,128)(2,1)S(1)} %collective-permute-done.33.refs_9_) | copy-start | bytes 983044
  169.6 14.6 %collective-permute-start.34 = (bf16[160,1024]{1,0:T(8,128)(2,1)S(1)}, bf16[160,1024]{1,0:T(8,128)(2,1)S(1)}, u32[]{:S(2)}, u32[]{:S(2)}) collective-permute-start(bf16[160,1024]{1,0:T(8,128)(2,1)S(1)} %collective-permute-done.33.refs_9_), channel_id=1, source_target_pairs={{0,193},{1,0},{64,1},{65,64},{128,65},{129,128},{192,129},{193,192... | collective-permute-start | bytes 983048 | tf_op jit(solution)/shard_map/ppermute | solution.py:383
  173.1 17.6 %copy-start.3 = (bf16[160,1024]{1,0:T(8,128)(2,1)}, bf16[160,1024]{1,0:T(8,128)(2,1)S(1)}, u32[]{:S(2)}) copy-start(bf16[160,1024]{1,0:T(8,128)(2,1)S(1)} %collective-permute-done.28.refs_1_.refs_11_) | copy-start | bytes 983044
  173.1 14.0 %collective-permute-start.35 = (bf16[160,1024]{1,0:T(8,128)(2,1)S(1)}, bf16[160,1024]{1,0:T(8,128)(2,1)S(1)}, u32[]{:S(2)}, u32[]{:S(2)}) collective-permute-start(bf16[160,1024]{1,0:T(8,128)(2,1)S(1)} %collective-permute-done.28.refs_1_.refs_11_), channel_id=1, source_target_pairs={{0,193},{1,0},{64,1},{65,64},{128,65},{129,128},{192,129},{193,192... | collective-permute-start | bytes 983048 | tf_op jit(solution)/shard_map/ppermute | solution.py:383
  176.6 14.1 %copy-start.4 = (bf16[160,1024]{1,0:T(8,128)(2,1)}, bf16[160,1024]{1,0:T(8,128)(2,1)S(1)}, u32[]{:S(2)}) copy-start(bf16[160,1024]{1,0:T(8,128)(2,1)S(1)} %collective-permute-done.31.refs_2_.refs_12_) | copy-start | bytes 983044
  176.6 14.0 %collective-permute-start.36 = (bf16[160,1024]{1,0:T(8,128)(2,1)S(1)}, bf16[160,1024]{1,0:T(8,128)(2,1)S(1)}, u32[]{:S(2)}, u32[]{:S(2)}) collective-permute-start(bf16[160,1024]{1,0:T(8,128)(2,1)S(1)} %collective-permute-done.31.refs_2_.refs_12_), channel_id=1, source_target_pairs={{0,1},{1,64},{64,65},{65,128},{128,129},{129,192},{192,193},{193,0... | collective-permute-start | bytes 983048 | tf_op jit(solution)/shard_map/ppermute | solution.py:383
  176.7 1.9 copy-start.2
  184.3 9.7 %copy-start.5 = (bf16[160,1024]{1,0:T(8,128)(2,1)}, bf16[160,1024]{1,0:T(8,128)(2,1)S(1)}, u32[]{:S(2)}) copy-start(bf16[160,1024]{1,0:T(8,128)(2,1)S(1)} %collective-permute-done.25.refs_0_.refs_10_) | copy-start | bytes 983044
  184.3 9.7 %copy-start.6 = (bf16[160,1024]{1,0:T(8,128)(2,1)}, bf16[160,1024]{1,0:T(8,128)(2,1)S(1)}, u32[]{:S(2)}) copy-start(bf16[160,1024]{1,0:T(8,128)(2,1)S(1)} %collective-permute-done.34.refs_3_.refs_13_) | copy-start | bytes 983044
  187.1 6.9 %copy-start.7 = (bf16[160,1024]{1,0:T(8,128)(2,1)}, bf16[160,1024]{1,0:T(8,128)(2,1)S(1)}, u32[]{:S(2)}) copy-start(bf16[160,1024]{1,0:T(8,128)(2,1)S(1)} %collective-permute-done.35.refs_4_.refs_14_) | copy-start | bytes 983044
  190.7 3.3 %copy-start.8 = (bf16[160,1024]{1,0:T(8,128)(2,1)}, bf16[160,1024]{1,0:T(8,128)(2,1)S(1)}, u32[]{:S(2)}) copy-start(bf16[160,1024]{1,0:T(8,128)(2,1)S(1)} %collective-permute-done.36.refs_5_.refs_15_) | copy-start | bytes 983044
  194.0 4.5 %collective-permute-start.37 = (bf16[16,32,512]{2,1,0:T(8,128)(2,1)S(1)}, bf16[16,32,512]{2,1,0:T(8,128)(2,1)S(1)}, u32[]{:S(2)}, u32[]{:S(2)}) collective-permute-start(bf16[16,32,512]{2,1,0:T(8,128)(2,1)S(1)} %get-tuple-element.58), channel_id=1, source_target_pairs={{0,2},{2,0},{4,6},{6,4},{8,10},{10,8},{12,14},{14,12},{16,18},{18,... | collective-permute-start | bytes 1572872 | tf_op jit(solution)/shard_map/ppermute | solution.py:495
  199.5 14.3 %all-to-all-start.4 = ((bf16[16,32,512]{2,1,0:T(8,128)(2,1)}), bf16[16,32,512]{2,1,0:T(8,128)(2,1)S(1)}, u32[]{:S(2)}, u32[]{:S(2)}) async-start(bf16[16,32,512]{2,1,0:T(8,128)(2,1)} %add_convert_fusion), calls=%async_computation.4 | async-start | bytes 1048576 | tf_op jit(solution)/shard_map/all_to_all | solution.py:497

commit v6 on v5

--- a/solution.py
+++ b/solution.py
@@ -490,8 +490,8 @@
     low, high, divergence = logit_grads(where, stats, weights, student, teachers)
     blocks, hops = ring_gather((low, high), ring)
 
-    part = early_features(where, blocks[:-6], hops[:-6], head)
-    keep, give = late_features(where, blocks[-6:], hops[-6:], head, part, ring, rows // vocs)
+    part = early_features(where, blocks[:-2], hops[:-2], head)
+    keep, give = late_features(where, blocks[-2:], hops[-2:], head, part, ring, rows // vocs)
     given = lax.ppermute(give, "voc", cores)
     sums, where = lax.optimization_barrier(((keep + given.astype(F32)).astype(BF16), where))
     sums = lax.all_to_all(sums, "voc", 0, 0, axis_index_groups=groups)

time: 215 us -> 218 us (1.014)
    ppermute x1, starting transfers between devices: 2.98 us -> 5.48 us  [on_device(): given = lax.ppermute(give, 'voc', cores)]
  transfers between devices with their start and end apart: 43 -> 43, of which waited for: 29 -> 28; matrix products, arithmetic and copies ran while one was open for 3% -> 3% of each run, Pallas kernels for 10% -> 10%
where the time goes in v6:
time: 218 us; the launch traced here: 217 us
  starting transfers between devices  87.8 us (40%)
  waiting for transfers between devices  81.2 us (37%)
  Pallas kernels  30.1 us (14%)
  local copies, waits for them, and re-layouts  12.9 us (6%)
  other arithmetic  2.82 us (1%)
    ppermute x20, waiting for transfers between devices, shift(): return lax.ppermute(values, 'voc', pairs)  28.8 us
    ppermute x20, starting transfers between devices, shift(): return lax.ppermute(values, 'voc', pairs)  28.2 us
    ppermute x14, waiting for transfers between devices, ring_shift(): lax.ppermute(values, RING, [(i, (i + step) % size) for i in range(size)])  25.8 us
    ppermute x14, starting transfers between devices, ring_shift(): lax.ppermute(values, RING, [(i, (i + step) % size) for i in range(size)])  19.9 us
    ppermute x3, starting transfers between devices, on_device(): lax.ppermute(part, 'tok', [(i, (i + shift) % toks) for i in range(toks)])  11.4 us
    pallas_call x1, Pallas kernels, head_parts(): pl.pallas_call(functools.partial(head_kernel, hops), grid=(vocab // tile,...  8.83 us
    all_to_all x1, waiting for transfers between devices, on_device(): lax.all_to_all(stats, ('tok', 'voc', 'sub'), 0, 0, axis_index_groups=mixed)  8.65 us
    all_to_all x1, starting transfers between devices, on_device(): lax.all_to_all(stats, ('tok', 'voc', 'sub'), 0, 0, axis_index_groups=mixed)  7.32 us
  transfers between devices with their start and end apart: 43, of which 28 were waited for; matrix products, arithmetic and copies ran while one was open for 3% of the time, Pallas kernels for 10%

profile of v6, /device:TPU:1, one launch (start us, length us, event | category | flops | bytes accessed | tf_op | source)
XLA Modules:
  0.0 216.7 jit_solution(5237401997488378493)
XLA Ops:
  0.7 0.8 broadcast_subtract_fusion
  2.9 3.9 %collective-permute-start = (bf16[320,256]{1,0:T(8,128)(2,1)S(1)}, bf16[320,256]{1,0:T(8,128)(2,1)S(1)}, u32[]{:S(2)}, u32[]{:S(2)}) collective-permute-start(bf16[320,256]{1,0:T(8,128)(2,1)S(1)} %get-tuple-element.70), channel_id=1, source_target_pairs={{0,64},{64,128},{128,192},{192,0},{1,65},{65,129},{129,193},{193,1... | collective-permute-start | bytes 491528 | tf_op jit(solution)/shard_map/ppermute | solution.py:467
  6.7 5.1 %collective-permute-start.1 = (bf16[320,256]{1,0:T(8,128)(2,1)S(1)}, bf16[320,256]{1,0:T(8,128)(2,1)S(1)}, u32[]{:S(2)}, u32[]{:S(2)}) collective-permute-start(bf16[320,256]{1,0:T(8,128)(2,1)S(1)} %get-tuple-element.69), channel_id=1, source_target_pairs={{0,128},{64,192},{128,0},{192,64},{1,129},{65,193},{129,1},{193,65... | collective-permute-start | bytes 491528 | tf_op jit(solution)/shard_map/ppermute | solution.py:467
  11.9 2.4 %collective-permute-start.2 = (bf16[320,256]{1,0:T(8,128)(2,1)S(1)}, bf16[320,256]{1,0:T(8,128)(2,1)S(1)}, u32[]{:S(2)}, u32[]{:S(2)}) collective-permute-start(bf16[320,256]{1,0:T(8,128)(2,1)S(1)} %get-tuple-element.68), channel_id=1, source_target_pairs={{0,192},{64,0},{128,64},{192,128},{1,193},{65,1},{129,65},{193,129... | collective-permute-start | bytes 491528 | tf_op jit(solution)/shard_map/ppermute | solution.py:467
  14.2 0.8 constant_dynamic-slice_fusion
  15.1 0.7 broadcast_in_dim.28
  15.9 3.4 %all-to-all-start = ((bf16[8,128,128]{1,2,0:T(8,128)(2,1)}), bf16[8,128,128]{1,2,0:T(8,128)(2,1)S(1)}, u32[]{:S(2)}, u32[]{:S(2)}) async-start(bf16[8,128,128]{1,2,0:T(8,128)(2,1)} %broadcast_in_dim.28), calls=%async_computation | async-start | bytes 524288 | tf_op jit(solution)/shard_map/all_to_all | solution.py:407
  19.3 4.4 %copy.22 = bf16[2560,512]{1,0:T(8,128)(2,1)} copy(bf16[2560,512]{0,1:T(8,128)(2,1)} %bitcast.28) | data formatting | bytes 5242880 | tf_op jit(solution)/shard_map/transpose | solution.py:473
  23.8 5.1 %collective-permute-done.2.refs_3_ = bf16[320,256]{1,0:T(8,128)(2,1)S(1)} collective-permute-done((bf16[320,256]{1,0:T(8,128)(2,1)S(1)}, bf16[320,256]{1,0:T(8,128)(2,1)S(1)}, u32[]{:S(2)}, u32[]{:S(2)}) %collective-permute-start.2) | collective-permute-done | bytes 163872 | tf_op jit(solution)/shard_map/ppermute | solution.py:467
  29.5 2.8 %all-to-all-done = bf16[8,128,128]{1,2,0:T(8,128)(2,1)S(1)} async-done(((bf16[8,128,128]{1,2,0:T(8,128)(2,1)}), bf16[8,128,128]{1,2,0:T(8,128)(2,1)S(1)}, u32[]{:S(2)}, u32[]{:S(2)}) %all-to-all-start) | async-done | bytes 262176 | tf_op jit(solution)/shard_map/all_to_all | solution.py:407
  32.3 5.1 %all-to-all-start.1 = ((bf16[8,320,512]{2,1,0:T(8,128)(2,1)}), bf16[8,320,512]{2,1,0:T(8,128)(2,1)}, u32[]{:S(2)}, u32[]{:S(2)}) async-start(bf16[8,320,512]{2,1,0:T(8,128)(2,1)} %bitcast.29), calls=%async_computation.1 | async-start | bytes 5242880 | tf_op jit(solution)/shard_map/all_to_all | solution.py:479
  37.4 1.3 collective-permute-start.3
  38.7 2.5 %collective-permute-start.4 = (bf16[128,512]{1,0:T(8,128)(2,1)S(1)}, bf16[128,512]{1,0:T(8,128)(2,1)S(1)}, u32[]{:S(2)}, u32[]{:S(2)}) collective-permute-start(bf16[128,512]{1,0:T(8,128)(2,1)S(1)} %get-tuple-element.36), channel_id=1, source_target_pairs={{0,32},{2,34},{4,36},{6,38},{8,40},{10,42},{12,44},{14,46},{16,48}... | collective-permute-start | bytes 393224 | tf_op jit(solution)/shard_map/ppermute | solution.py:418
  41.2 1.1 collective-permute-start.5
  42.3 1.3 collective-permute-start.6
  43.6 2.6 %collective-permute-start.7 = (bf16[128,512]{1,0:T(8,128)(2,1)S(1)}, bf16[128,512]{1,0:T(8,128)(2,1)S(1)}, u32[]{:S(2)}, u32[]{:S(2)}) collective-permute-start(bf16[128,512]{1,0:T(8,128)(2,1)S(1)} %get-tuple-element.40), channel_id=1, source_target_pairs={{0,8},{2,10},{4,12},{6,14},{8,0},{10,2},{12,4},{14,6},{16,24},{18,... | collective-permute-start | bytes 393224 | tf_op jit(solution)/shard_map/ppermute | solution.py:418
  46.3 1.1 collective-permute-start.8
  47.7 2.7 %collective-permute-done.7 = bf16[128,512]{1,0:T(8,128)(2,1)S(1)} collective-permute-done((bf16[128,512]{1,0:T(8,128)(2,1)S(1)}, bf16[128,512]{1,0:T(8,128)(2,1)S(1)}, u32[]{:S(2)}, u32[]{:S(2)}) %collective-permute-start.7) | collective-permute-done | bytes 131104 | tf_op jit(solution)/shard_map/ppermute | solution.py:418
  50.9 1.0 collective-permute-start.12
  51.9 1.5 collective-permute-start.14
  53.5 2.3 %collective-permute-start.11 = (bf16[512,512]{1,0:T(8,128)(2,1)S(1)}, bf16[512,512]{1,0:T(8,128)(2,1)S(1)}, u32[]{:S(2)}, u32[]{:S(2)}) collective-permute-start(bf16[512,512]{1,0:T(8,128)(2,1)S(1)} %constant_dynamic-update-slice_fusion.refs_0_), channel_id=1, source_target_pairs={{0,8},{2,10},{4,12},{6,14},{8,0},{10,2},{12,4},{14,6},{16,24},{18,... | collective-permute-start | bytes 1572872 | tf_op jit(solution)/shard_map/ppermute | solution.py:418
  55.8 1.0 collective-permute-start.13
  56.8 5.3 %collective-permute-done.10.refs_6_ = bf16[512,512]{1,0:T(8,128)(2,1)S(1)} collective-permute-done((bf16[512,512]{1,0:T(8,128)(2,1)S(1)}, bf16[512,512]{1,0:T(8,128)(2,1)S(1)}, u32[]{:S(2)}, u32[]{:S(2)}) %collective-permute-start.10) | collective-permute-done | bytes 524320 | tf_op jit(solution)/shard_map/ppermute | solution.py:418
  62.1 1.0 collective-permute-start.9
  63.1 8.2 %collective-permute-done.12.refs_10_ = bf16[512,512]{1,0:T(8,128)(2,1)S(1)} collective-permute-done((bf16[512,512]{1,0:T(8,128)(2,1)S(1)}, bf16[512,512]{1,0:T(8,128)(2,1)S(1)}, u32[]{:S(2)}, u32[]{:S(2)}) %collective-permute-start.12) | collective-permute-done | bytes 524320 | tf_op jit(solution)/shard_map/ppermute | solution.py:418
  71.3 4.8 %collective-permute-done.14.refs_14_ = bf16[512,512]{1,0:T(8,128)(2,1)S(1)} collective-permute-done((bf16[512,512]{1,0:T(8,128)(2,1)S(1)}, bf16[512,512]{1,0:T(8,128)(2,1)S(1)}, u32[]{:S(2)}, u32[]{:S(2)}) %collective-permute-start.14) | collective-permute-done | bytes 524320 | tf_op jit(solution)/shard_map/ppermute | solution.py:418
  76.2 2.7 %collective-permute-done.13.refs_12_ = bf16[512,512]{1,0:T(8,128)(2,1)S(1)} collective-permute-done((bf16[512,512]{1,0:T(8,128)(2,1)S(1)}, bf16[512,512]{1,0:T(8,128)(2,1)S(1)}, u32[]{:S(2)}, u32[]{:S(2)}) %collective-permute-start.13) | collective-permute-done | bytes 524320 | tf_op jit(solution)/shard_map/ppermute | solution.py:418
  78.8 9.0 %collective-permute-start.15 = (bf16[512,512]{1,0:T(8,128)(2,1)S(1)}, bf16[512,512]{1,0:T(8,128)(2,1)S(1)}, u32[]{:S(2)}, u32[]{:S(2)}) collective-permute-start(bf16[512,512]{1,0:T(8,128)(2,1)S(1)} %constant_dynamic-update-slice_fusion.refs_0_), channel_id=1, source_target_pairs={{0,2},{2,0},{4,6},{6,4},{8,10},{10,8},{12,14},{14,12},{16,18},{18,... | collective-permute-start | bytes 1572872 | tf_op jit(solution)/shard_map/ppermute | solution.py:418
  91.6 0.7 collective-permute-done.19.refs_9_
  92.3 0.7 collective-permute-done.20.refs_11_
  93.1 0.7 collective-permute-done.21.refs_13_
  93.8 0.7 collective-permute-done.22.refs_15_
  94.6 5.5 %shard_map.85.features_ref.refs_16_ = bf16[4096,1024]{1,0:T(8,128)(2,1)} custom-call(s32[4]{0:T(128)S(1)} %pad_add_fusion.where_ref, bf16[512,512]{1,0:T(8,128)(2,1)S(1)} %constant_dynamic-update-slice_fusion.refs_0_, bf16[512,512]{1,0:T(8,128)(2,1)S(1)} %collective-permute-done.15.refs_1_, bf16[512,512]{1,0:T(8,128)(2,1)S(1)} %constant_dynamic-update-slice_fusion.4.refs_2_, ...), custom_call_target="tpu_custom_call" | custom-call | tf_op jit(solution)/shard_map/pallas_call | solution.py:103
  100.1 3.4 %copy-done.1 = bf16[4096,1024]{1,0:T(8,128)(2,1)S(1)} copy-done((bf16[4096,1024]{1,0:T(8,128)(2,1)S(1)}, bf16[4096,1024]{1,0:T(8,128)(2,1)}, u32[]{:S(2)}) %copy-start.1) | copy-done | bytes 8388632
  103.5 5.8 %shard_map.86 = (f32[320,1024]{1,0:T(8,128)S(1)}, f32[16,24,128]{2,1,0:T(8,128)}) custom-call(bf16[8,320,512]{2,1,0:T(8,128)(2,1)} %all-to-all-done.1.head_hbm, bf16[4096,1024]{1,0:T(8,128)(2,1)S(1)} %copy-done.1, bf16[4,320,256]{2,1,0:T(8,128)(2,1)S(1)} %shard_map.84.teacher_ref), custom_call_target="tpu_custom_call" | custom-call | flops 2684354560 | bytes 12582912 | tf_op jit(solution)/shard_map/pallas_call | solution.py:151
  109.3 7.3 %all-to-all-start.2 = ((f32[16,24,128]{2,1,0:T(8,128)}), f32[16,24,128]{2,1,0:T(8,128)S(1)}, u32[]{:S(2)}, u32[]{:S(2)}) async-start(f32[16,24,128]{2,1,0:T(8,128)} %get-tuple-element.53), calls=%async_computation.2 | async-start | bytes 393216 | tf_op jit(solution)/shard_map/all_to_all | solution.py:487
  116.8 8.7 %all-to-all-done.2 = f32[16,24,128]{2,1,0:T(8,128)S(1)} async-done(((f32[16,24,128]{2,1,0:T(8,128)}), f32[16,24,128]{2,1,0:T(8,128)S(1)}, u32[]{:S(2)}, u32[]{:S(2)}) %all-to-all-start.2) | async-done | bytes 196640 | tf_op jit(solution)/shard_map/all_to_all | solution.py:487
  126.3 3.5 %all-to-all-start.3 = ((f32[16,24,128]{2,1,0:T(8,128)}), f32[16,24,128]{2,1,0:T(8,128)S(1)}, u32[]{:S(2)}, u32[]{:S(2)}) async-start(f32[16,24,128]{2,1,0:T(8,128)} %broadcast_in_dim.29), calls=%async_computation.3 | async-start | bytes 393216 | tf_op jit(solution)/shard_map/all_to_all | solution.py:489
  129.9 6.9 %all-to-all-done.3.stats_ref = f32[16,24,128]{2,1,0:T(8,128)S(1)} async-done(((f32[16,24,128]{2,1,0:T(8,128)}), f32[16,24,128]{2,1,0:T(8,128)S(1)}, u32[]{:S(2)}, u32[]{:S(2)}) %all-to-all-start.3) | async-done | bytes 196640 | tf_op jit(solution)/shard_map/all_to_all | solution.py:489
  136.8 1.1 shard_map.87
  137.9 2.2 %collective-permute-start.23 = (bf16[160,1024]{1,0:T(8,128)(2,1)S(1)}, bf16[160,1024]{1,0:T(8,128)(2,1)S(1)}, u32[]{:S(2)}, u32[]{:S(2)}) collective-permute-start(bf16[160,1024]{1,0:T(8,128)(2,1)S(1)} %get-tuple-element.55.refs_0_), channel_id=1, source_target_pairs={{0,193},{1,0},{64,1},{65,64},{128,65},{129,128},{192,129},{193,192... | collective-permute-start | bytes 983048 | tf_op jit(solution)/shard_map/ppermute | solution.py:383
  140.8 2.1 collective-permute-start.32
  142.8 2.6 %collective-permute-done.23.refs_3_ = bf16[160,1024]{1,0:T(8,128)(2,1)S(1)} collective-permute-done((bf16[160,1024]{1,0:T(8,128)(2,1)S(1)}, bf16[160,1024]{1,0:T(8,128)(2,1)S(1)}, u32[]{:S(2)}, u32[]{:S(2)}) %collective-permute-start.23) | collective-permute-done | bytes 327712 | tf_op jit(solution)/shard_map/ppermute | solution.py:383
  145.4 3.4 %collective-permute-start.24 = (bf16[160,1024]{1,0:T(8,128)(2,1)S(1)}, bf16[160,1024]{1,0:T(8,128)(2,1)S(1)}, u32[]{:S(2)}, u32[]{:S(2)}) collective-permute-start(bf16[160,1024]{1,0:T(8,128)(2,1)S(1)} %collective-permute-done.23.refs_3_), channel_id=1, source_target_pairs={{0,193},{1,0},{64,1},{65,64},{128,65},{129,128},{192,129},{193,192... | collective-permute-start | bytes 983048 | tf_op jit(solution)/shard_map/ppermute | solution.py:383
  148.8 6.7 %collective-permute-done.31.refs_2_ = bf16[160,1024]{1,0:T(8,128)(2,1)S(1)} collective-permute-done((bf16[160,1024]{1,0:T(8,128)(2,1)S(1)}, bf16[160,1024]{1,0:T(8,128)(2,1)S(1)}, u32[]{:S(2)}, u32[]{:S(2)}) %collective-permute-start.31) | collective-permute-done | bytes 327712 | tf_op jit(solution)/shard_map/ppermute | solution.py:383
  155.6 2.7 %collective-permute-start.34 = (bf16[160,1024]{1,0:T(8,128)(2,1)S(1)}, bf16[160,1024]{1,0:T(8,128)(2,1)S(1)}, u32[]{:S(2)}, u32[]{:S(2)}) collective-permute-start(bf16[160,1024]{1,0:T(8,128)(2,1)S(1)} %collective-permute-done.32.refs_5_), channel_id=1, source_target_pairs={{0,193},{1,0},{64,1},{65,64},{128,65},{129,128},{192,129},{193,192... | collective-permute-start | bytes 983048 | tf_op jit(solution)/shard_map/ppermute | solution.py:383
  158.3 1.2 collective-permute-done.24.refs_7_
  159.5 3.4 %collective-permute-start.25 = (bf16[160,1024]{1,0:T(8,128)(2,1)S(1)}, bf16[160,1024]{1,0:T(8,128)(2,1)S(1)}, u32[]{:S(2)}, u32[]{:S(2)}) collective-permute-start(bf16[160,1024]{1,0:T(8,128)(2,1)S(1)} %collective-permute-done.24.refs_7_), channel_id=1, source_target_pairs={{0,193},{1,0},{64,1},{65,64},{128,65},{129,128},{192,129},{193,192... | collective-permute-start | bytes 983048 | tf_op jit(solution)/shard_map/ppermute | solution.py:383
  162.9 6.7 %collective-permute-done.33.refs_6_ = bf16[160,1024]{1,0:T(8,128)(2,1)S(1)} collective-permute-done((bf16[160,1024]{1,0:T(8,128)(2,1)S(1)}, bf16[160,1024]{1,0:T(8,128)(2,1)S(1)}, u32[]{:S(2)}, u32[]{:S(2)}) %collective-permute-start.33) | collective-permute-done | bytes 327712 | tf_op jit(solution)/shard_map/ppermute | solution.py:383
  169.6 2.7 %collective-permute-start.36 = (bf16[160,1024]{1,0:T(8,128)(2,1)S(1)}, bf16[160,1024]{1,0:T(8,128)(2,1)S(1)}, u32[]{:S(2)}, u32[]{:S(2)}) collective-permute-start(bf16[160,1024]{1,0:T(8,128)(2,1)S(1)} %collective-permute-done.34.refs_9_), channel_id=1, source_target_pairs={{0,193},{1,0},{64,1},{65,64},{128,65},{129,128},{192,129},{193,192... | collective-permute-start | bytes 983048 | tf_op jit(solution)/shard_map/ppermute | solution.py:383
  172.3 0.8 collective-permute-done.25.refs_11_
  173.1 2.8 %collective-permute-start.26 = (bf16[160,1024]{1,0:T(8,128)(2,1)S(1)}, bf16[160,1024]{1,0:T(8,128)(2,1)S(1)}, u32[]{:S(2)}, u32[]{:S(2)}) collective-permute-start(bf16[160,1024]{1,0:T(8,128)(2,1)S(1)} %collective-permute-done.25.refs_11_), channel_id=1, source_target_pairs={{0,193},{1,0},{64,1},{65,64},{128,65},{129,128},{192,129},{193,192... | collective-permute-start | bytes 983048 | tf_op jit(solution)/shard_map/ppermute | solution.py:383
  175.9 0.8 collective-permute-done.29.refs_12_
  176.7 7.0 %collective-permute-done.35.refs_10_ = bf16[160,1024]{1,0:T(8,128)(2,1)S(1)} collective-permute-done((bf16[160,1024]{1,0:T(8,128)(2,1)S(1)}, bf16[160,1024]{1,0:T(8,128)(2,1)S(1)}, u32[]{:S(2)}, u32[]{:S(2)}) %collective-permute-start.35) | collective-permute-done | bytes 327712 | tf_op jit(solution)/shard_map/ppermute | solution.py:383
  183.7 1.9 copy-done.2
  185.5 6.1 %shard_map.88.refs_3_ = f32[1024,512]{1,0:T(8,128)S(1)} custom-call(s32[4]{0:T(128)S(1)} %pad_add_fusion.where_ref, bf16[160,1024]{1,0:T(8,128)(2,1)S(1)} %get-tuple-element.55.refs_0_, bf16[160,1024]{1,0:T(8,128)(2,1)S(1)} %get-tuple-element.56.refs_1_, bf16[160,1024]{1,0:T(8,128)(2,1)S(1)} %collective-permute-done.31.refs_2_, ...), custom_call_target="tpu_custom_call" | custom-call | flops 2684354560 | bytes 8388608 | tf_op jit(solution)/shard_map/pallas_call | solution.py:254
  191.8 2.2 shard_map.89
  194.0 5.5 %collective-permute-start.37 = (bf16[16,32,512]{2,1,0:T(8,128)(2,1)S(1)}, bf16[16,32,512]{2,1,0:T(8,128)(2,1)S(1)}, u32[]{:S(2)}, u32[]{:S(2)}) collective-permute-start(bf16[16,32,512]{2,1,0:T(8,128)(2,1)S(1)} %get-tuple-element.58), channel_id=1, source_target_pairs={{0,2},{2,0},{4,6},{6,4},{8,10},{10,8},{12,14},{14,12},{16,18},{18,... | collective-permute-start | bytes 1572872 | tf_op jit(solution)/shard_map/ppermute | solution.py:495
  199.5 1.5 collective-permute-done.37
  201.0 1.0 add_convert_fusion
  202.0 3.6 %all-to-all-start.4 = ((bf16[16,32,512]{2,1,0:T(8,128)(2,1)}), bf16[16,32,512]{2,1,0:T(8,128)(2,1)S(1)}, u32[]{:S(2)}, u32[]{:S(2)}) async-start(bf16[16,32,512]{2,1,0:T(8,128)(2,1)} %add_convert_fusion), calls=%async_computation.4 | async-start | bytes 1048576 | tf_op jit(solution)/shard_map/all_to_all | solution.py:497
  205.6 8.8 %shard_map.90 = (f32[512,2560]{1,0:T(8,128)}, bf16[128,2560]{1,0:T(8,128)(2,1)}) custom-call(s32[4]{0:T(128)} %copy-done.19, bf16[160,1024]{1,0:T(8,128)(2,1)} %copy-done.5, bf16[160,1024]{1,0:T(8,128)(2,1)} %copy-done.6, bf16[160,1024]{1,0:T(8,128)(2,1)} %copy-done.9, bf16[160,1024]{1,0:T(8,128)(2,1)} %copy-done.7, bf16[160,1024]{1,0:T(8,128)(2,1)} %copy-done.8, ...), custom_call_target="tpu_custom_call" | custom-call | flops 2684354560 | bytes 12582912 | tf_op jit(solution)/shard_map/pallas_call | solution.py:357
  214.4 1.5 all-to-all-done.4
  216.0 0.7 convert_reduce_fusion
  (102 shorter events, 8.6 us)
Async XLA Ops:
  0.6 1.3 copy-start
  2.9 20.9 %collective-permute-start = (bf16[320,256]{1,0:T(8,128)(2,1)S(1)}, bf16[320,256]{1,0:T(8,128)(2,1)S(1)}, u32[]{:S(2)}, u32[]{:S(2)}) collective-permute-start(bf16[320,256]{1,0:T(8,128)(2,1)S(1)} %get-tuple-element.70), channel_id=1, source_target_pairs={{0,64},{64,128},{128,192},{192,0},{1,65},{65,129},{129,193},{193,1... | collective-permute-start | bytes 491528 | tf_op jit(solution)/shard_map/ppermute | solution.py:467
  6.7 17.0 %collective-permute-start.1 = (bf16[320,256]{1,0:T(8,128)(2,1)S(1)}, bf16[320,256]{1,0:T(8,128)(2,1)S(1)}, u32[]{:S(2)}, u32[]{:S(2)}) collective-permute-start(bf16[320,256]{1,0:T(8,128)(2,1)S(1)} %get-tuple-element.69), channel_id=1, source_target_pairs={{0,128},{64,192},{128,0},{192,64},{1,129},{65,193},{129,1},{193,65... | collective-permute-start | bytes 491528 | tf_op jit(solution)/shard_map/ppermute | solution.py:467
  11.9 17.0 %collective-permute-start.2 = (bf16[320,256]{1,0:T(8,128)(2,1)S(1)}, bf16[320,256]{1,0:T(8,128)(2,1)S(1)}, u32[]{:S(2)}, u32[]{:S(2)}) collective-permute-start(bf16[320,256]{1,0:T(8,128)(2,1)S(1)} %get-tuple-element.68), channel_id=1, source_target_pairs={{0,192},{64,0},{128,64},{192,128},{1,193},{65,1},{129,65},{193,129... | collective-permute-start | bytes 491528 | tf_op jit(solution)/shard_map/ppermute | solution.py:467
  15.9 16.4 %all-to-all-start = ((bf16[8,128,128]{1,2,0:T(8,128)(2,1)}), bf16[8,128,128]{1,2,0:T(8,128)(2,1)S(1)}, u32[]{:S(2)}, u32[]{:S(2)}) async-start(bf16[8,128,128]{1,2,0:T(8,128)(2,1)} %broadcast_in_dim.28), calls=%async_computation | async-start | bytes 524288 | tf_op jit(solution)/shard_map/all_to_all | solution.py:407
  23.8 168.1 %copy-start.19 = (s32[4]{0:T(128)}, s32[4]{0:T(128)S(1)}, u32[]{:S(2)}) copy-start(s32[4]{0:T(128)S(1)} %pad_add_fusion.where_ref) | copy-start | bytes 52
  32.3 67.8 %all-to-all-start.1 = ((bf16[8,320,512]{2,1,0:T(8,128)(2,1)}), bf16[8,320,512]{2,1,0:T(8,128)(2,1)}, u32[]{:S(2)}, u32[]{:S(2)}) async-start(bf16[8,320,512]{2,1,0:T(8,128)(2,1)} %bitcast.29), calls=%async_computation.1 | async-start | bytes 5242880 | tf_op jit(solution)/shard_map/all_to_all | solution.py:479
  37.4 8.8 %collective-permute-start.3 = (bf16[128,512]{1,0:T(8,128)(2,1)S(1)}, bf16[128,512]{1,0:T(8,128)(2,1)S(1)}, u32[]{:S(2)}, u32[]{:S(2)}) collective-permute-start(bf16[128,512]{1,0:T(8,128)(2,1)S(1)} %get-tuple-element.36), channel_id=1, source_target_pairs={{0,16},{2,18},{4,20},{6,22},{8,24},{10,26},{12,28},{14,30},{16,32}... | collective-permute-start | bytes 393224 | tf_op jit(solution)/shard_map/ppermute | solution.py:418
  38.7 8.6 %collective-permute-start.4 = (bf16[128,512]{1,0:T(8,128)(2,1)S(1)}, bf16[128,512]{1,0:T(8,128)(2,1)S(1)}, u32[]{:S(2)}, u32[]{:S(2)}) collective-permute-start(bf16[128,512]{1,0:T(8,128)(2,1)S(1)} %get-tuple-element.36), channel_id=1, source_target_pairs={{0,32},{2,34},{4,36},{6,38},{8,40},{10,42},{12,44},{14,46},{16,48}... | collective-permute-start | bytes 393224 | tf_op jit(solution)/shard_map/ppermute | solution.py:418
  41.2 6.1 %collective-permute-start.5 = (bf16[128,512]{1,0:T(8,128)(2,1)S(1)}, bf16[128,512]{1,0:T(8,128)(2,1)S(1)}, u32[]{:S(2)}, u32[]{:S(2)}) collective-permute-start(bf16[128,512]{1,0:T(8,128)(2,1)S(1)} %get-tuple-element.36), channel_id=1, source_target_pairs={{0,48},{2,50},{4,52},{6,54},{8,56},{10,58},{12,60},{14,62},{16,0},... | collective-permute-start | bytes 393224 | tf_op jit(solution)/shard_map/ppermute | solution.py:418
  42.3 5.4 %collective-permute-start.6 = (bf16[128,512]{1,0:T(8,128)(2,1)S(1)}, bf16[128,512]{1,0:T(8,128)(2,1)S(1)}, u32[]{:S(2)}, u32[]{:S(2)}) collective-permute-start(bf16[128,512]{1,0:T(8,128)(2,1)S(1)} %get-tuple-element.40), channel_id=1, source_target_pairs={{0,4},{2,6},{4,8},{6,10},{8,12},{10,14},{12,0},{14,2},{16,20},{18,... | collective-permute-start | bytes 393224 | tf_op jit(solution)/shard_map/ppermute | solution.py:418
  43.6 6.8 %collective-permute-start.7 = (bf16[128,512]{1,0:T(8,128)(2,1)S(1)}, bf16[128,512]{1,0:T(8,128)(2,1)S(1)}, u32[]{:S(2)}, u32[]{:S(2)}) collective-permute-start(bf16[128,512]{1,0:T(8,128)(2,1)S(1)} %get-tuple-element.40), channel_id=1, source_target_pairs={{0,8},{2,10},{4,12},{6,14},{8,0},{10,2},{12,4},{14,6},{16,24},{18,... | collective-permute-start | bytes 393224 | tf_op jit(solution)/shard_map/ppermute | solution.py:418
  46.3 4.2 %collective-permute-start.8 = (bf16[128,512]{1,0:T(8,128)(2,1)S(1)}, bf16[128,512]{1,0:T(8,128)(2,1)S(1)}, u32[]{:S(2)}, u32[]{:S(2)}) collective-permute-start(bf16[128,512]{1,0:T(8,128)(2,1)S(1)} %get-tuple-element.40), channel_id=1, source_target_pairs={{0,12},{2,14},{4,0},{6,2},{8,4},{10,6},{12,8},{14,10},{16,28},{18,... | collective-permute-start | bytes 393224 | tf_op jit(solution)/shard_map/ppermute | solution.py:418
  50.5 11.6 %collective-permute-start.10 = (bf16[512,512]{1,0:T(8,128)(2,1)S(1)}, bf16[512,512]{1,0:T(8,128)(2,1)S(1)}, u32[]{:S(2)}, u32[]{:S(2)}) collective-permute-start(bf16[512,512]{1,0:T(8,128)(2,1)S(1)} %constant_dynamic-update-slice_fusion.4.refs_2_), channel_id=1, source_target_pairs={{0,16},{2,18},{4,20},{6,22},{8,24},{10,26},{12,28},{14,30},{16,32}... | collective-permute-start | bytes 1572872 | tf_op jit(solution)/shard_map/ppermute | solution.py:418
  50.9 20.4 %collective-permute-start.12 = (bf16[512,512]{1,0:T(8,128)(2,1)S(1)}, bf16[512,512]{1,0:T(8,128)(2,1)S(1)}, u32[]{:S(2)}, u32[]{:S(2)}) collective-permute-start(bf16[512,512]{1,0:T(8,128)(2,1)S(1)} %constant_dynamic-update-slice_fusion.4.refs_2_), channel_id=1, source_target_pairs={{0,32},{2,34},{4,36},{6,38},{8,40},{10,42},{12,44},{14,46},{16,48}... | collective-permute-start | bytes 1572872 | tf_op jit(solution)/shard_map/ppermute | solution.py:418
  51.9 24.3 %collective-permute-start.14 = (bf16[512,512]{1,0:T(8,128)(2,1)S(1)}, bf16[512,512]{1,0:T(8,128)(2,1)S(1)}, u32[]{:S(2)}, u32[]{:S(2)}) collective-permute-start(bf16[512,512]{1,0:T(8,128)(2,1)S(1)} %constant_dynamic-update-slice_fusion.4.refs_2_), channel_id=1, source_target_pairs={{0,48},{2,50},{4,52},{6,54},{8,56},{10,58},{12,60},{14,62},{16,0},... | collective-permute-start | bytes 1572872 | tf_op jit(solution)/shard_map/ppermute | solution.py:418
  53.5 22.6 %collective-permute-start.11 = (bf16[512,512]{1,0:T(8,128)(2,1)S(1)}, bf16[512,512]{1,0:T(8,128)(2,1)S(1)}, u32[]{:S(2)}, u32[]{:S(2)}) collective-permute-start(bf16[512,512]{1,0:T(8,128)(2,1)S(1)} %constant_dynamic-update-slice_fusion.refs_0_), channel_id=1, source_target_pairs={{0,8},{2,10},{4,12},{6,14},{8,0},{10,2},{12,4},{14,6},{16,24},{18,... | collective-permute-start | bytes 1572872 | tf_op jit(solution)/shard_map/ppermute | solution.py:418
  55.8 23.0 %collective-permute-start.13 = (bf16[512,512]{1,0:T(8,128)(2,1)S(1)}, bf16[512,512]{1,0:T(8,128)(2,1)S(1)}, u32[]{:S(2)}, u32[]{:S(2)}) collective-permute-start(bf16[512,512]{1,0:T(8,128)(2,1)S(1)} %constant_dynamic-update-slice_fusion.refs_0_), channel_id=1, source_target_pairs={{0,12},{2,14},{4,0},{6,2},{8,4},{10,6},{12,8},{14,10},{16,28},{18,... | collective-permute-start | bytes 1572872 | tf_op jit(solution)/shard_map/ppermute | solution.py:418
  62.1 16.7 %collective-permute-start.9 = (bf16[512,512]{1,0:T(8,128)(2,1)S(1)}, bf16[512,512]{1,0:T(8,128)(2,1)S(1)}, u32[]{:S(2)}, u32[]{:S(2)}) collective-permute-start(bf16[512,512]{1,0:T(8,128)(2,1)S(1)} %constant_dynamic-update-slice_fusion.refs_0_), channel_id=1, source_target_pairs={{0,4},{2,6},{4,8},{6,10},{8,12},{10,14},{12,0},{14,2},{16,20},{18,... | collective-permute-start | bytes 1572872 | tf_op jit(solution)/shard_map/ppermute | solution.py:418
  78.8 10.5 %collective-permute-start.15 = (bf16[512,512]{1,0:T(8,128)(2,1)S(1)}, bf16[512,512]{1,0:T(8,128)(2,1)S(1)}, u32[]{:S(2)}, u32[]{:S(2)}) collective-permute-start(bf16[512,512]{1,0:T(8,128)(2,1)S(1)} %constant_dynamic-update-slice_fusion.refs_0_), channel_id=1, source_target_pairs={{0,2},{2,0},{4,6},{6,4},{8,10},{10,8},{12,14},{14,12},{16,18},{18,... | collective-permute-start | bytes 1572872 | tf_op jit(solution)/shard_map/ppermute | solution.py:418
  87.8 2.3 %collective-permute-start.16 = (bf16[512,512]{1,0:T(8,128)(2,1)S(1)}, bf16[512,512]{1,0:T(8,128)(2,1)S(1)}, u32[]{:S(2)}, u32[]{:S(2)}) collective-permute-start(bf16[512,512]{1,0:T(8,128)(2,1)S(1)} %constant_dynamic-update-slice_fusion.4.refs_2_), channel_id=1, source_target_pairs={{0,2},{2,0},{4,6},{6,4},{8,10},{10,8},{12,14},{14,12},{16,18},{18,... | collective-permute-start | bytes 1572872 | tf_op jit(solution)/shard_map/ppermute | solution.py:418
  87.8 3.0 %collective-permute-start.17 = (bf16[512,512]{1,0:T(8,128)(2,1)S(1)}, bf16[512,512]{1,0:T(8,128)(2,1)S(1)}, u32[]{:S(2)}, u32[]{:S(2)}) collective-permute-start(bf16[512,512]{1,0:T(8,128)(2,1)S(1)} %collective-permute-done.9.refs_4_), channel_id=1, source_target_pairs={{0,2},{2,0},{4,6},{6,4},{8,10},{10,8},{12,14},{14,12},{16,18},{18,... | collective-permute-start | bytes 1572872 | tf_op jit(solution)/shard_map/ppermute | solution.py:418
  88.3 3.3 %collective-permute-start.18 = (bf16[512,512]{1,0:T(8,128)(2,1)S(1)}, bf16[512,512]{1,0:T(8,128)(2,1)S(1)}, u32[]{:S(2)}, u32[]{:S(2)}) collective-permute-start(bf16[512,512]{1,0:T(8,128)(2,1)S(1)} %collective-permute-done.10.refs_6_), channel_id=1, source_target_pairs={{0,2},{2,0},{4,6},{6,4},{8,10},{10,8},{12,14},{14,12},{16,18},{18,... | collective-permute-start | bytes 1572872 | tf_op jit(solution)/shard_map/ppermute | solution.py:418
  88.3 4.0 %collective-permute-start.19 = (bf16[512,512]{1,0:T(8,128)(2,1)S(1)}, bf16[512,512]{1,0:T(8,128)(2,1)S(1)}, u32[]{:S(2)}, u32[]{:S(2)}) collective-permute-start(bf16[512,512]{1,0:T(8,128)(2,1)S(1)} %collective-permute-done.11.refs_8_), channel_id=1, source_target_pairs={{0,2},{2,0},{4,6},{6,4},{8,10},{10,8},{12,14},{14,12},{16,18},{18,... | collective-permute-start | bytes 1572872 | tf_op jit(solution)/shard_map/ppermute | solution.py:418
  89.3 3.7 %collective-permute-start.20 = (bf16[512,512]{1,0:T(8,128)(2,1)S(1)}, bf16[512,512]{1,0:T(8,128)(2,1)S(1)}, u32[]{:S(2)}, u32[]{:S(2)}) collective-permute-start(bf16[512,512]{1,0:T(8,128)(2,1)S(1)} %collective-permute-done.12.refs_10_), channel_id=1, source_target_pairs={{0,2},{2,0},{4,6},{6,4},{8,10},{10,8},{12,14},{14,12},{16,18},{18,... | collective-permute-start | bytes 1572872 | tf_op jit(solution)/shard_map/ppermute | solution.py:418
  90.1 3.7 %collective-permute-start.21 = (bf16[512,512]{1,0:T(8,128)(2,1)S(1)}, bf16[512,512]{1,0:T(8,128)(2,1)S(1)}, u32[]{:S(2)}, u32[]{:S(2)}) collective-permute-start(bf16[512,512]{1,0:T(8,128)(2,1)S(1)} %collective-permute-done.13.refs_12_), channel_id=1, source_target_pairs={{0,2},{2,0},{4,6},{6,4},{8,10},{10,8},{12,14},{14,12},{16,18},{18,... | collective-permute-start | bytes 1572872 | tf_op jit(solution)/shard_map/ppermute | solution.py:418
  90.8 3.7 %collective-permute-start.22 = (bf16[512,512]{1,0:T(8,128)(2,1)S(1)}, bf16[512,512]{1,0:T(8,128)(2,1)S(1)}, u32[]{:S(2)}, u32[]{:S(2)}) collective-permute-start(bf16[512,512]{1,0:T(8,128)(2,1)S(1)} %collective-permute-done.14.refs_14_), channel_id=1, source_target_pairs={{0,2},{2,0},{4,6},{6,4},{8,10},{10,8},{12,14},{14,12},{16,18},{18,... | collective-permute-start | bytes 1572872 | tf_op jit(solution)/shard_map/ppermute | solution.py:418
  100.1 3.4 %copy-start.1 = (bf16[4096,1024]{1,0:T(8,128)(2,1)S(1)}, bf16[4096,1024]{1,0:T(8,128)(2,1)}, u32[]{:S(2)}) copy-start(bf16[4096,1024]{1,0:T(8,128)(2,1)} %shard_map.85.features_ref.refs_16_) | copy-start | bytes 25165828
  103.5 13.1 %copy-start.20 = (s32[32]{0:T(128)S(1)}, s32[32]{0:T(128)}, u32[]{:S(2)}) copy-start(s32[32]{0:T(128)} %param.9) | copy-start | bytes 388
  109.3 16.2 %all-to-all-start.2 = ((f32[16,24,128]{2,1,0:T(8,128)}), f32[16,24,128]{2,1,0:T(8,128)S(1)}, u32[]{:S(2)}, u32[]{:S(2)}) async-start(f32[16,24,128]{2,1,0:T(8,128)} %get-tuple-element.53), calls=%async_computation.2 | async-start | bytes 393216 | tf_op jit(solution)/shard_map/all_to_all | solution.py:487
  126.3 10.4 %all-to-all-start.3 = ((f32[16,24,128]{2,1,0:T(8,128)}), f32[16,24,128]{2,1,0:T(8,128)S(1)}, u32[]{:S(2)}, u32[]{:S(2)}) async-start(f32[16,24,128]{2,1,0:T(8,128)} %broadcast_in_dim.29), calls=%async_computation.3 | async-start | bytes 393216 | tf_op jit(solution)/shard_map/all_to_all | solution.py:489
  137.9 53.8 %copy-start.5 = (bf16[160,1024]{1,0:T(8,128)(2,1)}, bf16[160,1024]{1,0:T(8,128)(2,1)S(1)}, u32[]{:S(2)}) copy-start(bf16[160,1024]{1,0:T(8,128)(2,1)S(1)} %get-tuple-element.55.refs_0_) | copy-start | bytes 983044
  137.9 53.8 %copy-start.6 = (bf16[160,1024]{1,0:T(8,128)(2,1)}, bf16[160,1024]{1,0:T(8,128)(2,1)S(1)}, u32[]{:S(2)}) copy-start(bf16[160,1024]{1,0:T(8,128)(2,1)S(1)} %get-tuple-element.56.refs_1_) | copy-start | bytes 983044
  137.9 7.5 %collective-permute-start.23 = (bf16[160,1024]{1,0:T(8,128)(2,1)S(1)}, bf16[160,1024]{1,0:T(8,128)(2,1)S(1)}, u32[]{:S(2)}, u32[]{:S(2)}) collective-permute-start(bf16[160,1024]{1,0:T(8,128)(2,1)S(1)} %get-tuple-element.55.refs_0_), channel_id=1, source_target_pairs={{0,193},{1,0},{64,1},{65,64},{128,65},{129,128},{192,129},{193,192... | collective-permute-start | bytes 983048 | tf_op jit(solution)/shard_map/ppermute | solution.py:383
  140.1 8.7 %collective-permute-start.27 = (bf16[160,1024]{1,0:T(8,128)(2,1)S(1)}, bf16[160,1024]{1,0:T(8,128)(2,1)S(1)}, u32[]{:S(2)}, u32[]{:S(2)}) collective-permute-start(bf16[160,1024]{1,0:T(8,128)(2,1)S(1)} %get-tuple-element.56.refs_1_), channel_id=1, source_target_pairs={{0,1},{1,64},{64,65},{65,128},{128,129},{129,192},{192,193},{193,0... | collective-permute-start | bytes 983048 | tf_op jit(solution)/shard_map/ppermute | solution.py:383
  140.1 15.5 %collective-permute-start.31 = (bf16[160,1024]{1,0:T(8,128)(2,1)S(1)}, bf16[160,1024]{1,0:T(8,128)(2,1)S(1)}, u32[]{:S(2)}, u32[]{:S(2)}) collective-permute-start(bf16[160,1024]{1,0:T(8,128)(2,1)S(1)} %get-tuple-element.55.refs_0_), channel_id=1, source_target_pairs={{0,1},{1,64},{64,65},{65,128},{128,129},{129,192},{192,193},{193,0... | collective-permute-start | bytes 983048 | tf_op jit(solution)/shard_map/ppermute | solution.py:383
  140.8 14.8 %collective-permute-start.32 = (bf16[160,1024]{1,0:T(8,128)(2,1)S(1)}, bf16[160,1024]{1,0:T(8,128)(2,1)S(1)}, u32[]{:S(2)}, u32[]{:S(2)}) collective-permute-start(bf16[160,1024]{1,0:T(8,128)(2,1)S(1)} %get-tuple-element.56.refs_1_), channel_id=1, source_target_pairs={{0,193},{1,0},{64,1},{65,64},{128,65},{129,128},{192,129},{193,192... | collective-permute-start | bytes 983048 | tf_op jit(solution)/shard_map/ppermute | solution.py:383
  145.4 46.3 %copy-start.7 = (bf16[160,1024]{1,0:T(8,128)(2,1)}, bf16[160,1024]{1,0:T(8,128)(2,1)S(1)}, u32[]{:S(2)}) copy-start(bf16[160,1024]{1,0:T(8,128)(2,1)S(1)} %collective-permute-done.23.refs_3_) | copy-start | bytes 983044
  145.4 14.0 %collective-permute-start.24 = (bf16[160,1024]{1,0:T(8,128)(2,1)S(1)}, bf16[160,1024]{1,0:T(8,128)(2,1)S(1)}, u32[]{:S(2)}, u32[]{:S(2)}) collective-permute-start(bf16[160,1024]{1,0:T(8,128)(2,1)S(1)} %collective-permute-done.23.refs_3_), channel_id=1, source_target_pairs={{0,193},{1,0},{64,1},{65,64},{128,65},{129,128},{192,129},{193,192... | collective-permute-start | bytes 983048 | tf_op jit(solution)/shard_map/ppermute | solution.py:383
  148.8 42.8 %copy-start.8 = (bf16[160,1024]{1,0:T(8,128)(2,1)}, bf16[160,1024]{1,0:T(8,128)(2,1)S(1)}, u32[]{:S(2)}) copy-start(bf16[160,1024]{1,0:T(8,128)(2,1)S(1)} %collective-permute-done.27.refs_4_) | copy-start | bytes 983044
  148.8 14.0 %collective-permute-start.28 = (bf16[160,1024]{1,0:T(8,128)(2,1)S(1)}, bf16[160,1024]{1,0:T(8,128)(2,1)S(1)}, u32[]{:S(2)}, u32[]{:S(2)}) collective-permute-start(bf16[160,1024]{1,0:T(8,128)(2,1)S(1)} %collective-permute-done.27.refs_4_), channel_id=1, source_target_pairs={{0,1},{1,64},{64,65},{65,128},{128,129},{129,192},{192,193},{193,0... | collective-permute-start | bytes 983048 | tf_op jit(solution)/shard_map/ppermute | solution.py:383
  155.6 36.1 %copy-start.9 = (bf16[160,1024]{1,0:T(8,128)(2,1)}, bf16[160,1024]{1,0:T(8,128)(2,1)S(1)}, u32[]{:S(2)}) copy-start(bf16[160,1024]{1,0:T(8,128)(2,1)S(1)} %collective-permute-done.31.refs_2_) | copy-start | bytes 983044
  155.6 14.0 %collective-permute-start.33 = (bf16[160,1024]{1,0:T(8,128)(2,1)S(1)}, bf16[160,1024]{1,0:T(8,128)(2,1)S(1)}, u32[]{:S(2)}, u32[]{:S(2)}) collective-permute-start(bf16[160,1024]{1,0:T(8,128)(2,1)S(1)} %collective-permute-done.31.refs_2_), channel_id=1, source_target_pairs={{0,1},{1,64},{64,65},{65,128},{128,129},{129,192},{192,193},{193,0... | collective-permute-start | bytes 983048 | tf_op jit(solution)/shard_map/ppermute | solution.py:383
  155.6 36.1 %copy-start.10 = (bf16[160,1024]{1,0:T(8,128)(2,1)}, bf16[160,1024]{1,0:T(8,128)(2,1)S(1)}, u32[]{:S(2)}) copy-start(bf16[160,1024]{1,0:T(8,128)(2,1)S(1)} %collective-permute-done.32.refs_5_) | copy-start | bytes 983044
  155.6 14.0 %collective-permute-start.34 = (bf16[160,1024]{1,0:T(8,128)(2,1)S(1)}, bf16[160,1024]{1,0:T(8,128)(2,1)S(1)}, u32[]{:S(2)}, u32[]{:S(2)}) collective-permute-start(bf16[160,1024]{1,0:T(8,128)(2,1)S(1)} %collective-permute-done.32.refs_5_), channel_id=1, source_target_pairs={{0,193},{1,0},{64,1},{65,64},{128,65},{129,128},{192,129},{193,192... | collective-permute-start | bytes 983048 | tf_op jit(solution)/shard_map/ppermute | solution.py:383
  159.5 32.2 %copy-start.11 = (bf16[160,1024]{1,0:T(8,128)(2,1)}, bf16[160,1024]{1,0:T(8,128)(2,1)S(1)}, u32[]{:S(2)}) copy-start(bf16[160,1024]{1,0:T(8,128)(2,1)S(1)} %collective-permute-done.24.refs_7_) | copy-start | bytes 983044
  159.5 13.6 %collective-permute-start.25 = (bf16[160,1024]{1,0:T(8,128)(2,1)S(1)}, bf16[160,1024]{1,0:T(8,128)(2,1)S(1)}, u32[]{:S(2)}, u32[]{:S(2)}) collective-permute-start(bf16[160,1024]{1,0:T(8,128)(2,1)S(1)} %collective-permute-done.24.refs_7_), channel_id=1, source_target_pairs={{0,193},{1,0},{64,1},{65,64},{128,65},{129,128},{192,129},{193,192... | collective-permute-start | bytes 983048 | tf_op jit(solution)/shard_map/ppermute | solution.py:383
  162.9 28.8 %copy-start.12 = (bf16[160,1024]{1,0:T(8,128)(2,1)}, bf16[160,1024]{1,0:T(8,128)(2,1)S(1)}, u32[]{:S(2)}) copy-start(bf16[160,1024]{1,0:T(8,128)(2,1)S(1)} %collective-permute-done.28.refs_8_) | copy-start | bytes 983044
  162.9 13.8 %collective-permute-start.29 = (bf16[160,1024]{1,0:T(8,128)(2,1)S(1)}, bf16[160,1024]{1,0:T(8,128)(2,1)S(1)}, u32[]{:S(2)}, u32[]{:S(2)}) collective-permute-start(bf16[160,1024]{1,0:T(8,128)(2,1)S(1)} %collective-permute-done.28.refs_8_), channel_id=1, source_target_pairs={{0,1},{1,64},{64,65},{65,128},{128,129},{129,192},{192,193},{193,0... | collective-permute-start | bytes 983048 | tf_op jit(solution)/shard_map/ppermute | solution.py:383
  169.6 22.1 %copy-start.13 = (bf16[160,1024]{1,0:T(8,128)(2,1)}, bf16[160,1024]{1,0:T(8,128)(2,1)S(1)}, u32[]{:S(2)}) copy-start(bf16[160,1024]{1,0:T(8,128)(2,1)S(1)} %collective-permute-done.33.refs_6_) | copy-start | bytes 983044
  169.6 14.0 %collective-permute-start.35 = (bf16[160,1024]{1,0:T(8,128)(2,1)S(1)}, bf16[160,1024]{1,0:T(8,128)(2,1)S(1)}, u32[]{:S(2)}, u32[]{:S(2)}) collective-permute-start(bf16[160,1024]{1,0:T(8,128)(2,1)S(1)} %collective-permute-done.33.refs_6_), channel_id=1, source_target_pairs={{0,1},{1,64},{64,65},{65,128},{128,129},{129,192},{192,193},{193,0... | collective-permute-start | bytes 983048 | tf_op jit(solution)/shard_map/ppermute | solution.py:383
  169.6 22.1 %copy-start.14 = (bf16[160,1024]{1,0:T(8,128)(2,1)}, bf16[160,1024]{1,0:T(8,128)(2,1)S(1)}, u32[]{:S(2)}) copy-start(bf16[160,1024]{1,0:T(8,128)(2,1)S(1)} %collective-permute-done.34.refs_9_) | copy-start | bytes 983044
  169.6 14.0 %collective-permute-start.36 = (bf16[160,1024]{1,0:T(8,128)(2,1)S(1)}, bf16[160,1024]{1,0:T(8,128)(2,1)S(1)}, u32[]{:S(2)}, u32[]{:S(2)}) collective-permute-start(bf16[160,1024]{1,0:T(8,128)(2,1)S(1)} %collective-permute-done.34.refs_9_), channel_id=1, source_target_pairs={{0,193},{1,0},{64,1},{65,64},{128,65},{129,128},{192,129},{193,192... | collective-permute-start | bytes 983048 | tf_op jit(solution)/shard_map/ppermute | solution.py:383
  173.1 18.7 %copy-start.15 = (bf16[160,1024]{1,0:T(8,128)(2,1)}, bf16[160,1024]{1,0:T(8,128)(2,1)S(1)}, u32[]{:S(2)}) copy-start(bf16[160,1024]{1,0:T(8,128)(2,1)S(1)} %collective-permute-done.25.refs_11_) | copy-start | bytes 983044
  173.1 18.7 %collective-permute-start.26 = (bf16[160,1024]{1,0:T(8,128)(2,1)S(1)}, bf16[160,1024]{1,0:T(8,128)(2,1)S(1)}, u32[]{:S(2)}, u32[]{:S(2)}) collective-permute-start(bf16[160,1024]{1,0:T(8,128)(2,1)S(1)} %collective-permute-done.25.refs_11_), channel_id=1, source_target_pairs={{0,193},{1,0},{64,1},{65,64},{128,65},{129,128},{192,129},{193,192... | collective-permute-start | bytes 983048 | tf_op jit(solution)/shard_map/ppermute | solution.py:383
  176.6 15.1 %copy-start.16 = (bf16[160,1024]{1,0:T(8,128)(2,1)}, bf16[160,1024]{1,0:T(8,128)(2,1)S(1)}, u32[]{:S(2)}) copy-start(bf16[160,1024]{1,0:T(8,128)(2,1)S(1)} %collective-permute-done.29.refs_12_) | copy-start | bytes 983044
  176.6 15.2 %collective-permute-start.30 = (bf16[160,1024]{1,0:T(8,128)(2,1)S(1)}, bf16[160,1024]{1,0:T(8,128)(2,1)S(1)}, u32[]{:S(2)}, u32[]{:S(2)}) collective-permute-start(bf16[160,1024]{1,0:T(8,128)(2,1)S(1)} %collective-permute-done.29.refs_12_), channel_id=1, source_target_pairs={{0,1},{1,64},{64,65},{65,128},{128,129},{129,192},{192,193},{193,0... | collective-permute-start | bytes 983048 | tf_op jit(solution)/shard_map/ppermute | solution.py:383
  183.7 8.1 %copy-start.17 = (bf16[160,1024]{1,0:T(8,128)(2,1)}, bf16[160,1024]{1,0:T(8,128)(2,1)S(1)}, u32[]{:S(2)}) copy-start(bf16[160,1024]{1,0:T(8,128)(2,1)S(1)} %collective-permute-done.35.refs_10_) | copy-start | bytes 983044
  183.7 1.9 copy-start.2
  185.5 6.3 %copy-start.18 = (bf16[160,1024]{1,0:T(8,128)(2,1)}, bf16[160,1024]{1,0:T(8,128)(2,1)S(1)}, u32[]{:S(2)}) copy-start(bf16[160,1024]{1,0:T(8,128)(2,1)S(1)} %collective-permute-done.36.refs_13_) | copy-start | bytes 983044
  191.8 2.2 %copy-start.3 = (bf16[160,1024]{1,0:T(8,128)(2,1)}, bf16[160,1024]{1,0:T(8,128)(2,1)S(1)}, u32[]{:S(2)}) copy-start(bf16[160,1024]{1,0:T(8,128)(2,1)S(1)} %collective-permute-done.26.refs_0_.refs_14_) | copy-start | bytes 983044
  191.8 2.2 %copy-start.4 = (bf16[160,1024]{1,0:T(8,128)(2,1)}, bf16[160,1024]{1,0:T(8,128)(2,1)S(1)}, u32[]{:S(2)}) copy-start(bf16[160,1024]{1,0:T(8,128)(2,1)S(1)} %collective-permute-done.30.refs_1_.refs_15_) | copy-start | bytes 983044
  194.0 7.0 %collective-permute-start.37 = (bf16[16,32,512]{2,1,0:T(8,128)(2,1)S(1)}, bf16[16,32,512]{2,1,0:T(8,128)(2,1)S(1)}, u32[]{:S(2)}, u32[]{:S(2)}) collective-permute-start(bf16[16,32,512]{2,1,0:T(8,128)(2,1)S(1)} %get-tuple-element.58), channel_id=1, source_target_pairs={{0,2},{2,0},{4,6},{6,4},{8,10},{10,8},{12,14},{14,12},{16,18},{18,... | collective-permute-start | bytes 1572872 | tf_op jit(solution)/shard_map/ppermute | solution.py:495
  202.0 14.0 %all-to-all-start.4 = ((bf16[16,32,512]{2,1,0:T(8,128)(2,1)}), bf16[16,32,512]{2,1,0:T(8,128)(2,1)S(1)}, u32[]{:S(2)}, u32[]{:S(2)}) async-start(bf16[16,32,512]{2,1,0:T(8,128)(2,1)} %add_convert_fusion), calls=%async_computation.4 | async-start | bytes 1048576 | tf_op jit(solution)/shard_map/all_to_all | solution.py:497
